TPU v7x, 32 devices: a whole 2x2x4 slice. The times are simulated.
32 devices in a mesh: row: 4 (over x, core), col: 8 (over z, y).
Axes of the slice: x: 2, y: 2, z: 4, core: 2. Of those that a mesh axis runs over, the one named last changes fastest.
Arguments:
- filtered: float32 [8192, 2048], P(('row', 'col')), as said below
- hamiltonian_applied: float32 [8192, 2048], P(('row', 'col')), as said below
- rotation: float32 [2048, 2048], replicated, may hold values from -0.125 to 0.125
Outputs:
- intersection: float32 [2048, 2048], P('row', 'col')
- projected: float32 [2048, 2048], P('row', 'col')
- rotated: float32 [8192, 2048], P(('row', 'col'))
Inputs may be any that keep to these rules, and one draw needn't show every extreme that they name: `filtered`: finite real values. `hamiltonian_applied`: finite real values.
All inputs are finite; a program needn't handle non-finite values.
Results may differ from a plain program's by a relative error of at most 0.00005.
Values sent between devices are 32-bit elements; how exact they have to be, the bound alone decides.
No kernel may reach another device: no remote copies, remote signals or barrier semaphores. Data moves between devices by JAX's collectives and lax.ppermute only.
A program may use at most 192 MiB of HBM per device.

v0:
```python
import jax
import jax.numpy as jnp
from jax import lax
from jax.sharding import PartitionSpec as P


def inner_rows(first, second):
    return jnp.einsum(
        "gi,gj->ij",
        first,
        second,
        precision=lax.Precision.HIGHEST,
        preferred_element_type=jnp.float32,
    )


def product(first, second):
    return jnp.dot(
        first, second, precision=lax.Precision.HIGHEST, preferred_element_type=jnp.float32
    )


def local(filtered, hamiltonian_applied, rotation):
    cells = filtered.shape[0]
    col_count = lax.axis_size("col")
    row_count = lax.axis_size("row")
    scale = 1.0 / (cells * col_count * row_count)
    psi_band, ham_band = (
        lax.all_to_all(filtered, "col", split_axis=1, concat_axis=0, tiled=True),
        lax.all_to_all(hamiltonian_applied, "col", split_axis=1, concat_axis=0, tiled=True),
    )
    piece = lax.all_gather(psi_band, "col", axis=1, tiled=True)
    over_term = inner_rows(piece, psi_band) * scale
    proj_term = inner_rows(piece, ham_band) * scale
    over_term, proj_term = (over_term, proj_term)
    intersection, projected = (
        lax.psum_scatter(over_term, "row", scatter_dimension=0, tiled=True),
        lax.psum_scatter(proj_term, "row", scatter_dimension=0, tiled=True),
    )
    rotated = product(filtered, rotation)
    return (intersection, projected, rotated)


def solution(mesh):
    return jax.shard_map(
        local,
        mesh=mesh,
        in_specs=(P(("row", "col"), None), P(("row", "col"), None), P()),
        out_specs=(P("row", "col"), P("row", "col"), P(("row", "col"), None)),
        check_vma=False,
    )
```

profile of v0, /device:TPU:2, one launch (start us, length us, event | category | flops | bytes accessed | tf_op | source)
XLA Modules:
  0.0 435.4 jit_solution(15934875969827322497)
XLA Ops:
  7.2 0.0 all-gather.2.cloned.1.call-start
  7.2 2.9 copy.6
  10.1 54.1 %all_to_all.38 = f32[256,8,256]{0,2,1:T(8,128)S(1)} all-to-all(f32[256,8,256]{0,2,1:T(8,128)} %bitcast.17), channel_id=1, replica_groups=mesh['row'=4,'col'=8] {'col'}, dimensions={1} | all-to-all | bytes 4194304 | tf_op jit(solution)/shard_map/all_to_all | solution.py:29
  64.2 1.8 copy.7
  66.0 0.0 copy-start.2
  66.0 0.0 all-gather.2.cloned.1.call-update
  66.0 1.6 copy-done.2
  67.6 1.8 copy.8
  69.4 0.0 copy-start
  69.4 4.5 %all-to-all-start.1 = ((f32[256,8,256]{0,2,1:T(8,128)}), f32[256,8,256]{0,2,1:T(8,128)}, u32[]{:S(2)}, u32[]{:S(2)}) async-start(f32[256,8,256]{0,2,1:T(8,128)} %bitcast.15), calls=%async_computation.2 | async-start | bytes 4194304 | tf_op jit(solution)/shard_map/all_to_all | solution.py:30
  73.9 0.0 reduce-scatter.3.cloned.1.call-start
  74.0 261.8 %all-gather.2.cloned.1.call-done = f32[2048,2048]{1,0:T(8,128)} async-done(((f32[2048,256]{1,0:T(8,128)}), f32[2048,2048]{1,0:T(8,128)}) %all-gather.2.cloned.1.call-update) | async-done | bytes 16777232 | tf_op jit(solution)/shard_map/all_gather | solution.py:32
  335.8 0.0 copy-done
  335.8 29.7 %convolution_multiply_fusion.1 = f32[2048,256]{1,0:T(8,128)} fusion(f32[2048,2048]{1,0:T(8,128)} %all-gather.2.cloned.1.call-done, f32[2048,256]{1,0:T(8,128)S(1)} %bitcast.13), kind=kOutput, calls=%fused_computation.1 | convolution fusion | flops 12885426176 | bytes 20971520 | tf_op jit(solution)/shard_map/gi,gj->ij/dot_general | solution.py:8
  365.5 0.0 reduce-scatter.3.cloned.1.call-update
  365.5 0.2 reduce-scatter.5.cloned.1.call-start
  365.7 0.0 all-to-all-done.1
  365.7 1.9 copy.9
  367.7 30.0 %convolution_multiply_fusion = f32[2048,256]{1,0:T(8,128)} fusion(f32[2048,2048]{1,0:T(8,128)} %all-gather.2.cloned.1.call-done, f32[2048,256]{1,0:T(8,128)S(1)} %bitcast.14), kind=kOutput, calls=%fused_computation | convolution fusion | flops 12885426176 | bytes 20971520 | tf_op jit(solution)/shard_map/gi,gj->ij/dot_general | solution.py:8
  397.6 0.0 copy-start.1
  397.6 0.0 reduce-scatter.5.cloned.1.call-update
  397.7 1.6 copy-done.1
  399.2 17.8 %fusion = f32[256,2048]{1,0:T(8,128)} fusion(f32[256,2048]{1,0:T(8,128)S(1)} %copy-done.1, f32[2048,2048]{1,0:T(8,128)} %param.5), kind=kOutput, calls=%fused_computation.2 | convolution fusion | flops 12884901888 | bytes 20971520 | tf_op jit(solution)/shard_map/dot_general | solution.py:18
  417.0 0.0 reduce-scatter.3.cloned.1.call-done
  417.0 11.8 %reduce-scatter.5.cloned.1.call-done = f32[512,256]{1,0:T(8,128)} async-done(((f32[2048,256]{1,0:T(8,128)}), f32[512,256]{1,0:T(8,128)}) %reduce-scatter.5.cloned.1.call-update) | async-done | bytes 524304 | tf_op jit(solution)/shard_map/reduce_scatter | solution.py:38
Async XLA Ops:
  7.2 328.6 %all-gather.2.cloned.1.call-start = ((), (), s32[]{:S(2)}) async-start(), calls=%async_computation.4 | async-start | bytes 18874368 | tf_op jit(solution)/shard_map/all_gather | solution.py:32
  66.0 1.6 copy-start.2
  69.4 266.4 %copy-start = (f32[8,256,256]{2,1,0:T(8,128)S(1)}, f32[8,256,256]{2,1,0:T(8,128)}, u32[]{:S(2)}) copy-start(f32[8,256,256]{2,1,0:T(8,128)} %copy.7) | copy-start | bytes 6291460
  69.4 296.3 %all-to-all-start.1 = ((f32[256,8,256]{0,2,1:T(8,128)}), f32[256,8,256]{0,2,1:T(8,128)}, u32[]{:S(2)}, u32[]{:S(2)}) async-start(f32[256,8,256]{0,2,1:T(8,128)} %bitcast.15), calls=%async_computation.2 | async-start | bytes 4194304 | tf_op jit(solution)/shard_map/all_to_all | solution.py:30
  73.9 343.1 %reduce-scatter.3.cloned.1.call-start = ((), (), s32[]{:S(2)}) async-start(), calls=%async_computation.5 | async-start | bytes 2621440 | tf_op jit(solution)/shard_map/reduce_scatter | solution.py:37
  365.5 63.3 %reduce-scatter.5.cloned.1.call-start = ((), (), s32[]{:S(2)}) async-start(), calls=%async_computation.6 | async-start | bytes 2621440 | tf_op jit(solution)/shard_map/reduce_scatter | solution.py:38
  397.6 1.6 copy-start.1
Sparse Core Ops, SparseCore 0:
  66.1 269.6 all-gather.1
  365.6 28.4 reduce-scatter.2
  397.8 31.0 reduce-scatter.4
where the time goes:
time: 438 us; the launch traced here: 435 us
  waiting for transfers between devices  274 us (63%)
  matrix products  77.4 us (18%)
  blocking collectives  54.1 us (12%)
  between operations  13.8 us (3%)
  local copies, waits for them, and re-layouts  11.6 us (3%)
  starting transfers between devices  4.81 us (1%)
    all_gather x1, waiting for transfers between devices, local(): piece = lax.all_gather(psi_band, 'col', axis=1, tiled=True)  262 us
    dot_general x2, matrix products, inner_rows(): jnp.einsum('gi,gj->ij', first, second, precision=lax.Precision.HIGHEST, p...  59.6 us
    all_to_all x1, blocking collectives, local(): lax.all_to_all(filtered, 'col', split_axis=1, concat_axis=0, tiled=True)  54.1 us
    dot_general x1, matrix products, product(): jnp.dot(first, second, precision=lax.Precision.HIGHEST, preferred_element...  17.8 us
    reduce_scatter x1, waiting for transfers between devices, local(): lax.psum_scatter(proj_term, 'row', scatter_dimension=0, tiled=True)  11.8 us
  transfers between devices with their start and end apart: 4, of which 2 were waited for; matrix products, arithmetic and copies ran while one was open for 19% of the time, Pallas kernels for 0%

commit v1 on v0

v1 whole, which is shorter than its diff:
```python
import jax
import jax.numpy as jnp
from jax import lax
from jax.sharding import PartitionSpec as P


def bit_reversed(count):
    bits = count.bit_length() - 1
    return [int(format(i, f"0{bits}b")[::-1], 2) if bits else 0 for i in range(count)]


def contract(first, second):
    return lax.dot_general(
        first,
        second,
        (((0,), (0,)), ((), ())),
        precision=lax.Precision.HIGH,
        preferred_element_type=jnp.float32,
    )


def swap(value, axis, bit):
    count = lax.axis_size(axis)
    return lax.ppermute(value, axis, [(i, i ^ (1 << bit)) for i in range(count)])


def halve(part, dim, axis, bit):
    mine = (lax.axis_index(axis) >> bit) & 1
    half = part.shape[dim] // 2
    keep = lax.dynamic_slice_in_dim(part, mine * half, half, dim)
    send = lax.dynamic_slice_in_dim(part, (1 - mine) * half, half, dim)
    return keep + swap(send, axis, bit)


def scatter_sum(part):
    rows, cols = lax.axis_size("row"), lax.axis_size("col")
    for bit in range(rows.bit_length() - 1):
        part = halve(part, 0, "row", bit)
    for bit in range(1, cols.bit_length() - 1):
        part = halve(part, 1, "col", bit)
    return part


def local(filtered, hamiltonian_applied, rotation):
    cells, orbitals = filtered.shape
    R, C = lax.axis_size("row"), lax.axis_size("col")
    Z = C // 2
    b = orbitals // C
    scale = 1.0 / (cells * C * R)
    r, c = lax.axis_index("row"), lax.axis_index("col")
    z, y = c // 2, c % 2
    row_order, col_order = bit_reversed(R), bit_reversed(Z)

    def pick(array, parity):
        return lax.dynamic_index_in_dim(array.reshape(cells, -1, 2, b), parity, 2, keepdims=False)

    psi_own, psi_other = pick(filtered, y), pick(filtered, 1 - y)
    ham_own, ham_other = pick(hamiltonian_applied, y), pick(hamiltonian_applied, 1 - y)
    near = jnp.concatenate([psi_own, swap(psi_other, "col", 0)], 0)
    ham = jnp.concatenate([ham_own, swap(ham_other, "col", 0)], 0)
    far = jnp.concatenate([psi_other, swap(psi_own, "col", 0)], 0)

    def side(blocks, order):
        return jnp.concatenate([blocks[:, i] for i in order], 1)

    ham_cols = side(ham, col_order)
    proj_near = scatter_sum(contract(side(near, row_order), ham_cols))

    over = jnp.concatenate(
        [
            contract(
                jnp.concatenate([near[:, i] if i <= j else far[:, i] for i in row_order], 1),
                near[:, j],
            )
            for j in col_order
        ],
        1,
    )
    half = b // 2
    piece = half // Z
    odd = jnp.where(y == 0, far[:, :, :half], near[:, :, half:])
    even = jnp.where(y == 0, near, far)
    parts = []
    for n, i in enumerate(row_order):
        extra = contract(odd[:, i], even[:, i])
        extra = jnp.concatenate([extra[j * piece : (j + 1) * piece] for j in col_order], 1)
        parts += [over[n * b : (n + 1) * b], extra]
    over = scatter_sum(jnp.concatenate(parts, 0)) * scale
    main, extra = over[:b], over[b:]
    later = (r > z).astype(jnp.int32)
    h = y ^ later
    pairs = [
        (i * C + 2 * j + p, j * C + 2 * i + (p ^ int(i > j)))
        for i in range(R)
        for j in range(Z)
        for p in range(2)
        if i != j
    ]
    mirrored = lax.ppermute(main.T, ("row", "col"), pairs)
    whole = lax.all_gather(extra, "col", axis=0)
    whole = whole.reshape(Z, 2, piece, b).transpose(1, 0, 2, 3).reshape(b, b)
    mirrored = jnp.where(r == z, jnp.where(y == 0, whole, whole.T), mirrored)
    intersection = jnp.where(
        h == 0, jnp.concatenate([main, mirrored], 0), jnp.concatenate([mirrored, main], 0)
    )

    proj_far = scatter_sum(contract(side(far, row_order), ham_cols))
    projected = scale * jnp.where(
        y == 0,
        jnp.concatenate([proj_near, proj_far], 0),
        jnp.concatenate([proj_far, proj_near], 0),
    )
    rotated = jnp.dot(
        filtered, rotation, precision=lax.Precision.HIGH, preferred_element_type=jnp.float32
    )
    return (intersection, projected, rotated)


def solution(mesh):
    return jax.shard_map(
        local,
        mesh=mesh,
        in_specs=(P(("row", "col"), None), P(("row", "col"), None), P()),
        out_specs=(P("row", "col"), P("row", "col"), P(("row", "col"), None)),
        check_vma=False,
    )
```

time: 438 us -> 289 us (0.66)
  waiting for transfers between devices: 274 us -> 128 us
  matrix products: 77.4 us -> 25.8 us
  local copies, waits for them, and re-layouts: 11.6 us -> 56.4 us
  other arithmetic: 0 us -> 24.3 us
  blocking collectives: 54.1 us -> 31.9 us
  starting transfers between devices: 4.81 us -> 19.7 us
  between operations: 13.8 us -> 1.14 us
    all_gather x1 -> x0, waiting for transfers between devices: 262 us -> none  [local(): piece = lax.all_gather(psi_band, 'col', axis=1, tiled=True)]
    ppermute x0 -> x16, waiting for transfers between devices: none -> 128 us  [the longest x15 128 us: swap(): return lax.ppermute(value, axis, [(i, i ^ 1 << bit) for i in range(count)])]
    all_to_all x1 -> x0, blocking collectives: 54.1 us -> none  [local(): lax.all_to_all(filtered, 'col', split_axis=1, concat_axis=0, tiled=True)]
    dot_general x3 -> x11, matrix products: 77.4 us -> 25.8 us  [the longest x10 13 us: contract(): lax.dot_general(first, second, (((0,), (0,)), ((), ())), precision=lax.Pr...]
    all_gather x0 -> x1, blocking collectives: none -> 31.9 us  [local(): whole = lax.all_gather(extra, 'col', axis=0)]
    dynamic_slice x0 -> x20, local copies, waits for them, and re-layouts: none -> 27.1 us  [the longest x15 18 us: halve(): send = lax.dynamic_slice_in_dim(part, (1 - mine) * half, half, dim)]
    ppermute x0 -> x16, starting transfers between devices: none -> 19.7 us  [the longest x15 17.4 us: swap(): return lax.ppermute(value, axis, [(i, i ^ 1 << bit) for i in range(count)])]
    add x0 -> x11, other arithmetic: none -> 16.6 us  [halve(): return keep + swap(send, axis, bit)]
  transfers between devices with their start and end apart: 4 -> 16, of which waited for: 2 -> 8; matrix products, arithmetic and copies ran while one was open for 19% -> 30% of each run, Pallas kernels for 0% -> 0%
where the time goes in v1:
time: 289 us; the launch traced here: 287 us
  waiting for transfers between devices  128 us (44%)
  local copies, waits for them, and re-layouts  56.4 us (20%)
  blocking collectives  31.9 us (11%)
  matrix products  25.8 us (9%)
  other arithmetic  24.3 us (8%)
  starting transfers between devices  19.7 us (7%)
    ppermute x15, waiting for transfers between devices, swap(): return lax.ppermute(value, axis, [(i, i ^ 1 << bit) for i in range(count)])  128 us
    all_gather x1, blocking collectives, local(): whole = lax.all_gather(extra, 'col', axis=0)  31.9 us
    dynamic_slice x15, local copies, waits for them, and re-layouts, halve(): send = lax.dynamic_slice_in_dim(part, (1 - mine) * half, half, dim)  18 us
    ppermute x15, starting transfers between devices, swap(): return lax.ppermute(value, axis, [(i, i ^ 1 << bit) for i in range(count)])  17.4 us
    add x11, other arithmetic, halve(): return keep + swap(send, axis, bit)  16.6 us
    dot_general x10, matrix products, contract(): lax.dot_general(first, second, (((0,), (0,)), ((), ())), precision=lax.Pr...  13 us
    dot_general x1, matrix products, local(): jnp.dot(filtered, rotation, precision=lax.Precision.HIGH, preferred_eleme...  12.8 us
    unnamed x35, local copies, waits for them, and re-layouts  9.61 us
  transfers between devices with their start and end apart: 16, of which 8 were waited for; matrix products, arithmetic and copies ran while one was open for 30% of the time, Pallas kernels for 0%

profile of v1, /device:TPU:2, one launch (start us, length us, event | category | flops | bytes accessed | tf_op | source)
XLA Modules:
  0.0 287.2 jit_solution(18297967029663355045)
XLA Ops:
  0.6 1.9 copy.76
  2.6 2.9 %copy.93 = f32[256,2048]{0,1:T(8,128)} copy(f32[256,2048]{1,0:T(8,128)} %param.4) | data formatting | bytes 4194304 | tf_op args[1]
  5.5 3.3 %constant_dynamic-slice_fusion.9 = (f32[256,4,1,256]{0,3,2,1:T(8,128)}, f32[256,4,1,256]{0,3,2,1:T(8,128)}, f32[256,4,1,256]{0,3,2,1:T(8,128)}, f32[256,4,1,256]{0,3,2,1:T(8,128)S(1)}) fusion(f32[256,4,2,256]{0,3,2,1:T(8,128)} %bitcast.79, s32[]{:T(128)S(6)} %select_n.115, s32[]{:T(128)S(6)} %select_n.116, f32[256,4,2,256]{0,3,2,1:T(8,128)S(1)} %bitcast.78), kind=kLoop, calls=%fused_computation.119 | loop fusion | bytes 8388616 | tf_op jit(solution)/shard_map/jit(dynamic_index_in_dim)/dynamic_slice | solution.py:55
  9.1 1.6 collective-permute-start
  11.9 2.6 copy.95
  15.7 2.5 copy.94
  18.2 17.1 %collective-permute-done = f32[256,4,256]{2,0,1:T(8,128)} collective-permute-done((f32[256,4,256]{2,0,1:T(8,128)S(1)}, f32[256,4,256]{2,0,1:T(8,128)}, u32[]{:S(2)}, u32[]{:S(2)}) %collective-permute-start) | collective-permute-done | bytes 1048608 | tf_op jit(solution)/shard_map/ppermute | solution.py:24
  35.3 22.4 %collective-permute-done.1 = f32[256,4,256]{2,0,1:T(8,128)S(1)} collective-permute-done((f32[256,4,256]{2,0,1:T(8,128)S(1)}, f32[256,4,256]{2,0,1:T(8,128)S(1)}, u32[]{:S(2)}, u32[]{:S(2)}) %collective-permute-start.1) | collective-permute-done | bytes 1048608 | tf_op jit(solution)/shard_map/ppermute | solution.py:24
  58.9 1.5 fusion.4
  60.8 1.3 fusion.26
  64.4 14.7 %collective-permute-done.7 = f32[256,4,256]{2,0,1:T(8,128)} collective-permute-done((f32[256,4,256]{2,0,1:T(8,128)}, f32[256,4,256]{2,0,1:T(8,128)}, u32[]{:S(2)}, u32[]{:S(2)}) %collective-permute-start.7) | collective-permute-done | bytes 1048608 | tf_op jit(solution)/shard_map/ppermute | solution.py:24
  79.1 1.3 fusion.14
  80.5 3.5 %fusion.6 = f32[1024,1024]{1,0:T(8,128)S(1)} fusion(f32[512,256]{1,0:T(8,128)S(1)} %get-tuple-element.32, f32[512,256]{1,0:T(8,128)S(1)} %get-tuple-element.31, f32[512,256]{1,0:T(8,128)S(1)} %get-tuple-element.30, f32[512,256]{1,0:T(8,128)S(1)} %get-tuple-element.29, f32[512,256]{1,0:T(8,128)S(1)} %get-tuple-element.21, ...), kind=kOutput, calls=%fused_computation.52 | convolution fusion | flops 3224371200 | bytes 8388608 | tf_op jit(solution)/shard_map/dot_general | solution.py:13
  84.0 1.8 constant_dynamic-slice_fusion.7
  89.0 1.2 fusion.1
  90.2 3.5 %fusion.3 = f32[1024,1024]{1,0:T(8,128)S(1)} fusion(f32[512,256]{1,0:T(8,128)S(1)} %get-tuple-element.28, f32[512,256]{1,0:T(8,128)S(1)} %get-tuple-element.27, f32[512,256]{1,0:T(8,128)S(1)} %get-tuple-element.26, f32[512,256]{1,0:T(8,128)S(1)} %get-tuple-element.25, f32[512,256]{1,0:T(8,128)S(1)} %get-tuple-element.21, ...), kind=kOutput, calls=%fused_computation.44 | convolution fusion | flops 3224371200 | bytes 8388608 | tf_op jit(solution)/shard_map/dot_general | solution.py:13
  93.7 1.8 constant_dynamic-slice_fusion.3
  97.6 1.4 fusion.46
  102.7 1.9 copy.79
  104.6 6.7 %concatenate.69 = f32[1152,1024]{0,1:T(8,128)} concatenate(f32[256,1024]{0,1:T(8,128)} %get-tuple-element.18, f32[32,1024]{0,1:T(8,128)} %copy.79, f32[256,1024]{0,1:T(8,128)S(1)} %get-tuple-element.17, f32[32,1024]{0,1:T(8,128)} %copy.80, f32[256,1024]{0,1:T(8,128)S(1)} %get-tuple-element.16, f32[32,1024]{0,1:T(8,128)} %copy.81, f32[256,1024]{0,1:T(8,128)S(1)} %get-tuple-element.15, ...), dimensions={0} | concatenate | bytes 9437184 | tf_op jit(solution)/shard_map/concatenate | solution.py:88
  111.3 2.5 constant_dynamic-slice_fusion.13
  113.7 2.1 copy.83
  116.0 2.8 dynamic-slice_add_fusion.2
  120.2 2.0 dynamic-slice_add_fusion.1
  124.0 1.7 collective-permute-start.13
  125.7 2.1 copy.84
  127.8 3.4 %dynamic-slice_add_fusion = f32[576,1024]{0,1:T(8,128)S(1)} fusion(f32[576,1024]{0,1:T(8,128)} %copy.84, f32[1152,1024]{0,1:T(8,128)} %concatenate.69, s32[]{:T(128)S(6)} %select_n.121), kind=kLoop, calls=%fused_computation.40 | loop fusion | flops 589824 | bytes 7077892 | tf_op jit(solution)/shard_map/add | solution.py:32
  131.2 1.6 constant_dynamic-slice_fusion.12
  132.8 2.9 %copy.85 = f32[288,1024]{1,0:T(8,128)} copy(f32[288,1024]{0,1:T(8,128)} %constant_dynamic-slice_fusion.12) | data formatting | bytes 2359296 | tf_op jit(solution)/shard_map/dynamic_slice | solution.py:31
  136.0 12.8 %fusion.51 = f32[256,2048]{1,0:T(8,128)} fusion(f32[256,2048]{1,0:T(8,128)} %param.3, f32[2048,2048]{1,0:T(8,128)} %param.5), kind=kOutput, calls=%fused_computation.137 | convolution fusion | flops 6442450944 | bytes 20971520 | tf_op jit(solution)/shard_map/dot_general | solution.py:113
  148.8 1.8 dynamic-slice_add_fusion.5
  151.6 1.8 collective-permute-start.10
  153.4 15.3 %collective-permute-done.13 = f32[256,1024]{1,0:T(8,128)} collective-permute-done((f32[256,1024]{1,0:T(8,128)}, f32[256,1024]{1,0:T(8,128)}, u32[]{:S(2)}, u32[]{:S(2)}) %collective-permute-start.13) | collective-permute-done | bytes 1048608 | tf_op jit(solution)/shard_map/ppermute | solution.py:24
  168.7 1.4 dynamic-slice_add_fusion.4
  171.2 1.6 collective-permute-start.14
  172.8 20.6 %collective-permute-done.3 = f32[288,1024]{1,0:T(8,128)} collective-permute-done((f32[288,1024]{1,0:T(8,128)}, f32[288,1024]{1,0:T(8,128)}, u32[]{:S(2)}, u32[]{:S(2)}) %collective-permute-start.3) | collective-permute-done | bytes 1179680 | tf_op jit(solution)/shard_map/ppermute | solution.py:24
  193.4 2.9 %copy.86 = f32[288,1024]{0,1:T(8,128)} copy(f32[288,1024]{1,0:T(8,128)} %collective-permute-done.3) | data formatting | bytes 2359296 | tf_op jit(solution)/shard_map/ppermute | solution.py:24
  196.3 1.9 dynamic-slice_add_fusion.3
  200.6 1.6 collective-permute-start.4
  203.3 2.6 collective-permute-start.11
  207.1 14.2 %collective-permute-done.4 = f32[288,512]{1,0:T(8,128)} collective-permute-done((f32[288,512]{1,0:T(8,128)}, f32[288,512]{1,0:T(8,128)}, u32[]{:S(2)}, u32[]{:S(2)}) %collective-permute-start.4) | collective-permute-done | bytes 589856 | tf_op jit(solution)/shard_map/ppermute | solution.py:24
  221.3 1.3 copy.88
  222.8 1.8 collective-permute-start.5
  224.5 1.3 collective-permute-start.15
  226.8 21.7 %collective-permute-done.5 = f32[288,256]{0,1:T(8,128)S(1)} collective-permute-done((f32[288,256]{0,1:T(8,128)S(1)}, f32[288,256]{0,1:T(8,128)S(1)}, u32[]{:S(2)}, u32[]{:S(2)}) %collective-permute-start.5) | collective-permute-done | bytes 294944 | tf_op jit(solution)/shard_map/ppermute | solution.py:24
  248.8 2.4 collective-permute-start.6
  251.1 1.9 collective-permute-done.15
  254.0 31.9 %all-gather = f32[256,256]{1,0:T(8,128)S(1)} all-gather(f32[32,256]{1,0:T(8,128)S(1)} %copy.89), channel_id=2, replica_groups=mesh['row'=4,'col'=8] {'col'}, dimensions={0}, use_global_device_ids=true | all-gather | bytes 294912 | tf_op jit(solution)/shard_map/all_gather | solution.py:100
  (95 shorter events, 29.2 us)
Async XLA Ops:
  8.8 1.9 copy-start.8
  9.1 26.2 %collective-permute-start = (f32[256,4,256]{2,0,1:T(8,128)S(1)}, f32[256,4,256]{2,0,1:T(8,128)}, u32[]{:S(2)}, u32[]{:S(2)}) collective-permute-start(f32[256,4,256]{2,0,1:T(8,128)S(1)} %bitcast.70), channel_id=1, source_target_pairs={{0,1},{1,0},{2,3},{3,2},{4,5},{5,4},{6,7},{7,6},{8,9},{9,8},{10,11... | collective-permute-start | bytes 3145736 | tf_op jit(solution)/shard_map/ppermute | solution.py:24
  11.1 46.7 %collective-permute-start.1 = (f32[256,4,256]{2,0,1:T(8,128)S(1)}, f32[256,4,256]{2,0,1:T(8,128)S(1)}, u32[]{:S(2)}, u32[]{:S(2)}) collective-permute-start(f32[256,4,256]{2,0,1:T(8,128)S(1)} %bitcast.74), channel_id=1, source_target_pairs={{0,1},{1,0},{2,3},{3,2},{4,5},{5,4},{6,7},{7,6},{8,9},{9,8},{10,11... | collective-permute-start | bytes 3145736 | tf_op jit(solution)/shard_map/ppermute | solution.py:24
  14.5 64.6 %collective-permute-start.7 = (f32[256,4,256]{2,0,1:T(8,128)}, f32[256,4,256]{2,0,1:T(8,128)}, u32[]{:S(2)}, u32[]{:S(2)}) collective-permute-start(f32[256,4,256]{2,0,1:T(8,128)} %bitcast.82), channel_id=1, source_target_pairs={{0,1},{1,0},{2,3},{3,2},{4,5},{5,4},{6,7},{7,6},{8,9},{9,8},{10,11... | collective-permute-start | bytes 3145736 | tf_op jit(solution)/shard_map/ppermute | solution.py:24
  63.3 15.8 %copy-start.13 = (f32[256,4,1,256]{3,0,2,1:T(8,128)S(1)}, f32[256,4,1,256]{3,0,2,1:T(8,128)}, u32[]{:S(2)}) copy-start(f32[256,4,1,256]{3,0,2,1:T(8,128)} %copy.94) | copy-start | bytes 3145732
  84.0 2.7 copy-start.5
  86.7 29.3 %collective-permute-start.8 = (f32[512,1024]{1,0:T(8,128)}, f32[512,1024]{1,0:T(8,128)}, u32[]{:S(2)}, u32[]{:S(2)}) collective-permute-start(f32[512,1024]{1,0:T(8,128)} %constant_dynamic-slice_fusion.7), channel_id=1, source_target_pairs={{0,8},{8,0},{16,24},{24,16},{1,9},{9,1},{17,25},{25,17},{2,10},{10... | collective-permute-start | bytes 6291464 | tf_op jit(solution)/shard_map/ppermute | solution.py:24
  93.7 2.7 copy-start.6
  96.4 23.8 %collective-permute-start.12 = (f32[512,1024]{1,0:T(8,128)}, f32[512,1024]{1,0:T(8,128)}, u32[]{:S(2)}, u32[]{:S(2)}) collective-permute-start(f32[512,1024]{1,0:T(8,128)} %constant_dynamic-slice_fusion.3), channel_id=1, source_target_pairs={{0,8},{8,0},{16,24},{24,16},{1,9},{9,1},{17,25},{25,17},{2,10},{10... | collective-permute-start | bytes 6291464 | tf_op jit(solution)/shard_map/ppermute | solution.py:24
  115.8 9.9 %collective-permute-start.2 = (f32[576,1024]{1,0:T(8,128)}, f32[576,1024]{1,0:T(8,128)S(1)}, u32[]{:S(2)}, u32[]{:S(2)}) collective-permute-start(f32[576,1024]{1,0:T(8,128)} %copy.83), channel_id=1, source_target_pairs={{0,8},{8,0},{16,24},{24,16},{1,9},{9,1},{17,25},{25,17},{2,10},{10... | collective-permute-start | bytes 7077896 | tf_op jit(solution)/shard_map/ppermute | solution.py:24
  116.0 4.3 %copy-start.7 = (f32[1024,1024]{1,0:T(8,128)S(1)}, f32[1024,1024]{1,0:T(8,128)}, u32[]{:S(2)}) copy-start(f32[1024,1024]{1,0:T(8,128)} %copy-done.6) | copy-start | bytes 12582916
  118.8 3.5 %copy-start = (f32[512,1024]{1,0:T(8,128)}, f32[512,1024]{1,0:T(8,128)S(1)}, u32[]{:S(2)}) copy-start(f32[512,1024]{1,0:T(8,128)S(1)} %dynamic-slice_add_fusion.2) | copy-start | bytes 6291460
  119.9 28.9 %collective-permute-start.9 = (f32[256,1024]{1,0:T(8,128)}, f32[256,1024]{1,0:T(8,128)}, u32[]{:S(2)}, u32[]{:S(2)}) collective-permute-start(f32[256,1024]{1,0:T(8,128)} %constant_dynamic-slice_fusion.6), channel_id=1, source_target_pairs={{0,16},{8,24},{16,0},{24,8},{1,17},{9,25},{17,1},{25,9},{2,18},{10... | collective-permute-start | bytes 3145736 | tf_op jit(solution)/shard_map/ppermute | solution.py:24
  122.2 1.8 copy-start.1
  124.0 44.7 %collective-permute-start.13 = (f32[256,1024]{1,0:T(8,128)}, f32[256,1024]{1,0:T(8,128)}, u32[]{:S(2)}, u32[]{:S(2)}) collective-permute-start(f32[256,1024]{1,0:T(8,128)} %constant_dynamic-slice_fusion.2), channel_id=1, source_target_pairs={{0,16},{8,24},{16,0},{24,8},{1,17},{9,25},{17,1},{25,9},{2,18},{10... | collective-permute-start | bytes 3145736 | tf_op jit(solution)/shard_map/ppermute | solution.py:24
  135.7 57.7 %collective-permute-start.3 = (f32[288,1024]{1,0:T(8,128)}, f32[288,1024]{1,0:T(8,128)}, u32[]{:S(2)}, u32[]{:S(2)}) collective-permute-start(f32[288,1024]{1,0:T(8,128)} %copy.85), channel_id=1, source_target_pairs={{0,16},{8,24},{16,0},{24,8},{1,17},{9,25},{17,1},{25,9},{2,18},{10... | collective-permute-start | bytes 3538952 | tf_op jit(solution)/shard_map/ppermute | solution.py:24
  148.8 19.9 %copy-start.2 = (f32[512,1024]{1,0:T(8,128)S(1)}, f32[512,1024]{1,0:T(8,128)}, u32[]{:S(2)}) copy-start(f32[512,1024]{1,0:T(8,128)} %copy-done.1) | copy-start | bytes 6291460
  150.7 19.4 %copy-start.9 = (f32[256,1024]{1,0:T(8,128)}, f32[256,1024]{1,0:T(8,128)S(1)}, u32[]{:S(2)}) copy-start(f32[256,1024]{1,0:T(8,128)S(1)} %dynamic-slice_add_fusion.5) | copy-start | bytes 3145732
  151.6 50.6 %collective-permute-start.10 = (f32[256,512]{1,0:T(8,128)}, f32[256,512]{1,0:T(8,128)}, u32[]{:S(2)}, u32[]{:S(2)}) collective-permute-start(f32[256,512]{1,0:T(8,128)} %constant_dynamic-slice_fusion.5), channel_id=1, source_target_pairs={{0,2},{1,3},{2,0},{3,1},{4,6},{5,7},{6,4},{7,5},{8,10},{9,11},{10,... | collective-permute-start | bytes 1572872 | tf_op jit(solution)/shard_map/ppermute | solution.py:24
  170.1 1.1 copy-start.11
  171.2 34.8 %collective-permute-start.14 = (f32[256,512]{1,0:T(8,128)}, f32[256,512]{1,0:T(8,128)}, u32[]{:S(2)}, u32[]{:S(2)}) collective-permute-start(f32[256,512]{1,0:T(8,128)} %constant_dynamic-slice_fusion.1), channel_id=1, source_target_pairs={{0,2},{1,3},{2,0},{3,1},{4,6},{5,7},{6,4},{7,5},{8,10},{9,11},{10,... | collective-permute-start | bytes 1572872 | tf_op jit(solution)/shard_map/ppermute | solution.py:24
  198.2 1.2 copy-start.3
  199.4 2.7 copy-start.10
  199.5 6.5 %copy-start.12 = (f32[256,1024]{1,0:T(8,128)S(1)}, f32[256,1024]{1,0:T(8,128)}, u32[]{:S(2)}) copy-start(f32[256,1024]{1,0:T(8,128)} %copy-done.11) | copy-start | bytes 3145732
  200.6 20.7 %collective-permute-start.4 = (f32[288,512]{1,0:T(8,128)}, f32[288,512]{1,0:T(8,128)}, u32[]{:S(2)}, u32[]{:S(2)}) collective-permute-start(f32[288,512]{1,0:T(8,128)} %copy.87), channel_id=1, source_target_pairs={{0,2},{1,3},{2,0},{3,1},{4,6},{5,7},{6,4},{7,5},{8,10},{9,11},{10,... | collective-permute-start | bytes 1769480 | tf_op jit(solution)/shard_map/ppermute | solution.py:24
  203.3 3.8 %copy-start.14 = (f32[256,512]{1,0:T(8,128)}, f32[256,512]{1,0:T(8,128)S(1)}, u32[]{:S(2)}) copy-start(f32[256,512]{1,0:T(8,128)S(1)} %dynamic-slice_add_fusion.8) | copy-start | bytes 1572868
  203.3 19.3 %copy-start.4 = (f32[288,1024]{0,1:T(8,128)S(1)}, f32[288,1024]{0,1:T(8,128)}, u32[]{:S(2)}) copy-start(f32[288,1024]{0,1:T(8,128)} %copy-done.3) | copy-start | bytes 3538948
  203.3 22.5 %collective-permute-start.11 = (f32[256,256]{1,0:T(8,128)S(1)}, f32[256,256]{1,0:T(8,128)}, u32[]{:S(2)}, u32[]{:S(2)}) collective-permute-start(f32[256,256]{1,0:T(8,128)S(1)} %constant_dynamic-slice_fusion.4), channel_id=1, source_target_pairs={{0,4},{1,5},{2,6},{3,7},{4,0},{5,1},{6,2},{7,3},{8,12},{9,13},{10,... | collective-permute-start | bytes 786440 | tf_op jit(solution)/shard_map/ppermute | solution.py:24
  222.6 3.2 %copy-start.15 = (f32[256,512]{1,0:T(8,128)S(1)}, f32[256,512]{1,0:T(8,128)}, u32[]{:S(2)}) copy-start(f32[256,512]{1,0:T(8,128)} %copy-done.14) | copy-start | bytes 1572868
  222.8 25.8 %collective-permute-start.5 = (f32[288,256]{0,1:T(8,128)S(1)}, f32[288,256]{0,1:T(8,128)S(1)}, u32[]{:S(2)}, u32[]{:S(2)}) collective-permute-start(f32[288,256]{0,1:T(8,128)S(1)} %constant_dynamic-slice_fusion.10), channel_id=1, source_target_pairs={{0,4},{1,5},{2,6},{3,7},{4,0},{5,1},{6,2},{7,3},{8,12},{9,13},{10,... | collective-permute-start | bytes 884744 | tf_op jit(solution)/shard_map/ppermute | solution.py:24
  224.5 28.5 %collective-permute-start.15 = (f32[256,256]{1,0:T(8,128)S(1)}, f32[256,256]{1,0:T(8,128)S(1)}, u32[]{:S(2)}, u32[]{:S(2)}) collective-permute-start(f32[256,256]{1,0:T(8,128)S(1)} %constant_dynamic-slice_fusion), channel_id=1, source_target_pairs={{0,4},{1,5},{2,6},{3,7},{4,0},{5,1},{6,2},{7,3},{8,12},{9,13},{10,... | collective-permute-start | bytes 786440 | tf_op jit(solution)/shard_map/ppermute | solution.py:24
  248.8 37.3 %collective-permute-start.6 = (f32[256,256]{0,1:T(8,128)S(1)}, f32[256,256]{0,1:T(8,128)S(1)}, u32[]{:S(2)}, u32[]{:S(2)}) collective-permute-start(f32[256,256]{0,1:T(8,128)S(1)} %bitcast.84), channel_id=1, source_target_pairs={{2,8},{3,9},{4,16},{5,17},{6,24},{7,25},{8,3},{9,2},{12,18},{13,19... | collective-permute-start | bytes 786440 | tf_op jit(solution)/shard_map/ppermute | solution.py:99

commit v2 on v0

v2 whole, which is shorter than its diff:
```python
import jax
import jax.numpy as jnp
from jax import lax
from jax.experimental import pallas as pl
from jax.experimental.pallas import tpu as pltpu
from jax.sharding import PartitionSpec as P


VMEM_LIMIT = 48 * 2**20


def split(value):
    high = value.astype(jnp.bfloat16)
    return high, (value - high.astype(jnp.float32)).astype(jnp.bfloat16)


def multiply(left, right):
    dot = lambda a, b: jnp.dot(a, b, preferred_element_type=jnp.float32)
    (lh, ll), (rh, rl) = left, right
    return dot(lh, rh) + (dot(ll, rh) + dot(lh, rl))


class Device:
    def __init__(self, orbitals):
        self.R, self.C = lax.axis_size("row"), lax.axis_size("col")
        self.X, self.Z = self.R // 2, self.C // 2
        self.b = orbitals // self.C
        r, c = lax.axis_index("row"), lax.axis_index("col")
        self.r, self.c, self.y, self.z = r, c, c % 2, c // 2
        x_bits = self.X.bit_length() - 1
        z_bits = self.Z.bit_length() - 1
        self.bits = [r % 2, self.y]
        self.bits += [(r >> (1 + i)) & 1 for i in range(x_bits)]
        self.bits += [(self.z >> i) & 1 for i in range(z_bits)]
        self.x_top = 1 + x_bits
        self.x_rest = list(range(2, 1 + x_bits))
        self.z_bits = list(range(2 + x_bits, 2 + x_bits + z_bits))
        self.at = jnp.stack(self.bits + [r, self.z]).astype(jnp.int32)
        self.last, self.waits = None, []

    def axis_bit(self, bit):
        if bit < self.z_bits[0]:
            return "row", bit - 1
        return "col", bit - self.z_bits[0] + 1

    def swap(self, value, bit):
        axis, shift = self.axis_bit(bit)
        return flip(value, axis, 1 << shift)

    def wait(self, total):
        self.waits += total.terms[-1][0]

    def call(self, body, name, arrays, in_specs, out_shapes, out_specs, grid=(), scratch=()):
        after = ([] if self.last is None else [self.last]) + self.waits
        self.waits = []
        count = len(arrays)

        def ordered(at, *refs):
            body(at, *refs[:count], *refs[count + len(after) :])

        outs = pl.pallas_call(
            ordered,
            name=name,
            out_shape=[jax.ShapeDtypeStruct(s, jnp.float32) for s in out_shapes],
            grid_spec=pltpu.PrefetchScalarGridSpec(
                num_scalar_prefetch=1,
                grid=grid,
                in_specs=list(in_specs) + [pl.BlockSpec(memory_space=pl.ANY)] * len(after),
                out_specs=list(out_specs),
                scratch_shapes=list(scratch),
            ),
            compiler_params=pltpu.CompilerParams(vmem_limit_bytes=VMEM_LIMIT),
            cost_estimate=pl.CostEstimate(flops=0, bytes_accessed=0, transcendentals=0),
        )(self.at, *arrays, *after)
        self.last = outs[0]
        return outs


def flip(value, axis, mask):
    count = lax.axis_size(axis)
    return lax.ppermute(value, axis, [(i, i ^ mask) for i in range(count)])


VMEM = pl.BlockSpec(memory_space=pltpu.VMEM)


def after(value, other):
    return lax.optimization_barrier((value, other))[0]


def whole(array):
    return pl.BlockSpec(array.shape, lambda i, at: (0,) * array.ndim)


def part(dev, name, array):
    cells, b = array.shape[0], dev.b

    def body(at, source, own, other):
        even, odd = source[:, :b], source[:, b:]
        first = at[1] == 0
        own[...] = jnp.where(first, even, odd)
        other[...] = jnp.where(first, odd, even)

    block = lambda width: pl.BlockSpec((cells, width), lambda i, at: (0, i))
    return dev.call(
        body, name, [array], [block(2 * b)], [(cells, dev.R * b)] * 2,
        [block(b)] * 2, grid=(dev.R,),
    )


def part_cores(dev, own, other, image):
    cells, b, X, Z = own.shape[0], dev.b, dev.X, dev.Z
    n = Z * b

    def body(at, image, other, own, for_core, for_near):
        for_core[:, :n] = image[...]
        for xi in range(X):
            block = slice(xi * b, (xi + 1) * b)
            for side in range(2):
                r = slice((2 * xi + side) * b, (2 * xi + side + 1) * b)

                @pl.when(at[0] == side)
                def _(block=block, r=r):
                    for_near[:cells, block] = own[:, r]

                @pl.when(at[0] != side)
                def _(block=block, r=r, xi=xi):
                    for_near[cells:, block] = own[:, r]
                    for_core[:, n + xi * b : n + (xi + 1) * b] = other[:, r]

    return dev.call(
        body, "part_cores", [image, other, own], [VMEM] * 3,
        [(cells, n + X * b), (2 * cells, X * b)], [VMEM] * 2,
    )


class Rows:
    def __init__(self, dev, *sources):
        self.X = dev.X
        self.arrays, self.specs, self.cells = [], [], []
        for array, cells, index in sources:
            self.cells.append(cells)
            for xi in range(dev.X):
                self.arrays.append(array)
                self.specs.append(
                    pl.BlockSpec((cells, dev.b), lambda i, at, xi=xi, index=index: index(xi, at))
                )

    def blocks(self, refs):
        return [
            [ref[...] for ref in refs[m * self.X : (m + 1) * self.X]]
            for m in range(len(self.cells))
        ]


def column_blocks(dev, name, rows, cut, width, columns, zs, writes, out_rows):
    X, b = dev.X, dev.b
    top = X // 2
    first, stride = zs
    steps = dev.Z // stride
    nr, nc = len(rows.arrays), len(columns)
    total = sum(rows.cells)

    def body(at, *refs):
        lefts, rights = refs[:nr], refs[nr : nr + nc]
        keep, send, high, low = refs[nr + nc :]

        @pl.when(pl.program_id(0) == 0)
        def _():
            start = 0
            for cells, blocks in zip(rows.cells, rows.blocks(lefts)):
                for xi, block in enumerate(blocks):
                    index = (slice(xi * width, (xi + 1) * width), slice(start, start + cells))
                    turned = block.T[cut * width : (cut + 1) * width]
                    high[index], low[index] = split(turned)
                start += cells

        right = split(jnp.concatenate([ref[...] for ref in rights], 0))
        value = multiply((high[...], low[...]), right)
        zz = stride * pl.program_id(0) + first
        for xi in range(X):
            part = value[xi * width : (xi + 1) * width]
            for side, target in ((at[dev.x_top], keep), (1 - at[dev.x_top], send)):
                for at_rows, condition, result in writes(at, 2 * xi + at[0], zz, part):
                    flag = side == xi // top
                    if condition is not None:
                        flag = jnp.logical_and(flag, condition)

                    @pl.when(flag)
                    def _(target=target, at_rows=at_rows, result=result):
                        target[xi % top, 0, at_rows] = result()

    out = pl.BlockSpec((top, 1, out_rows, b), lambda i, at: (0, i, 0, 0))
    return dev.call(
        body, name, [*rows.arrays, *columns],
        rows.specs
        + [
            pl.BlockSpec((array.shape[0], b), lambda i, at: (0, stride * i + first))
            for array in columns
        ],
        [(top, steps, out_rows, b)] * 2, [out] * 2, grid=(steps,),
        scratch=[pltpu.VMEM((X * width, total), jnp.bfloat16)] * 2,
    )


def project(dev, rows, cut, width, images, zs=(0, 1)):
    writes = lambda at, r, zz, part: [(slice(None), None, lambda: part)]
    return column_blocks(dev, "project", rows, cut, width, images, zs, writes, width)


def lower_rows(dev):
    half = dev.b // 2
    return half // 2 if half % 128 == 0 else half


def overlap(dev, rows, columns, same):
    b = dev.b
    half = b // 2
    more = lower_rows(dev) if same else 0

    def mirrored(part):
        return part[:, half:].T if half % 128 == 0 else part.T[half:]

    def lower(part):
        if more == half:
            return part[half:]
        corner = part[half:, half:]
        return jnp.concatenate([corner[:more], corner[more:]], 1)

    def writes(at, r, zz, part):
        straight = (r <= zz) if same else (at[1] == 0)
        out = [
            (slice(0, half), straight, lambda: part[:half]),
            (slice(0, half), jnp.logical_not(straight), lambda: mirrored(part)),
        ]
        if same:
            out += [
                (slice(half, half + more), r == zz, lambda: lower(part)),
                (slice(half, half + more), r != zz, lambda: jnp.zeros((more, b), jnp.float32)),
            ]
        return out

    return column_blocks(
        dev, "overlap_same" if same else "overlap_mixed", rows, 0, b, columns, (0, 1),
        writes, half + more,
    )


class Sum:
    def __init__(self, rows, *terms):
        self.rows = rows
        self.terms = [(term, [], [], 0) for term in terms]

    def counts(self):
        arrays, xs, zs, _ = self.terms[0]
        n0, n1 = arrays[0].shape[:2]
        return n0 >> len(xs), (n1 * len(arrays)) >> len(zs)


def gather(dev, body, name, sums, pick, arrays_in, out_shapes):
    arrays, slots, shapes = [], [], []
    for total in sums:
        n0, n1 = total.counts()
        if pick == "every":
            n1 = dev.Z - 1
        elif pick is not None:
            n0, n1 = (n0 // 2, n1) if pick[0] == "x" else (n0, n1 // 2)
        for term, _, _, _ in total.terms:
            slots.append(list(range(len(arrays), len(arrays) + len(term))))
            arrays += term
            shapes.append((n0, n1, total.rows, dev.b))
    count, more = len(arrays), len(arrays_in)

    def kernel(at, *refs):
        sources, refs = refs[:count], refs[count:]
        inputs, refs = refs[:more], refs[more:]
        outs, refs = refs[: len(out_shapes)], refs[len(out_shapes) :]
        buffers, sems = refs[:-1], refs[-1]
        waits, k = [], 0
        for total in sums:
            for _, xs, zs, row in total.terms:
                n0, n1, rows, _ = shapes[k]
                xs = [at[bit] for bit in xs]
                zs = [at[bit] for bit in zs]
                if pick == "every":
                    zs = []
                elif pick is not None:
                    (xs if pick[0] == "x" else zs).append(1 - at[pick[1]])
                x_step, z_step = 1 << len(xs), 1 << len(zs)
                x_base = sum((v << i for i, v in enumerate(xs)), 0)
                z_base = sum((v << i for i, v in enumerate(zs)), 0)
                for i in range(n0):
                    for j in range(n1):
                        xi, zi = i * x_step + x_base, j * z_step + z_base
                        if pick == "every":
                            zi = at[len(dev.bits) + 1] ^ (j + 1)
                        target, sem = buffers[k].at[i, j], sems.at[k, i * n1 + j]
                        pair = [sources[slot] for slot in slots[k]]
                        take = zi if len(pair) == 1 else zi // 2
                        copies = [
                            pltpu.make_async_copy(ref.at[xi, take, pl.ds(row, rows)], target, sem)
                            for ref in pair
                        ]
                        if len(pair) == 1:
                            copies[0].start()
                        else:
                            for parity in range(2):
                                pl.when(zi % 2 == parity)(copies[parity].start)
                        waits.append(copies[0])
                k += 1
        for copy in waits:
            copy.wait()
        values, k = [], 0
        for total in sums:
            values.append(buffers[k : k + len(total.terms)])
            k += len(total.terms)
        body(at, values, inputs, outs)

    most = max(shape[0] * shape[1] for shape in shapes)
    return dev.call(
        kernel, name, arrays + arrays_in,
        [pl.BlockSpec(memory_space=pl.ANY)] * count + [VMEM] * more,
        out_shapes, [VMEM] * len(out_shapes),
        scratch=[pltpu.VMEM(shape, jnp.float32) for shape in shapes]
        + [pltpu.SemaphoreType.DMA((len(shapes), most))],
    )


def added(buffers, index):
    total = buffers[0][index]
    for buffer in buffers[1:]:
        total = total + buffer[index]
    return total


def halve(dev, sums, kind, bit):
    n0, n1 = sums[0].counts()
    n0, n1 = (n0 // 2, n1) if kind == "x" else (n0, n1 // 2)
    firsts = [sum(total.rows for total in sums[:k]) for k in range(len(sums) + 1)]

    def body(at, values, inputs, outs):
        for k, total in enumerate(sums):
            for i in range(n0):
                for j in range(n1):
                    outs[0][i, j, firsts[k] : firsts[k + 1]] = added(values[k], (i, j))

    (out,) = gather(
        dev, body, "halve", sums, (kind, bit), [], [(n0, n1, firsts[-1], dev.b)]
    )
    came = dev.swap(out, bit)
    for first, total in zip(firsts, sums):
        total.terms = [
            (arrays, xs + [bit] * (kind == "x"), zs + [bit] * (kind == "z"), row)
            for arrays, xs, zs, row in total.terms
        ] + [((came,), [], [], first)]


def scatter(dev, sums):
    firsts = [sum(total.rows for total in sums[:k]) for k in range(len(sums) + 1)]
    n0 = sums[0].counts()[0]
    others = range(1, dev.Z)

    def body(at, values, inputs, outs):
        for j, out in enumerate(outs):
            for k, total in enumerate(sums):
                for i in range(n0):
                    out[i, 0, firsts[k] : firsts[k + 1]] = added(values[k], (i, j))

    outs = gather(
        dev, body, "scatter", sums, "every", [], [(n0, 1, firsts[-1], dev.b) for _ in others]
    )
    came = [flip(out, "col", 2 * mask) for mask, out in zip(others, outs)]
    for first, total in zip(firsts, sums):
        total.terms = [(arrays, xs, dev.z_bits, row) for arrays, xs, zs, row in total.terms]
        total.terms += [((array,), [], [], first) for array in came]


def finish(dev, total, scale):
    def body(at, values, inputs, outs):
        outs[0][...] = added(values[0], (0, 0)) * scale

    return gather(dev, body, "finish", [total], None, [], [(total.rows, dev.b)])[0]


def assemble_overlap(dev, same, same_half, mixed, mixed_half):
    b = dev.b
    half = b // 2
    more = lower_rows(dev)
    last = len(dev.bits)

    def body(at, same, same_half, mixed, mixed_half, out):
        r, z = at[last], at[last + 1]
        first = pl.multiple_of(at[1] * b, b)
        second = pl.multiple_of((1 - at[1]) * b, b)
        mine = same[:half]

        @pl.when(r < z)
        def _():
            out[pl.ds(first, b)] = jnp.concatenate([mine, same_half[...]], 0)

        @pl.when(r > z)
        def _():
            out[pl.ds(first, b)] = jnp.concatenate([same_half[...], mine], 0).T

        @pl.when(r == z)
        def _():
            lower = same[half:]
            if more < half:
                corner = jnp.concatenate([lower[:, :half], lower[:, half:]], 0)
                lower = jnp.concatenate([mine[:, half:].T, corner], 1)
            out[pl.ds(first, b)] = jnp.concatenate([mine, lower], 0)

        @pl.when(at[1] == 0)
        def _():
            out[pl.ds(second, b)] = jnp.concatenate([mixed[...], mixed_half[...]], 0)

        @pl.when(at[1] == 1)
        def _():
            out[pl.ds(second, b)] = jnp.concatenate([mixed_half[...], mixed[...]], 0).T

    arrays = [same, same_half, mixed, mixed_half]
    return dev.call(
        body, "assemble_overlap", arrays, [VMEM] * 4, [(2 * b, b)], [VMEM]
    )[0]


def rotate(dev, array, rotation):
    cells, orbitals = array.shape
    width = 256 if orbitals % 256 == 0 else orbitals

    def body(at, array, block, out, high, low):
        @pl.when(pl.program_id(0) == 0)
        def _():
            high[...], low[...] = split(array[...])

        out[...] = multiply((high[...], low[...]), split(block[...]))

    return dev.call(
        body, "rotate", [array, rotation],
        [whole(array), pl.BlockSpec((orbitals, width), lambda i, at: (0, i))],
        [array.shape], [pl.BlockSpec((cells, width), lambda i, at: (0, i))],
        grid=(orbitals // width,),
        scratch=[pltpu.VMEM((cells, orbitals), jnp.bfloat16)] * 2,
    )[0]


def local(filtered, hamiltonian_applied, rotation):
    cells, orbitals = filtered.shape
    dev = Device(orbitals)
    R, C, Z, b = dev.R, dev.C, dev.Z, dev.b
    half = b // 2
    scale = 1.0 / (cells * C * R)
    cuts = 2 if b % 256 == 0 else 1
    w = b // cuts

    across = lambda value: flip(value, "col", 1)
    core = lambda value: flip(value, "row", 1)

    def core_pieces(value):
        n = value.shape[0] // 2
        return [core(value[:n]), core(value[n:])]

    own, other = part(dev, "part_orbitals", filtered)
    near = across(other)
    image, image_other = part(dev, "part_images", hamiltonian_applied)
    image_near = across(image_other)
    for_core, for_near = part_cores(dev, own, other, image)
    far = across(for_near)
    own_core, from_core = core(own), core(for_core)
    rotated = rotate(dev, filtered, rotation)

    def reduced_x(rows, keep, send):
        total = Sum(rows, (keep,), (dev.swap(send, dev.x_top),))
        for bit in dev.x_rest:
            halve(dev, [total], "x", bit)
        return total

    near_core = core_pieces(after(near, rotated))
    columns = [own, own_core, near, *near_core]
    this = lambda xi, at: (0, 2 * xi + at[0])
    rows = Rows(dev, *((array, array.shape[0], this) for array in columns))
    same = reduced_x(half + lower_rows(dev), *overlap(dev, rows, columns, True))

    images = [image, from_core, image_near, *core_pieces(after(image_near, dev.last))]
    dev.wait(same)
    even = reduced_x(b, *project(dev, rows, 0, b, images, (0, 2)))
    halve(dev, [same], "z", dev.z_bits[0])
    odd = reduced_x(b, *project(dev, rows, 0, b, images, (1, 2)))
    proj_own = Sum(b)
    proj_own.terms = [(e[0] + o[0], *e[1:]) for e, o in zip(even.terms, odd.terms)]

    far_there = after(far, dev.last)[cells:]
    far_core = core_pieces(far_there)
    dev.wait(even)
    halve(dev, [same], "z", dev.z_bits[1])
    far_rows = Rows(
        dev,
        (other, cells, this),
        (from_core, cells, lambda xi, at: (0, Z + xi)),
        (far, cells, lambda xi, at: (0, xi)),
        *((array, array.shape[0], lambda xi, at: (0, xi)) for array in far_core),
    )
    proj_other = [reduced_x(w, *project(dev, far_rows, 0, w, images))]
    halve(dev, [proj_own], "z", dev.z_bits[0])
    mixed = reduced_x(half, *overlap(dev, far_rows, columns, False))
    for bit in dev.z_bits[2:]:
        halve(dev, [same], "z", bit)
    same = finish(dev, same, scale)
    same_pairs = [
        (i * C + 2 * j + p, j * C + 2 * i + p)
        for i in range(R) for j in range(Z) for p in range(2) if i != j
    ]
    same_half = lax.ppermute(same[:half], ("row", "col"), same_pairs)
    dev.wait(proj_other[0])
    for n in range(1, cuts):
        proj_other.append(reduced_x(w, *project(dev, far_rows, n, w, images)))
    for bit in dev.z_bits[1:]:
        halve(dev, [proj_own], "z", bit)
    halve(dev, [proj_other[0]], "z", dev.z_bits[0])
    scatter(dev, [mixed])
    for total in proj_other[1:]:
        scatter(dev, [total])
    for bit in dev.z_bits[1:]:
        halve(dev, [proj_other[0]], "z", bit)
    mixed = finish(dev, mixed, scale)
    mixed_pairs = [
        (i * C + 2 * j + p, j * C + 2 * i + 1 - p)
        for i in range(R) for j in range(Z) for p in range(2)
    ]
    mixed_half = lax.ppermute(mixed, ("row", "col"), mixed_pairs)

    def assemble(at, values, inputs, outs):
        first = pl.multiple_of(at[1] * b, b)
        second = pl.multiple_of((1 - at[1]) * b, b)
        outs[0][pl.ds(first, b)] = added(values[0], (0, 0)) * scale
        for n in range(cuts):
            outs[0][pl.ds(second + n * w, w)] = added(values[1 + n], (0, 0)) * scale

    (projected,) = gather(
        dev, assemble, "assemble", [proj_own, *proj_other], None, [], [(2 * b, b)]
    )
    intersection = assemble_overlap(dev, same, same_half, mixed, mixed_half)
    return (intersection, projected, rotated)


def solution(mesh):
    return jax.shard_map(
        local,
        mesh=mesh,
        in_specs=(P(("row", "col"), None), P(("row", "col"), None), P()),
        out_specs=(P("row", "col"), P("row", "col"), P(("row", "col"), None)),
        check_vma=False,
    )
```

time: 438 us -> 184 us (0.42)
  waiting for transfers between devices: 274 us -> 67 us
  matrix products: 77.4 us -> 0 us
  Pallas kernels: 0 us -> 68.8 us
  blocking collectives: 54.1 us -> 0 us
  starting transfers between devices: 4.81 us -> 42.8 us
  between operations: 13.8 us -> 1.03 us
  local copies, waits for them, and re-layouts: 11.6 us -> 3.52 us
    all_gather x1 -> x0, waiting for transfers between devices: 262 us -> none  [local(): piece = lax.all_gather(psi_band, 'col', axis=1, tiled=True)]
    dot_general x3 -> x0, matrix products: 77.4 us -> none  [the longest x2 59.6 us: inner_rows(): jnp.einsum('gi,gj->ij', first, second, precision=lax.Precision.HIGHEST, p...]
    pallas_call x0 -> x22, Pallas kernels: none -> 68.8 us  [call(): pl.pallas_call(ordered, name=name, out_shape=[jax.ShapeDtypeStruct(s, jnp...]
    ppermute x0 -> x31, waiting for transfers between devices: none -> 67 us  [the longest x29 58.6 us: flip(): return lax.ppermute(value, axis, [(i, i ^ mask) for i in range(count)])]
    all_to_all x1 -> x0, blocking collectives: 54.1 us -> none  [local(): lax.all_to_all(filtered, 'col', split_axis=1, concat_axis=0, tiled=True)]
    ppermute x0 -> x31, starting transfers between devices: none -> 42.8 us  [the longest x29 36.1 us: flip(): return lax.ppermute(value, axis, [(i, i ^ mask) for i in range(count)])]
    reduce_scatter x2 -> x0, waiting for transfers between devices: 11.8 us -> none  [the longest x1 11.8 us: local(): lax.psum_scatter(proj_term, 'row', scatter_dimension=0, tiled=True)]
    unnamed x8 -> x24, local copies, waits for them, and re-layouts: 7.86 us -> 3.19 us
  transfers between devices with their start and end apart: 4 -> 31, of which waited for: 2 -> 11; matrix products, arithmetic and copies ran while one was open for 19% -> 0% of each run, Pallas kernels for 0% -> 36%
where the time goes in v2:
time: 184 us; the launch traced here: 183 us
  Pallas kernels  68.8 us (37%)
  waiting for transfers between devices  67 us (36%)
  starting transfers between devices  42.8 us (23%)
  local copies, waits for them, and re-layouts  3.52 us (2%)
    pallas_call x22, Pallas kernels, call(): pl.pallas_call(ordered, name=name, out_shape=[jax.ShapeDtypeStruct(s, jnp...  68.8 us
    ppermute x29, waiting for transfers between devices, flip(): return lax.ppermute(value, axis, [(i, i ^ mask) for i in range(count)])  58.6 us
    ppermute x29, starting transfers between devices, flip(): return lax.ppermute(value, axis, [(i, i ^ mask) for i in range(count)])  36.1 us
    ppermute x1, waiting for transfers between devices, local(): same_half = lax.ppermute(same[:half], ('row', 'col'), same_pairs)  6.03 us
    ppermute x1, starting transfers between devices, local(): mixed_half = lax.ppermute(mixed, ('row', 'col'), mixed_pairs)  4.84 us
  transfers between devices with their start and end apart: 31, of which 11 were waited for; matrix products, arithmetic and copies ran while one was open for 0% of the time, Pallas kernels for 36%

profile of v2, /device:TPU:2, one launch (start us, length us, event | category | flops | bytes accessed | tf_op | source)
XLA Modules:
  0.0 183.1 jit_solution(6726544528768336159)
XLA Ops:
  0.7 1.6 copy-done.6
  2.3 1.1 part_orbitals.1
  3.4 1.6 collective-permute-start.1
  5.0 1.1 part_images.1
  6.7 0.8 part_cores.1
  8.3 13.7 %rotate.1.refs_15_ = f32[256,2048]{1,0:T(8,128)} custom-call(s32[7]{0:T(128)S(1)} %stack.31.at, f32[256,2048]{1,0:T(8,128)S(1)} %copy-done.7, f32[2048,2048]{1,0:T(8,128)} %refs_1_.1, f32[256,1536]{1,0:T(8,128)S(1)} %get-tuple-element.33.refs_2_), custom_call_target="tpu_custom_call" | custom-call | tf_op jit(solution)/shard_map/rotate/pallas_call | solution.py:61
  21.9 7.6 %collective-permute-done.1.refs_4_.refs_5_.refs_12_ = f32[256,1024]{1,0:T(8,128)S(1)} collective-permute-done((f32[256,1024]{1,0:T(8,128)S(1)}, f32[256,1024]{1,0:T(8,128)S(1)}, u32[]{:S(2)}, u32[]{:S(2)}) %collective-permute-start.1) | collective-permute-done | bytes 1048608 | tf_op jit(solution)/shard_map/ppermute | solution.py:81
  30.2 1.5 collective-permute-start.12
  32.4 6.6 %overlap_same.1 = (f32[1,4,192,256]{3,2,1,0:T(8,128)S(1)}, f32[1,4,192,256]{3,2,1,0:T(8,128)S(1)}) custom-call(s32[7]{0:T(128)S(1)} %stack.31.at, f32[256,1024]{1,0:T(8,128)S(1)} %get-tuple-element.30.refs_1_.refs_2_.refs_0_.refs_10_, f32[256,1024]{1,0:T(8,128)S(1)} %get-tuple-element.30.refs_1_.refs_2_.refs_0_.refs_10_, ...), custom_call_target="tpu_custom_call" | custom-call | tf_op jit(solution)/shard_map/overlap_same/pallas_call | solution.py:61
  39.0 13.0 %collective-permute-done.6.refs_12_ = f32[256,1024]{1,0:T(8,128)S(1)} collective-permute-done((f32[256,1024]{1,0:T(8,128)S(1)}, f32[256,1024]{1,0:T(8,128)S(1)}, u32[]{:S(2)}, u32[]{:S(2)}) %collective-permute-start.6) | collective-permute-done | bytes 1048608 | tf_op jit(solution)/shard_map/ppermute | solution.py:81
  52.7 1.4 collective-permute-done.8.refs_14_
  54.8 14.4 %collective-permute-done.4.refs_16_.refs_1_ = f32[1,4,192,256]{3,2,1,0:T(8,128)S(1)} collective-permute-done((f32[1,4,192,256]{3,2,1,0:T(8,128)S(1)}, f32[1,4,192,256]{3,2,1,0:T(8,128)S(1)}, u32[]{:S(2)}, u32[]{:S(2)}) %collective-permute-start.4) | collective-permute-done | bytes 786464 | tf_op jit(solution)/shard_map/ppermute | solution.py:81
  69.3 4.9 %project.4 = (f32[1,2,256,256]{3,2,1,0:T(8,128)S(1)}, f32[1,2,256,256]{3,2,1,0:T(8,128)S(1)}) custom-call(s32[7]{0:T(128)S(1)} %stack.31.at, f32[256,1024]{1,0:T(8,128)S(1)} %get-tuple-element.30.refs_1_.refs_2_.refs_0_.refs_10_, f32[256,1024]{1,0:T(8,128)S(1)} %get-tuple-element.30.refs_1_.refs_2_.refs_0_.refs_10_, f32[256,1024]{1,0:T(8,128)} %copy-done.2, ...), custom_call_target="tpu_custom_call" | custom-call | tf_op jit(solution)/shard_map/project/pallas_call | solution.py:61
  74.9 1.6 halve.6.refs_15_
  76.6 1.5 collective-permute-start.9
  78.1 4.8 %project.5 = (f32[1,2,256,256]{3,2,1,0:T(8,128)S(1)}, f32[1,2,256,256]{3,2,1,0:T(8,128)S(1)}) custom-call(s32[7]{0:T(128)S(1)} %stack.31.at, f32[256,1024]{1,0:T(8,128)S(1)} %get-tuple-element.30.refs_1_.refs_2_.refs_0_.refs_10_, f32[256,1024]{1,0:T(8,128)S(1)} %get-tuple-element.30.refs_1_.refs_2_.refs_0_.refs_10_, f32[256,1024]{1,0:T(8,128)S(1)} %copy-done.3, ...), custom_call_target="tpu_custom_call" | custom-call | tf_op jit(solution)/shard_map/project/pallas_call | solution.py:61
  83.5 1.5 collective-permute-start.15
  85.0 1.4 halve.7.refs_15_
  86.4 5.2 %project.6 = (f32[1,4,128,256]{3,2,1,0:T(8,128)S(1)}, f32[1,4,128,256]{3,2,1,0:T(8,128)S(1)}) custom-call(s32[7]{0:T(128)S(1)} %stack.31.at, f32[256,1024]{1,0:T(8,128)S(1)} %get-tuple-element.31.refs_1_.refs_0_, f32[256,1024]{1,0:T(8,128)S(1)} %get-tuple-element.31.refs_1_.refs_0_, f32[256,1536]{1,0:T(8,128)} %copy-done.10, f32[256,1536]{1,0:T(8,128)} %copy-done.10, ...), custom_call_target="tpu_custom_call" | custom-call | tf_op jit(solution)/shard_map/project/pallas_call | solution.py:61
  91.7 1.3 collective-permute-start.18
  93.0 5.3 %collective-permute-done.15.refs_3_ = f32[1,2,256,256]{3,2,1,0:T(8,128)S(1)} collective-permute-done((f32[1,2,256,256]{3,2,1,0:T(8,128)S(1)}, f32[1,2,256,256]{3,2,1,0:T(8,128)S(1)}, u32[]{:S(2)}, u32[]{:S(2)}) %collective-permute-start.15) | collective-permute-done | bytes 524320 | tf_op jit(solution)/shard_map/ppermute | solution.py:81
  98.3 1.0 halve.8.refs_15_
  99.9 2.5 %collective-permute-start.11 = (f32[1,1,192,256]{3,2,1,0:T(8,128)S(1)}, f32[1,1,192,256]{3,2,1,0:T(8,128)S(1)}, u32[]{:S(2)}, u32[]{:S(2)}) collective-permute-start(f32[1,1,192,256]{3,2,1,0:T(8,128)S(1)} %halve.7.refs_15_), channel_id=1, source_target_pairs={{0,4},{1,5},{2,6},{3,7},{4,0},{5,1},{6,2},{7,3},{8,12},{9,13},{10,... | collective-permute-start | bytes 589832 | tf_op jit(solution)/shard_map/ppermute | solution.py:81
  102.4 7.0 %overlap_mixed.1 = (f32[1,4,128,256]{3,2,1,0:T(8,128)S(1)}, f32[1,4,128,256]{3,2,1,0:T(8,128)S(1)}) custom-call(s32[7]{0:T(128)S(1)} %stack.31.at, f32[256,1024]{1,0:T(8,128)S(1)} %get-tuple-element.31.refs_1_.refs_0_, f32[256,1024]{1,0:T(8,128)S(1)} %get-tuple-element.31.refs_1_.refs_0_, f32[256,1536]{1,0:T(8,128)} %copy-done.10, f32[256,1536]{1,0:T(8,128)} %copy-done.10, ...), custom_call_target="tpu_custom_call" | custom-call | tf_op jit(solution)/shard_map/overlap_mixed/pallas_call | solution.py:61
  109.3 1.5 collective-permute-start.17
  110.9 2.9 %collective-permute-done.11.refs_3_ = f32[1,1,192,256]{3,2,1,0:T(8,128)S(1)} collective-permute-done((f32[1,1,192,256]{3,2,1,0:T(8,128)S(1)}, f32[1,1,192,256]{3,2,1,0:T(8,128)S(1)}, u32[]{:S(2)}, u32[]{:S(2)}) %collective-permute-start.11) | collective-permute-done | bytes 196640 | tf_op jit(solution)/shard_map/ppermute | solution.py:81
  113.8 1.6 finish.2.refs_15_.refs_0_
  115.5 5.4 %project.7 = (f32[1,4,128,256]{3,2,1,0:T(8,128)S(1)}, f32[1,4,128,256]{3,2,1,0:T(8,128)S(1)}) custom-call(s32[7]{0:T(128)S(1)} %stack.31.at, f32[256,1024]{1,0:T(8,128)S(1)} %get-tuple-element.31.refs_1_.refs_0_, f32[256,1024]{1,0:T(8,128)S(1)} %get-tuple-element.31.refs_1_.refs_0_, f32[256,1536]{1,0:T(8,128)} %copy-done.10, f32[256,1536]{1,0:T(8,128)} %copy-done.10, ...), custom_call_target="tpu_custom_call" | custom-call | tf_op jit(solution)/shard_map/project/pallas_call | solution.py:61
  120.9 1.5 collective-permute-start.24
  123.0 1.3 halve.10.refs_2_
  124.3 4.7 %collective-permute-start.23 = (f32[1,2,128,256]{3,2,1,0:T(8,128)S(1)}, f32[1,2,128,256]{3,2,1,0:T(8,128)S(1)}, u32[]{:S(2)}, u32[]{:S(2)}) collective-permute-start(f32[1,2,128,256]{3,2,1,0:T(8,128)S(1)} %halve.10.refs_2_), channel_id=1, source_target_pairs={{0,2},{1,3},{2,0},{3,1},{4,6},{5,7},{6,4},{7,5},{8,10},{9,11},{10,... | collective-permute-start | bytes 786440 | tf_op jit(solution)/shard_map/ppermute | solution.py:81
  129.0 1.7 scatter.2
  130.7 3.0 %collective-permute-start.21 = (f32[1,1,128,256]{3,2,1,0:T(8,128)S(1)}, f32[1,1,128,256]{3,2,1,0:T(8,128)S(1)}, u32[]{:S(2)}, u32[]{:S(2)}) collective-permute-start(f32[1,1,128,256]{3,2,1,0:T(8,128)S(1)} %get-tuple-element.51), channel_id=1, source_target_pairs={{0,4},{1,5},{2,6},{3,7},{4,0},{5,1},{6,2},{7,3},{8,12},{9,13},{10,... | collective-permute-start | bytes 393224 | tf_op jit(solution)/shard_map/ppermute | solution.py:81
  133.9 2.5 %collective-permute-start.20 = (f32[1,1,128,256]{3,2,1,0:T(8,128)S(1)}, f32[1,1,128,256]{3,2,1,0:T(8,128)S(1)}, u32[]{:S(2)}, u32[]{:S(2)}) collective-permute-start(f32[1,1,128,256]{3,2,1,0:T(8,128)S(1)} %get-tuple-element.50.refs_2_), channel_id=1, source_target_pairs={{0,2},{1,3},{2,0},{3,1},{4,6},{5,7},{6,4},{7,5},{8,10},{9,11},{10,... | collective-permute-start | bytes 393224 | tf_op jit(solution)/shard_map/ppermute | solution.py:81
  136.4 1.7 scatter.3
  138.1 1.1 halve.11.refs_5_
  139.2 1.7 collective-permute-start.27
  141.0 12.5 %collective-permute-done.21.refs_3_ = f32[1,1,128,256]{3,2,1,0:T(8,128)S(1)} collective-permute-done((f32[1,1,128,256]{3,2,1,0:T(8,128)S(1)}, f32[1,1,128,256]{3,2,1,0:T(8,128)S(1)}, u32[]{:S(2)}, u32[]{:S(2)}) %collective-permute-start.21) | collective-permute-done | bytes 131104 | tf_op jit(solution)/shard_map/ppermute | solution.py:81
  153.5 4.8 %collective-permute-start.29 = (f32[1,1,128,256]{3,2,1,0:T(8,128)S(1)}, f32[1,1,128,256]{3,2,1,0:T(8,128)S(1)}, u32[]{:S(2)}, u32[]{:S(2)}) collective-permute-start(f32[1,1,128,256]{3,2,1,0:T(8,128)S(1)} %get-tuple-element.55), channel_id=1, source_target_pairs={{0,4},{1,5},{2,6},{3,7},{4,0},{5,1},{6,2},{7,3},{8,12},{9,13},{10,... | collective-permute-start | bytes 393224 | tf_op jit(solution)/shard_map/ppermute | solution.py:81
  158.3 2.4 %collective-permute-start.30 = (f32[1,1,128,256]{3,2,1,0:T(8,128)S(1)}, f32[1,1,128,256]{3,2,1,0:T(8,128)S(1)}, u32[]{:S(2)}, u32[]{:S(2)}) collective-permute-start(f32[1,1,128,256]{3,2,1,0:T(8,128)S(1)} %get-tuple-element.56), channel_id=1, source_target_pairs={{0,6},{1,7},{2,4},{3,5},{4,2},{5,3},{6,0},{7,1},{8,14},{9,15},{10,... | collective-permute-start | bytes 393224 | tf_op jit(solution)/shard_map/ppermute | solution.py:81
  160.7 1.5 finish.3.refs_15_.refs_2_
  162.2 1.9 %collective-permute-start.16 = (f32[128,256]{1,0:T(8,128)S(1)}, f32[128,256]{1,0:T(8,128)S(1)}, u32[]{:S(2)}, u32[]{:S(2)}) collective-permute-start(f32[128,256]{1,0:T(8,128)S(1)} %slice.31), channel_id=1, source_target_pairs={{2,8},{3,9},{4,16},{5,17},{6,24},{7,25},{8,2},{9,3},{12,18},{13,19... | collective-permute-start | bytes 393224 | tf_op jit(solution)/shard_map/ppermute | solution.py:513
  164.1 4.8 %collective-permute-start.25 = (f32[128,256]{1,0:T(8,128)S(1)}, f32[128,256]{1,0:T(8,128)S(1)}, u32[]{:S(2)}, u32[]{:S(2)}) collective-permute-start(f32[128,256]{1,0:T(8,128)S(1)} %finish.3.refs_15_.refs_2_), channel_id=1, source_target_pairs={{0,1},{1,0},{2,9},{3,8},{4,17},{5,16},{6,25},{7,24},{8,3},{9,2},{1... | collective-permute-start | bytes 393224 | tf_op jit(solution)/shard_map/ppermute | solution.py:530
  169.0 3.2 %assemble.1.refs_4_ = f32[512,256]{1,0:T(8,128)} custom-call(s32[7]{0:T(128)S(1)} %stack.31.at, f32[1,2,256,256]{3,2,1,0:T(8,128)S(1)} %get-tuple-element.39.refs_2_.refs_0_, f32[1,2,256,256]{3,2,1,0:T(8,128)S(1)} %get-tuple-element.40.refs_3_.refs_1_, f32[1,2,256,256]{3,2,1,0:T(8,128)S(1)} %collective-permute-done.10.refs_4_.refs_2_, ...), custom_call_target="tpu_custom_call" | custom-call | tf_op jit(solution)/shard_map/assemble/pallas_call | solution.py:61
  172.2 6.0 %collective-permute-done.16.refs_1_ = f32[128,256]{1,0:T(8,128)S(1)} collective-permute-done((f32[128,256]{1,0:T(8,128)S(1)}, f32[128,256]{1,0:T(8,128)S(1)}, u32[]{:S(2)}, u32[]{:S(2)}) %collective-permute-start.16) | collective-permute-done | bytes 131104 | tf_op jit(solution)/shard_map/ppermute | solution.py:513
  178.2 2.4 %collective-permute-done.25.refs_3_ = f32[128,256]{1,0:T(8,128)S(1)} collective-permute-done((f32[128,256]{1,0:T(8,128)S(1)}, f32[128,256]{1,0:T(8,128)S(1)}, u32[]{:S(2)}, u32[]{:S(2)}) %collective-permute-start.25) | collective-permute-done | bytes 131104 | tf_op jit(solution)/shard_map/ppermute | solution.py:530
  180.6 1.0 copy-done.8
  181.6 1.5 assemble_overlap.1
  (65 shorter events, 7.1 us)
Async XLA Ops:
  0.7 1.6 copy-start.6
  2.3 2.7 %copy-start.9 = (f32[256,2048]{1,0:T(8,128)S(1)}, f32[256,2048]{1,0:T(8,128)}, u32[]{:S(2)}) copy-start(f32[256,2048]{1,0:T(8,128)} %refs_0_.4) | copy-start | bytes 6291460
  3.4 74.7 %copy-start = (f32[256,1024]{1,0:T(8,128)}, f32[256,1024]{1,0:T(8,128)S(1)}, u32[]{:S(2)}) copy-start(f32[256,1024]{1,0:T(8,128)S(1)} %get-tuple-element.30.refs_1_.refs_2_.refs_0_.refs_10_) | copy-start | bytes 3145732
  3.4 26.1 %collective-permute-start.1 = (f32[256,1024]{1,0:T(8,128)S(1)}, f32[256,1024]{1,0:T(8,128)S(1)}, u32[]{:S(2)}, u32[]{:S(2)}) collective-permute-start(f32[256,1024]{1,0:T(8,128)S(1)} %get-tuple-element.31.refs_1_.refs_0_), channel_id=1, source_target_pairs={{0,1},{1,0},{2,3},{3,2},{4,5},{5,4},{6,7},{7,6},{8,9},{9,8},{10,11... | collective-permute-start | bytes 3145736 | tf_op jit(solution)/shard_map/ppermute | solution.py:81
  5.0 25.2 %collective-permute-start = (f32[256,1024]{1,0:T(8,128)S(1)}, f32[256,1024]{1,0:T(8,128)S(1)}, u32[]{:S(2)}, u32[]{:S(2)}) collective-permute-start(f32[256,1024]{1,0:T(8,128)S(1)} %get-tuple-element.30.refs_1_.refs_2_.refs_0_.refs_10_), channel_id=1, source_target_pairs={{0,8},{8,0},{16,24},{24,16},{1,9},{9,1},{17,25},{25,17},{2,10},{10... | collective-permute-start | bytes 3145736 | tf_op jit(solution)/shard_map/ppermute | solution.py:81
  6.1 1.4 copy-start.4
  6.1 45.9 %collective-permute-start.6 = (f32[256,1024]{1,0:T(8,128)S(1)}, f32[256,1024]{1,0:T(8,128)S(1)}, u32[]{:S(2)}, u32[]{:S(2)}) collective-permute-start(f32[256,1024]{1,0:T(8,128)S(1)} %get-tuple-element.37), channel_id=1, source_target_pairs={{0,1},{1,0},{2,3},{3,2},{4,5},{5,4},{6,7},{7,6},{8,9},{9,8},{10,11... | collective-permute-start | bytes 3145736 | tf_op jit(solution)/shard_map/ppermute | solution.py:81
  6.7 1.6 copy-start.7
  7.5 45.2 %collective-permute-start.5 = (f32[256,1536]{1,0:T(8,128)S(1)}, f32[256,1536]{1,0:T(8,128)S(1)}, u32[]{:S(2)}, u32[]{:S(2)}) collective-permute-start(f32[256,1536]{1,0:T(8,128)S(1)} %get-tuple-element.33.refs_2_), channel_id=1, source_target_pairs={{0,8},{8,0},{16,24},{24,16},{1,9},{9,1},{17,25},{25,17},{2,10},{10... | collective-permute-start | bytes 4718600 | tf_op jit(solution)/shard_map/ppermute | solution.py:81
  29.5 9.5 %copy-start.1 = (f32[256,1024]{1,0:T(8,128)}, f32[256,1024]{1,0:T(8,128)S(1)}, u32[]{:S(2)}) copy-start(f32[256,1024]{1,0:T(8,128)S(1)} %collective-permute-done.1.refs_4_.refs_5_.refs_12_) | copy-start | bytes 3145732
  29.6 2.1 %collective-permute-start.3 = (f32[128,1024]{1,0:T(8,128)S(1)}, f32[128,1024]{1,0:T(8,128)S(1)}, u32[]{:S(2)}, u32[]{:S(2)}) collective-permute-start(f32[128,1024]{1,0:T(8,128)S(1)} %get-tuple-element.61), channel_id=1, source_target_pairs={{0,8},{8,0},{16,24},{24,16},{1,9},{9,1},{17,25},{25,17},{2,10},{10... | collective-permute-start | bytes 1572872 | tf_op jit(solution)/shard_map/ppermute | solution.py:81
  29.7 2.6 %collective-permute-start.2 = (f32[128,1024]{1,0:T(8,128)S(1)}, f32[128,1024]{1,0:T(8,128)S(1)}, u32[]{:S(2)}, u32[]{:S(2)}) collective-permute-start(f32[128,1024]{1,0:T(8,128)S(1)} %get-tuple-element.62), channel_id=1, source_target_pairs={{0,8},{8,0},{16,24},{24,16},{1,9},{9,1},{17,25},{25,17},{2,10},{10... | collective-permute-start | bytes 1572872 | tf_op jit(solution)/shard_map/ppermute | solution.py:81
  30.2 8.8 %copy-start.2 = (f32[256,1024]{1,0:T(8,128)}, f32[256,1024]{1,0:T(8,128)S(1)}, u32[]{:S(2)}) copy-start(f32[256,1024]{1,0:T(8,128)S(1)} %collective-permute-done.refs_2_.refs_3_.refs_11_) | copy-start | bytes 3145732
  30.2 52.7 %collective-permute-start.12 = (f32[512,512]{1,0:T(8,128)S(1)}, f32[512,512]{1,0:T(8,128)S(1)}, u32[]{:S(2)}, u32[]{:S(2)}) collective-permute-start(f32[512,512]{1,0:T(8,128)S(1)} %get-tuple-element.42), channel_id=1, source_target_pairs={{0,1},{1,0},{2,3},{3,2},{4,5},{5,4},{6,7},{7,6},{8,9},{9,8},{10,11... | collective-permute-start | bytes 3145736 | tf_op jit(solution)/shard_map/ppermute | solution.py:81
  52.0 17.3 %copy-start.11 = (f32[256,1024]{1,0:T(8,128)}, f32[256,1024]{1,0:T(8,128)S(1)}, u32[]{:S(2)}) copy-start(f32[256,1024]{1,0:T(8,128)S(1)} %collective-permute-done.6.refs_12_) | copy-start | bytes 3145732
  52.0 17.3 %collective-permute-start.4 = (f32[1,4,192,256]{3,2,1,0:T(8,128)S(1)}, f32[1,4,192,256]{3,2,1,0:T(8,128)S(1)}, u32[]{:S(2)}, u32[]{:S(2)}) collective-permute-start(f32[1,4,192,256]{3,2,1,0:T(8,128)S(1)} %get-tuple-element.36), channel_id=1, source_target_pairs={{0,16},{8,24},{16,0},{24,8},{1,17},{9,25},{17,1},{25,9},{2,18},{10... | collective-permute-start | bytes 2359304 | tf_op jit(solution)/shard_map/ppermute | solution.py:81
  52.1 2.0 %collective-permute-start.8 = (f32[128,1024]{1,0:T(8,128)S(1)}, f32[128,1024]{1,0:T(8,128)S(1)}, u32[]{:S(2)}, u32[]{:S(2)}) collective-permute-start(f32[128,1024]{1,0:T(8,128)S(1)} %get-tuple-element.59), channel_id=1, source_target_pairs={{0,8},{8,0},{16,24},{24,16},{1,9},{9,1},{17,25},{25,17},{2,10},{10... | collective-permute-start | bytes 1572872 | tf_op jit(solution)/shard_map/ppermute | solution.py:81
  52.2 2.6 %collective-permute-start.7 = (f32[128,1024]{1,0:T(8,128)S(1)}, f32[128,1024]{1,0:T(8,128)S(1)}, u32[]{:S(2)}, u32[]{:S(2)}) collective-permute-start(f32[128,1024]{1,0:T(8,128)S(1)} %get-tuple-element.60), channel_id=1, source_target_pairs={{0,8},{8,0},{16,24},{24,16},{1,9},{9,1},{17,25},{25,17},{2,10},{10... | collective-permute-start | bytes 1572872 | tf_op jit(solution)/shard_map/ppermute | solution.py:81
  52.7 16.6 %copy-start.10 = (f32[256,1536]{1,0:T(8,128)}, f32[256,1536]{1,0:T(8,128)S(1)}, u32[]{:S(2)}) copy-start(f32[256,1536]{1,0:T(8,128)S(1)} %collective-permute-done.5.refs_11_.refs_2_.refs_3_) | copy-start | bytes 4718596
  74.2 3.9 %copy-start.3 = (f32[256,1024]{1,0:T(8,128)S(1)}, f32[256,1024]{1,0:T(8,128)}, u32[]{:S(2)}) copy-start(f32[256,1024]{1,0:T(8,128)} %copy-done.2) | copy-start | bytes 3145732
  74.2 10.8 %collective-permute-start.10 = (f32[1,2,256,256]{3,2,1,0:T(8,128)S(1)}, f32[1,2,256,256]{3,2,1,0:T(8,128)S(1)}, u32[]{:S(2)}, u32[]{:S(2)}) collective-permute-start(f32[1,2,256,256]{3,2,1,0:T(8,128)S(1)} %get-tuple-element.41), channel_id=1, source_target_pairs={{0,16},{8,24},{16,0},{24,8},{1,17},{9,25},{17,1},{25,9},{2,18},{10... | collective-permute-start | bytes 1572872 | tf_op jit(solution)/shard_map/ppermute | solution.py:81
  76.6 8.5 %collective-permute-start.9 = (f32[1,2,192,256]{3,2,1,0:T(8,128)S(1)}, f32[1,2,192,256]{3,2,1,0:T(8,128)S(1)}, u32[]{:S(2)}, u32[]{:S(2)}) collective-permute-start(f32[1,2,192,256]{3,2,1,0:T(8,128)S(1)} %halve.6.refs_15_), channel_id=1, source_target_pairs={{0,2},{1,3},{2,0},{3,1},{4,6},{5,7},{6,4},{7,5},{8,10},{9,11},{10,... | collective-permute-start | bytes 1179656 | tf_op jit(solution)/shard_map/ppermute | solution.py:81
  82.9 3.5 %copy-start.5 = (f32[256,1024]{1,0:T(8,128)S(1)}, f32[256,1024]{1,0:T(8,128)}, u32[]{:S(2)}) copy-start(f32[256,1024]{1,0:T(8,128)} %copy-done.4) | copy-start | bytes 3145732
  83.0 3.5 %collective-permute-start.14 = (f32[128,512]{1,0:T(8,128)S(1)}, f32[128,512]{1,0:T(8,128)S(1)}, u32[]{:S(2)}, u32[]{:S(2)}) collective-permute-start(f32[128,512]{1,0:T(8,128)S(1)} %get-tuple-element.57), channel_id=1, source_target_pairs={{0,8},{8,0},{16,24},{24,16},{1,9},{9,1},{17,25},{25,17},{2,10},{10... | collective-permute-start | bytes 786440 | tf_op jit(solution)/shard_map/ppermute | solution.py:81
  83.0 3.4 %collective-permute-start.13 = (f32[128,512]{1,0:T(8,128)S(1)}, f32[128,512]{1,0:T(8,128)S(1)}, u32[]{:S(2)}, u32[]{:S(2)}) collective-permute-start(f32[128,512]{1,0:T(8,128)S(1)} %get-tuple-element.58), channel_id=1, source_target_pairs={{0,8},{8,0},{16,24},{24,16},{1,9},{9,1},{17,25},{25,17},{2,10},{10... | collective-permute-start | bytes 786440 | tf_op jit(solution)/shard_map/ppermute | solution.py:81
  83.5 14.8 %collective-permute-start.15 = (f32[1,2,256,256]{3,2,1,0:T(8,128)S(1)}, f32[1,2,256,256]{3,2,1,0:T(8,128)S(1)}, u32[]{:S(2)}, u32[]{:S(2)}) collective-permute-start(f32[1,2,256,256]{3,2,1,0:T(8,128)S(1)} %get-tuple-element.44), channel_id=1, source_target_pairs={{0,16},{8,24},{16,0},{24,8},{1,17},{9,25},{17,1},{25,9},{2,18},{10... | collective-permute-start | bytes 1572872 | tf_op jit(solution)/shard_map/ppermute | solution.py:81
  91.7 23.8 %collective-permute-start.18 = (f32[1,4,128,256]{3,2,1,0:T(8,128)S(1)}, f32[1,4,128,256]{3,2,1,0:T(8,128)S(1)}, u32[]{:S(2)}, u32[]{:S(2)}) collective-permute-start(f32[1,4,128,256]{3,2,1,0:T(8,128)S(1)} %get-tuple-element.48), channel_id=1, source_target_pairs={{0,16},{8,24},{16,0},{24,8},{1,17},{9,25},{17,1},{25,9},{2,18},{10... | collective-permute-start | bytes 1572872 | tf_op jit(solution)/shard_map/ppermute | solution.py:81
  99.3 23.0 %collective-permute-start.19 = (f32[1,2,256,256]{3,2,1,0:T(8,128)S(1)}, f32[1,2,256,256]{3,2,1,0:T(8,128)S(1)}, u32[]{:S(2)}, u32[]{:S(2)}) collective-permute-start(f32[1,2,256,256]{3,2,1,0:T(8,128)S(1)} %halve.8.refs_15_), channel_id=1, source_target_pairs={{0,2},{1,3},{2,0},{3,1},{4,6},{5,7},{6,4},{7,5},{8,10},{9,11},{10,... | collective-permute-start | bytes 1572872 | tf_op jit(solution)/shard_map/ppermute | solution.py:81
  99.9 13.9 %collective-permute-start.11 = (f32[1,1,192,256]{3,2,1,0:T(8,128)S(1)}, f32[1,1,192,256]{3,2,1,0:T(8,128)S(1)}, u32[]{:S(2)}, u32[]{:S(2)}) collective-permute-start(f32[1,1,192,256]{3,2,1,0:T(8,128)S(1)} %halve.7.refs_15_), channel_id=1, source_target_pairs={{0,4},{1,5},{2,6},{3,7},{4,0},{5,1},{6,2},{7,3},{8,12},{9,13},{10,... | collective-permute-start | bytes 589832 | tf_op jit(solution)/shard_map/ppermute | solution.py:81
  109.3 19.7 %collective-permute-start.17 = (f32[1,4,128,256]{3,2,1,0:T(8,128)S(1)}, f32[1,4,128,256]{3,2,1,0:T(8,128)S(1)}, u32[]{:S(2)}, u32[]{:S(2)}) collective-permute-start(f32[1,4,128,256]{3,2,1,0:T(8,128)S(1)} %get-tuple-element.47), channel_id=1, source_target_pairs={{0,16},{8,24},{16,0},{24,8},{1,17},{9,25},{17,1},{25,9},{2,18},{10... | collective-permute-start | bytes 1572872 | tf_op jit(solution)/shard_map/ppermute | solution.py:81
  120.9 13.1 %collective-permute-start.24 = (f32[1,4,128,256]{3,2,1,0:T(8,128)S(1)}, f32[1,4,128,256]{3,2,1,0:T(8,128)S(1)}, u32[]{:S(2)}, u32[]{:S(2)}) collective-permute-start(f32[1,4,128,256]{3,2,1,0:T(8,128)S(1)} %get-tuple-element.53), channel_id=1, source_target_pairs={{0,16},{8,24},{16,0},{24,8},{1,17},{9,25},{17,1},{25,9},{2,18},{10... | collective-permute-start | bytes 1572872 | tf_op jit(solution)/shard_map/ppermute | solution.py:81
  124.3 13.8 %collective-permute-start.23 = (f32[1,2,128,256]{3,2,1,0:T(8,128)S(1)}, f32[1,2,128,256]{3,2,1,0:T(8,128)S(1)}, u32[]{:S(2)}, u32[]{:S(2)}) collective-permute-start(f32[1,2,128,256]{3,2,1,0:T(8,128)S(1)} %halve.10.refs_2_), channel_id=1, source_target_pairs={{0,2},{1,3},{2,0},{3,1},{4,6},{5,7},{6,4},{7,5},{8,10},{9,11},{10,... | collective-permute-start | bytes 786440 | tf_op jit(solution)/shard_map/ppermute | solution.py:81
  129.0 33.2 %collective-permute-start.26 = (f32[1,1,256,256]{3,2,1,0:T(8,128)S(1)}, f32[1,1,256,256]{3,2,1,0:T(8,128)S(1)}, u32[]{:S(2)}, u32[]{:S(2)}) collective-permute-start(f32[1,1,256,256]{3,2,1,0:T(8,128)S(1)} %halve.9.refs_2_), channel_id=1, source_target_pairs={{0,4},{1,5},{2,6},{3,7},{4,0},{5,1},{6,2},{7,3},{8,12},{9,13},{10,... | collective-permute-start | bytes 786440 | tf_op jit(solution)/shard_map/ppermute | solution.py:81
  130.7 22.8 %collective-permute-start.21 = (f32[1,1,128,256]{3,2,1,0:T(8,128)S(1)}, f32[1,1,128,256]{3,2,1,0:T(8,128)S(1)}, u32[]{:S(2)}, u32[]{:S(2)}) collective-permute-start(f32[1,1,128,256]{3,2,1,0:T(8,128)S(1)} %get-tuple-element.51), channel_id=1, source_target_pairs={{0,4},{1,5},{2,6},{3,7},{4,0},{5,1},{6,2},{7,3},{8,12},{9,13},{10,... | collective-permute-start | bytes 393224 | tf_op jit(solution)/shard_map/ppermute | solution.py:81
  133.7 19.8 %collective-permute-start.22 = (f32[1,1,128,256]{3,2,1,0:T(8,128)S(1)}, f32[1,1,128,256]{3,2,1,0:T(8,128)S(1)}, u32[]{:S(2)}, u32[]{:S(2)}) collective-permute-start(f32[1,1,128,256]{3,2,1,0:T(8,128)S(1)} %get-tuple-element.52), channel_id=1, source_target_pairs={{0,6},{1,7},{2,4},{3,5},{4,2},{5,3},{6,0},{7,1},{8,14},{9,15},{10,... | collective-permute-start | bytes 393224 | tf_op jit(solution)/shard_map/ppermute | solution.py:81
  133.9 24.4 %collective-permute-start.20 = (f32[1,1,128,256]{3,2,1,0:T(8,128)S(1)}, f32[1,1,128,256]{3,2,1,0:T(8,128)S(1)}, u32[]{:S(2)}, u32[]{:S(2)}) collective-permute-start(f32[1,1,128,256]{3,2,1,0:T(8,128)S(1)} %get-tuple-element.50.refs_2_), channel_id=1, source_target_pairs={{0,2},{1,3},{2,0},{3,1},{4,6},{5,7},{6,4},{7,5},{8,10},{9,11},{10,... | collective-permute-start | bytes 393224 | tf_op jit(solution)/shard_map/ppermute | solution.py:81
  139.2 24.9 %collective-permute-start.27 = (f32[1,1,128,256]{3,2,1,0:T(8,128)S(1)}, f32[1,1,128,256]{3,2,1,0:T(8,128)S(1)}, u32[]{:S(2)}, u32[]{:S(2)}) collective-permute-start(f32[1,1,128,256]{3,2,1,0:T(8,128)S(1)} %halve.11.refs_5_), channel_id=1, source_target_pairs={{0,4},{1,5},{2,6},{3,7},{4,0},{5,1},{6,2},{7,3},{8,12},{9,13},{10,... | collective-permute-start | bytes 393224 | tf_op jit(solution)/shard_map/ppermute | solution.py:81
  153.5 15.5 %collective-permute-start.28 = (f32[1,1,128,256]{3,2,1,0:T(8,128)S(1)}, f32[1,1,128,256]{3,2,1,0:T(8,128)S(1)}, u32[]{:S(2)}, u32[]{:S(2)}) collective-permute-start(f32[1,1,128,256]{3,2,1,0:T(8,128)S(1)} %get-tuple-element.54.refs_3_), channel_id=1, source_target_pairs={{0,2},{1,3},{2,0},{3,1},{4,6},{5,7},{6,4},{7,5},{8,10},{9,11},{10,... | collective-permute-start | bytes 393224 | tf_op jit(solution)/shard_map/ppermute | solution.py:81
  153.5 15.5 %collective-permute-start.29 = (f32[1,1,128,256]{3,2,1,0:T(8,128)S(1)}, f32[1,1,128,256]{3,2,1,0:T(8,128)S(1)}, u32[]{:S(2)}, u32[]{:S(2)}) collective-permute-start(f32[1,1,128,256]{3,2,1,0:T(8,128)S(1)} %get-tuple-element.55), channel_id=1, source_target_pairs={{0,4},{1,5},{2,6},{3,7},{4,0},{5,1},{6,2},{7,3},{8,12},{9,13},{10,... | collective-permute-start | bytes 393224 | tf_op jit(solution)/shard_map/ppermute | solution.py:81
  158.3 10.7 %collective-permute-start.30 = (f32[1,1,128,256]{3,2,1,0:T(8,128)S(1)}, f32[1,1,128,256]{3,2,1,0:T(8,128)S(1)}, u32[]{:S(2)}, u32[]{:S(2)}) collective-permute-start(f32[1,1,128,256]{3,2,1,0:T(8,128)S(1)} %get-tuple-element.56), channel_id=1, source_target_pairs={{0,6},{1,7},{2,4},{3,5},{4,2},{5,3},{6,0},{7,1},{8,14},{9,15},{10,... | collective-permute-start | bytes 393224 | tf_op jit(solution)/shard_map/ppermute | solution.py:81
  162.2 16.0 %collective-permute-start.16 = (f32[128,256]{1,0:T(8,128)S(1)}, f32[128,256]{1,0:T(8,128)S(1)}, u32[]{:S(2)}, u32[]{:S(2)}) collective-permute-start(f32[128,256]{1,0:T(8,128)S(1)} %slice.31), channel_id=1, source_target_pairs={{2,8},{3,9},{4,16},{5,17},{6,24},{7,25},{8,2},{9,3},{12,18},{13,19... | collective-permute-start | bytes 393224 | tf_op jit(solution)/shard_map/ppermute | solution.py:513
  164.1 16.5 %collective-permute-start.25 = (f32[128,256]{1,0:T(8,128)S(1)}, f32[128,256]{1,0:T(8,128)S(1)}, u32[]{:S(2)}, u32[]{:S(2)}) collective-permute-start(f32[128,256]{1,0:T(8,128)S(1)} %finish.3.refs_15_.refs_2_), channel_id=1, source_target_pairs={{0,1},{1,0},{2,9},{3,8},{4,17},{5,16},{6,25},{7,24},{8,3},{9,2},{1... | collective-permute-start | bytes 393224 | tf_op jit(solution)/shard_map/ppermute | solution.py:530
  180.6 1.0 copy-start.8

commit v3 on v2

--- a/solution.py
+++ b/solution.py
@@ -456,9 +456,9 @@
     across = lambda value: flip(value, "col", 1)
     core = lambda value: flip(value, "row", 1)
 
-    def core_pieces(value):
-        n = value.shape[0] // 2
-        return [core(value[:n]), core(value[n:])]
+    def core_pieces(value, *ends):
+        ends = (*ends, value.shape[0])
+        return [core(value[first:end]) for first, end in zip((0, *ends), ends)]
 
     own, other = part(dev, "part_orbitals", filtered)
     near = across(other)
@@ -475,14 +475,13 @@
             halve(dev, [total], "x", bit)
         return total
 
-    near_core = core_pieces(after(near, rotated))
+    near_core = core_pieces(after(near, rotated), cells // 2)
     columns = [own, own_core, near, *near_core]
     this = lambda xi, at: (0, 2 * xi + at[0])
     rows = Rows(dev, *((array, array.shape[0], this) for array in columns))
     same = reduced_x(half + lower_rows(dev), *overlap(dev, rows, columns, True))
 
-    images = [image, from_core, image_near, *core_pieces(after(image_near, dev.last))]
-    dev.wait(same)
+    images = [image, from_core, image_near, *core_pieces(after(image_near, dev.last), cells * 3 // 8, cells * 11 // 16)]
     even = reduced_x(b, *project(dev, rows, 0, b, images, (0, 2)))
     halve(dev, [same], "z", dev.z_bits[0])
     odd = reduced_x(b, *project(dev, rows, 0, b, images, (1, 2)))
@@ -490,9 +489,8 @@
     proj_own.terms = [(e[0] + o[0], *e[1:]) for e, o in zip(even.terms, odd.terms)]
 
     far_there = after(far, dev.last)[cells:]
-    far_core = core_pieces(far_there)
+    far_core = core_pieces(far_there, cells // 2)
     dev.wait(even)
-    halve(dev, [same], "z", dev.z_bits[1])
     far_rows = Rows(
         dev,
         (other, cells, this),
@@ -500,9 +498,10 @@
         (far, cells, lambda xi, at: (0, xi)),
         *((array, array.shape[0], lambda xi, at: (0, xi)) for array in far_core),
     )
+    mixed = reduced_x(half, *overlap(dev, far_rows, columns, False))
+    halve(dev, [same], "z", dev.z_bits[1])
+    halve(dev, [proj_own], "z", dev.z_bits[0])
     proj_other = [reduced_x(w, *project(dev, far_rows, 0, w, images))]
-    halve(dev, [proj_own], "z", dev.z_bits[0])
-    mixed = reduced_x(half, *overlap(dev, far_rows, columns, False))
     for bit in dev.z_bits[2:]:
         halve(dev, [same], "z", bit)
     same = finish(dev, same, scale)
@@ -511,15 +510,18 @@
         for i in range(R) for j in range(Z) for p in range(2) if i != j
     ]
     same_half = lax.ppermute(same[:half], ("row", "col"), same_pairs)
-    dev.wait(proj_other[0])
+    halve(dev, [mixed], "z", dev.z_bits[0])
     for n in range(1, cuts):
         proj_other.append(reduced_x(w, *project(dev, far_rows, n, w, images)))
+    dev.waits.append(same_half)
     for bit in dev.z_bits[1:]:
         halve(dev, [proj_own], "z", bit)
+    for bit in dev.z_bits[1:]:
+        halve(dev, [mixed], "z", bit)
     halve(dev, [proj_other[0]], "z", dev.z_bits[0])
-    scatter(dev, [mixed])
     for total in proj_other[1:]:
-        scatter(dev, [total])
+        halve(dev, [total], "z", dev.z_bits[0])
+    dev.wait(proj_own)
     for bit in dev.z_bits[1:]:
         halve(dev, [proj_other[0]], "z", bit)
     mixed = finish(dev, mixed, scale)
@@ -528,6 +530,10 @@
         for i in range(R) for j in range(Z) for p in range(2)
     ]
     mixed_half = lax.ppermute(mixed, ("row", "col"), mixed_pairs)
+    for total in proj_other[1:]:
+        for bit in dev.z_bits[1:]:
+            halve(dev, [total], "z", bit)
+    intersection = assemble_overlap(dev, same, same_half, mixed, mixed_half)
 
     def assemble(at, values, inputs, outs):
         first = pl.multiple_of(at[1] * b, b)
@@ -539,7 +545,6 @@
     (projected,) = gather(
         dev, assemble, "assemble", [proj_own, *proj_other], None, [], [(2 * b, b)]
     )
-    intersection = assemble_overlap(dev, same, same_half, mixed, mixed_half)
     return (intersection, projected, rotated)
 
 

time: 184 us -> 164 us (0.89)
  starting transfers between devices: 42.8 us -> 29.1 us
  waiting for transfers between devices: 67 us -> 60.7 us
    ppermute x29 -> x28, starting transfers between devices: 36.1 us -> 20.2 us  [flip(): return lax.ppermute(value, axis, [(i, i ^ mask) for i in range(count)])]
    ppermute x29 -> x28, waiting for transfers between devices: 58.6 us -> 45.9 us  [flip(): return lax.ppermute(value, axis, [(i, i ^ mask) for i in range(count)])]
    ppermute x1, waiting for transfers between devices: 2.36 us -> 8.82 us  [local(): mixed_half = lax.ppermute(mixed, ('row', 'col'), mixed_pairs)]
    ppermute x1, starting transfers between devices: 1.92 us -> 5.47 us  [local(): same_half = lax.ppermute(same[:half], ('row', 'col'), same_pairs)]
    pallas_call x22 -> x24, Pallas kernels: 68.8 us -> 69.7 us  [call(): pl.pallas_call(ordered, name=name, out_shape=[jax.ShapeDtypeStruct(s, jnp...]
  transfers between devices with their start and end apart: 31 -> 30, of which waited for: 11 -> 16; matrix products, arithmetic and copies ran while one was open for 0% -> 0% of each run, Pallas kernels for 36% -> 40%
where the time goes in v3:
time: 164 us; the launch traced here: 163 us
  Pallas kernels  69.7 us (42%)
  waiting for transfers between devices  60.7 us (37%)
  starting transfers between devices  29.1 us (18%)
  local copies, waits for them, and re-layouts  2.12 us (1%)
    pallas_call x24, Pallas kernels, call(): pl.pallas_call(ordered, name=name, out_shape=[jax.ShapeDtypeStruct(s, jnp...  69.7 us
    ppermute x28, waiting for transfers between devices, flip(): return lax.ppermute(value, axis, [(i, i ^ mask) for i in range(count)])  45.9 us
    ppermute x28, starting transfers between devices, flip(): return lax.ppermute(value, axis, [(i, i ^ mask) for i in range(count)])  20.2 us
    ppermute x1, waiting for transfers between devices, local(): mixed_half = lax.ppermute(mixed, ('row', 'col'), mixed_pairs)  8.82 us
    ppermute x1, waiting for transfers between devices, local(): same_half = lax.ppermute(same[:half], ('row', 'col'), same_pairs)  5.92 us
    ppermute x1, starting transfers between devices, local(): same_half = lax.ppermute(same[:half], ('row', 'col'), same_pairs)  5.47 us
    ppermute x1, starting transfers between devices, local(): mixed_half = lax.ppermute(mixed, ('row', 'col'), mixed_pairs)  3.46 us
  transfers between devices with their start and end apart: 30, of which 16 were waited for; matrix products, arithmetic and copies ran while one was open for 0% of the time, Pallas kernels for 40%

profile of v3, /device:TPU:2, one launch (start us, length us, event | category | flops | bytes accessed | tf_op | source)
XLA Modules:
  0.0 162.9 jit_solution(10085072728972915256)
XLA Ops:
  0.7 1.6 copy-done.5
  2.3 1.1 part_orbitals.1
  3.4 1.6 collective-permute-start.1
  5.0 1.1 part_images.1
  6.1 0.8 part_cores.1
  8.1 13.7 %rotate.1.refs_15_ = f32[256,2048]{1,0:T(8,128)} custom-call(s32[7]{0:T(128)S(1)} %stack.31.at, f32[256,2048]{1,0:T(8,128)S(1)} %copy-done.6, f32[2048,2048]{1,0:T(8,128)} %refs_1_.1, f32[256,1536]{1,0:T(8,128)S(1)} %get-tuple-element.27.refs_2_), custom_call_target="tpu_custom_call" | custom-call | tf_op jit(solution)/shard_map/rotate/pallas_call | solution.py:61
  21.8 7.8 %collective-permute-done.1.refs_4_.refs_5_.refs_12_ = f32[256,1024]{1,0:T(8,128)S(1)} collective-permute-done((f32[256,1024]{1,0:T(8,128)S(1)}, f32[256,1024]{1,0:T(8,128)S(1)}, u32[]{:S(2)}, u32[]{:S(2)}) %collective-permute-start.1) | collective-permute-done | bytes 1048608 | tf_op jit(solution)/shard_map/ppermute | solution.py:81
  30.2 1.5 collective-permute-start.11
  31.8 0.6 collective-permute-done.2.refs_6_.refs_7_.refs_13_
  32.4 6.6 %overlap_same.1 = (f32[1,4,192,256]{3,2,1,0:T(8,128)S(1)}, f32[1,4,192,256]{3,2,1,0:T(8,128)S(1)}) custom-call(s32[7]{0:T(128)S(1)} %stack.31.at, f32[256,1024]{1,0:T(8,128)S(1)} %get-tuple-element.24.refs_1_.refs_2_.refs_0_.refs_10_, f32[256,1024]{1,0:T(8,128)S(1)} %get-tuple-element.24.refs_1_.refs_2_.refs_0_.refs_10_, ...), custom_call_target="tpu_custom_call" | custom-call | tf_op jit(solution)/shard_map/overlap_same/pallas_call | solution.py:61
  39.1 12.9 %collective-permute-done.6.refs_12_ = f32[256,1024]{1,0:T(8,128)S(1)} collective-permute-done((f32[256,1024]{1,0:T(8,128)S(1)}, f32[256,1024]{1,0:T(8,128)S(1)}, u32[]{:S(2)}, u32[]{:S(2)}) %collective-permute-start.6) | collective-permute-done | bytes 1048608 | tf_op jit(solution)/shard_map/ppermute | solution.py:81
  52.8 1.5 collective-permute-done.9.refs_15_
  54.8 4.8 %project.4 = (f32[1,2,256,256]{3,2,1,0:T(8,128)S(1)}, f32[1,2,256,256]{3,2,1,0:T(8,128)S(1)}) custom-call(s32[7]{0:T(128)S(1)} %stack.31.at, f32[256,1024]{1,0:T(8,128)S(1)} %get-tuple-element.24.refs_1_.refs_2_.refs_0_.refs_10_, f32[256,1024]{1,0:T(8,128)S(1)} %get-tuple-element.24.refs_1_.refs_2_.refs_0_.refs_10_, ...), custom_call_target="tpu_custom_call" | custom-call | tf_op jit(solution)/shard_map/project/pallas_call | solution.py:61
  59.6 1.6 %halve.10.refs_16_ = f32[1,2,192,256]{3,2,1,0:T(8,128)S(1)} custom-call(s32[7]{0:T(128)S(1)} %stack.31.at, f32[1,4,192,256]{3,2,1,0:T(8,128)S(1)} %get-tuple-element.29.refs_16_.refs_0_, f32[1,4,192,256]{3,2,1,0:T(8,128)S(1)} %collective-permute-done.4.refs_1_, f32[1,2,256,256]{3,2,1,0:T(8,128)S(1)} %get-tuple-element.33.refs_2_.refs_0_), custom_call_target="tpu_custom_call" | custom-call | tf_op jit(solution)/shard_map/halve/pallas_call | solution.py:61
  61.3 4.8 %project.5 = (f32[1,2,256,256]{3,2,1,0:T(8,128)S(1)}, f32[1,2,256,256]{3,2,1,0:T(8,128)S(1)}) custom-call(s32[7]{0:T(128)S(1)} %stack.31.at, f32[256,1024]{1,0:T(8,128)S(1)} %get-tuple-element.24.refs_1_.refs_2_.refs_0_.refs_10_, f32[256,1024]{1,0:T(8,128)S(1)} %get-tuple-element.24.refs_1_.refs_2_.refs_0_.refs_10_, ...), custom_call_target="tpu_custom_call" | custom-call | tf_op jit(solution)/shard_map/project/pallas_call | solution.py:61
  66.1 7.2 %collective-permute-done.11.refs_4_.refs_5_ = f32[512,512]{1,0:T(8,128)S(1)} collective-permute-done((f32[512,512]{1,0:T(8,128)S(1)}, f32[512,512]{1,0:T(8,128)S(1)}, u32[]{:S(2)}, u32[]{:S(2)}) %collective-permute-start.11) | collective-permute-done | bytes 1048608 | tf_op jit(solution)/shard_map/ppermute | solution.py:81
  73.9 1.6 collective-permute-start.10
  76.1 7.0 %overlap_mixed.1 = (f32[1,4,128,256]{3,2,1,0:T(8,128)S(1)}, f32[1,4,128,256]{3,2,1,0:T(8,128)S(1)}) custom-call(s32[7]{0:T(128)S(1)} %stack.31.at, f32[256,1024]{1,0:T(8,128)S(1)} %get-tuple-element.25.refs_1_.refs_0_, f32[256,1024]{1,0:T(8,128)S(1)} %get-tuple-element.25.refs_1_.refs_0_, f32[256,1536]{1,0:T(8,128)} %collective-permute-done.5.refs_11_.refs_2_.refs_3_, ...), custom_call_target="tpu_custom_call" | custom-call | tf_op jit(solution)/shard_map/overlap_mixed/pallas_call | solution.py:61
  83.1 1.5 collective-permute-start.18
  85.0 1.4 halve.11.refs_4_
  86.4 2.7 %collective-permute-start.15 = (f32[1,1,192,256]{3,2,1,0:T(8,128)S(1)}, f32[1,1,192,256]{3,2,1,0:T(8,128)S(1)}, u32[]{:S(2)}, u32[]{:S(2)}) collective-permute-start(f32[1,1,192,256]{3,2,1,0:T(8,128)S(1)} %halve.11.refs_4_), channel_id=1, source_target_pairs={{0,4},{1,5},{2,6},{3,7},{4,0},{5,1},{6,2},{7,3},{8,12},{9,13},{10,... | collective-permute-start | bytes 589832 | tf_op jit(solution)/shard_map/ppermute | solution.py:81
  89.1 1.3 collective-permute-done.16.refs_3_
  90.3 1.0 halve.12.refs_16_
  91.8 5.4 %project.6 = (f32[1,4,128,256]{3,2,1,0:T(8,128)S(1)}, f32[1,4,128,256]{3,2,1,0:T(8,128)S(1)}) custom-call(s32[7]{0:T(128)S(1)} %stack.31.at, f32[256,1024]{1,0:T(8,128)S(1)} %get-tuple-element.25.refs_1_.refs_0_, f32[256,1024]{1,0:T(8,128)S(1)} %get-tuple-element.25.refs_1_.refs_0_, f32[256,1536]{1,0:T(8,128)} %collective-permute-done.5.refs_11_.refs_2_.refs_3_, ...), custom_call_target="tpu_custom_call" | custom-call | tf_op jit(solution)/shard_map/project/pallas_call | solution.py:61
  97.8 1.6 %finish.2.refs_2_.refs_0_ = f32[192,256]{1,0:T(8,128)S(1)} custom-call(s32[7]{0:T(128)S(1)} %stack.31.at, f32[1,4,192,256]{3,2,1,0:T(8,128)S(1)} %get-tuple-element.29.refs_16_.refs_0_, f32[1,4,192,256]{3,2,1,0:T(8,128)S(1)} %collective-permute-done.4.refs_1_, f32[1,2,192,256]{3,2,1,0:T(8,128)S(1)} %collective-permute-done.10.refs_2_, ...), custom_call_target="tpu_custom_call" | custom-call | tf_op jit(solution)/shard_map/finish/pallas_call | solution.py:61
  99.4 2.2 %collective-permute-done.18.refs_1_ = f32[1,4,128,256]{3,2,1,0:T(8,128)S(1)} collective-permute-done((f32[1,4,128,256]{3,2,1,0:T(8,128)S(1)}, f32[1,4,128,256]{3,2,1,0:T(8,128)S(1)}, u32[]{:S(2)}, u32[]{:S(2)}) %collective-permute-start.18) | collective-permute-done | bytes 524320 | tf_op jit(solution)/shard_map/ppermute | solution.py:81
  101.6 1.3 halve.13.refs_16_
  102.9 5.2 %project.7 = (f32[1,4,128,256]{3,2,1,0:T(8,128)S(1)}, f32[1,4,128,256]{3,2,1,0:T(8,128)S(1)}) custom-call(s32[7]{0:T(128)S(1)} %stack.31.at, f32[256,1024]{1,0:T(8,128)S(1)} %get-tuple-element.25.refs_1_.refs_0_, f32[256,1024]{1,0:T(8,128)S(1)} %get-tuple-element.25.refs_1_.refs_0_, f32[256,1536]{1,0:T(8,128)} %collective-permute-done.5.refs_11_.refs_2_.refs_3_, ...), custom_call_target="tpu_custom_call" | custom-call | tf_op jit(solution)/shard_map/project/pallas_call | solution.py:61
  109.2 5.5 %collective-permute-start.17 = (f32[128,256]{1,0:T(8,128)S(1)}, f32[128,256]{1,0:T(8,128)S(1)}, u32[]{:S(2)}, u32[]{:S(2)}) collective-permute-start(f32[128,256]{1,0:T(8,128)S(1)} %slice.35), channel_id=1, source_target_pairs={{2,8},{3,9},{4,16},{5,17},{6,24},{7,25},{8,2},{9,3},{12,18},{13,19... | collective-permute-start | bytes 393224 | tf_op jit(solution)/shard_map/ppermute | solution.py:512
  114.6 5.9 %collective-permute-done.17.refs_6_.refs_1_ = f32[128,256]{1,0:T(8,128)S(1)} collective-permute-done((f32[128,256]{1,0:T(8,128)S(1)}, f32[128,256]{1,0:T(8,128)S(1)}, u32[]{:S(2)}, u32[]{:S(2)}) %collective-permute-start.17) | collective-permute-done | bytes 131104 | tf_op jit(solution)/shard_map/ppermute | solution.py:512
  120.6 0.7 halve.14.refs_3_
  121.4 1.1 halve.15.refs_2_
  122.5 1.3 halve.16.refs_2_
  123.8 1.2 collective-permute-start.23
  125.0 0.6 collective-permute-done.24.refs_1_.refs_11_
  125.7 1.3 halve.17.refs_3_
  127.5 2.7 %collective-permute-start.21 = (f32[1,1,128,256]{3,2,1,0:T(8,128)S(1)}, f32[1,1,128,256]{3,2,1,0:T(8,128)S(1)}, u32[]{:S(2)}, u32[]{:S(2)}) collective-permute-start(f32[1,1,128,256]{3,2,1,0:T(8,128)S(1)} %halve.15.refs_2_), channel_id=1, source_target_pairs={{0,4},{1,5},{2,6},{3,7},{4,0},{5,1},{6,2},{7,3},{8,12},{9,13},{10,... | collective-permute-start | bytes 393224 | tf_op jit(solution)/shard_map/ppermute | solution.py:81
  130.2 4.0 %collective-permute-done.25.refs_4_.refs_5_ = f32[1,1,256,256]{3,2,1,0:T(8,128)S(1)} collective-permute-done((f32[1,1,256,256]{3,2,1,0:T(8,128)S(1)}, f32[1,1,256,256]{3,2,1,0:T(8,128)S(1)}, u32[]{:S(2)}, u32[]{:S(2)}) %collective-permute-start.25) | collective-permute-done | bytes 262176 | tf_op jit(solution)/shard_map/ppermute | solution.py:81
  134.2 6.1 %collective-permute-done.23.refs_2_.refs_8_ = f32[1,2,128,256]{3,2,1,0:T(8,128)S(1)} collective-permute-done((f32[1,2,128,256]{3,2,1,0:T(8,128)S(1)}, f32[1,2,128,256]{3,2,1,0:T(8,128)S(1)}, u32[]{:S(2)}, u32[]{:S(2)}) %collective-permute-start.23) | collective-permute-done | bytes 262176 | tf_op jit(solution)/shard_map/ppermute | solution.py:81
  140.3 1.1 halve.18.refs_4_
  141.5 0.7 collective-permute-done.21.refs_3_
  142.2 1.3 finish.3.refs_3_.refs_2_
  143.5 3.5 %collective-permute-start.26 = (f32[128,256]{1,0:T(8,128)S(1)}, f32[128,256]{1,0:T(8,128)S(1)}, u32[]{:S(2)}, u32[]{:S(2)}) collective-permute-start(f32[128,256]{1,0:T(8,128)S(1)} %finish.3.refs_3_.refs_2_), channel_id=1, source_target_pairs={{0,1},{1,0},{2,9},{3,8},{4,17},{5,16},{6,25},{7,24},{8,3},{9,2},{1... | collective-permute-start | bytes 393224 | tf_op jit(solution)/shard_map/ppermute | solution.py:532
  147.0 1.1 halve.19.refs_4_
  148.1 1.2 collective-permute-start.29
  149.3 8.8 %collective-permute-done.26.refs_3_ = f32[128,256]{1,0:T(8,128)S(1)} collective-permute-done((f32[128,256]{1,0:T(8,128)S(1)}, f32[128,256]{1,0:T(8,128)S(1)}, u32[]{:S(2)}, u32[]{:S(2)}) %collective-permute-start.26) | collective-permute-done | bytes 131104 | tf_op jit(solution)/shard_map/ppermute | solution.py:532
  158.1 1.5 assemble_overlap.1.refs_14_
  159.6 3.1 %assemble.1 = f32[512,256]{1,0:T(8,128)} custom-call(s32[7]{0:T(128)S(1)} %stack.31.at, f32[1,2,256,256]{3,2,1,0:T(8,128)S(1)} %get-tuple-element.33.refs_2_.refs_0_, f32[1,2,256,256]{3,2,1,0:T(8,128)S(1)} %get-tuple-element.35.refs_15_.refs_1_, f32[1,2,256,256]{3,2,1,0:T(8,128)S(1)} %collective-permute-done.14.refs_16_.refs_2_, ...), custom_call_target="tpu_custom_call" | custom-call | tf_op jit(solution)/shard_map/assemble/pallas_call | solution.py:61
  (60 shorter events, 7.8 us)
Async XLA Ops:
  0.7 1.6 copy-start.5
  2.3 2.7 %copy-start.7 = (f32[256,2048]{1,0:T(8,128)S(1)}, f32[256,2048]{1,0:T(8,128)}, u32[]{:S(2)}) copy-start(f32[256,2048]{1,0:T(8,128)} %refs_0_.4) | copy-start | bytes 6291460
  3.4 57.9 %copy-start = (f32[256,1024]{1,0:T(8,128)}, f32[256,1024]{1,0:T(8,128)S(1)}, u32[]{:S(2)}) copy-start(f32[256,1024]{1,0:T(8,128)S(1)} %get-tuple-element.24.refs_1_.refs_2_.refs_0_.refs_10_) | copy-start | bytes 3145732
  3.4 26.1 %collective-permute-start.1 = (f32[256,1024]{1,0:T(8,128)S(1)}, f32[256,1024]{1,0:T(8,128)S(1)}, u32[]{:S(2)}, u32[]{:S(2)}) collective-permute-start(f32[256,1024]{1,0:T(8,128)S(1)} %get-tuple-element.25.refs_1_.refs_0_), channel_id=1, source_target_pairs={{0,1},{1,0},{2,3},{3,2},{4,5},{5,4},{6,7},{7,6},{8,9},{9,8},{10,11... | collective-permute-start | bytes 3145736 | tf_op jit(solution)/shard_map/ppermute | solution.py:81
  5.0 25.2 %collective-permute-start = (f32[256,1024]{1,0:T(8,128)S(1)}, f32[256,1024]{1,0:T(8,128)S(1)}, u32[]{:S(2)}, u32[]{:S(2)}) collective-permute-start(f32[256,1024]{1,0:T(8,128)S(1)} %get-tuple-element.24.refs_1_.refs_2_.refs_0_.refs_10_), channel_id=1, source_target_pairs={{0,8},{8,0},{16,24},{24,16},{1,9},{9,1},{17,25},{25,17},{2,10},{10... | collective-permute-start | bytes 3145736 | tf_op jit(solution)/shard_map/ppermute | solution.py:81
  6.1 1.0 copy-start.3
  6.1 2.0 %copy-start.6 = (f32[256,2048]{1,0:T(8,128)S(1)}, f32[256,2048]{1,0:T(8,128)}, u32[]{:S(2)}) copy-start(f32[256,2048]{1,0:T(8,128)} %refs_0_.5) | copy-start | bytes 6291460
  7.1 45.7 %collective-permute-start.5 = (f32[256,1536]{1,0:T(8,128)S(1)}, f32[256,1536]{1,0:T(8,128)}, u32[]{:S(2)}, u32[]{:S(2)}) collective-permute-start(f32[256,1536]{1,0:T(8,128)S(1)} %get-tuple-element.27.refs_2_), channel_id=1, source_target_pairs={{0,8},{8,0},{16,24},{24,16},{1,9},{9,1},{17,25},{25,17},{2,10},{10... | collective-permute-start | bytes 4718600 | tf_op jit(solution)/shard_map/ppermute | solution.py:81
  7.6 44.4 %collective-permute-start.6 = (f32[256,1024]{1,0:T(8,128)S(1)}, f32[256,1024]{1,0:T(8,128)S(1)}, u32[]{:S(2)}, u32[]{:S(2)}) collective-permute-start(f32[256,1024]{1,0:T(8,128)S(1)} %get-tuple-element.31), channel_id=1, source_target_pairs={{0,1},{1,0},{2,3},{3,2},{4,5},{5,4},{6,7},{7,6},{8,9},{9,8},{10,11... | collective-permute-start | bytes 3145736 | tf_op jit(solution)/shard_map/ppermute | solution.py:81
  29.5 9.5 %copy-start.1 = (f32[256,1024]{1,0:T(8,128)}, f32[256,1024]{1,0:T(8,128)S(1)}, u32[]{:S(2)}) copy-start(f32[256,1024]{1,0:T(8,128)S(1)} %collective-permute-done.1.refs_4_.refs_5_.refs_12_) | copy-start | bytes 3145732
  29.6 2.1 %collective-permute-start.3 = (f32[128,1024]{1,0:T(8,128)S(1)}, f32[128,1024]{1,0:T(8,128)S(1)}, u32[]{:S(2)}, u32[]{:S(2)}) collective-permute-start(f32[128,1024]{1,0:T(8,128)S(1)} %get-tuple-element.49), channel_id=1, source_target_pairs={{0,8},{8,0},{16,24},{24,16},{1,9},{9,1},{17,25},{25,17},{2,10},{10... | collective-permute-start | bytes 1572872 | tf_op jit(solution)/shard_map/ppermute | solution.py:81
  29.7 2.6 %collective-permute-start.2 = (f32[128,1024]{1,0:T(8,128)S(1)}, f32[128,1024]{1,0:T(8,128)S(1)}, u32[]{:S(2)}, u32[]{:S(2)}) collective-permute-start(f32[128,1024]{1,0:T(8,128)S(1)} %get-tuple-element.50), channel_id=1, source_target_pairs={{0,8},{8,0},{16,24},{24,16},{1,9},{9,1},{17,25},{25,17},{2,10},{10... | collective-permute-start | bytes 1572872 | tf_op jit(solution)/shard_map/ppermute | solution.py:81
  30.2 31.1 %copy-start.2 = (f32[256,1024]{1,0:T(8,128)}, f32[256,1024]{1,0:T(8,128)S(1)}, u32[]{:S(2)}) copy-start(f32[256,1024]{1,0:T(8,128)S(1)} %collective-permute-done.refs_2_.refs_3_.refs_11_) | copy-start | bytes 3145732
  30.2 43.1 %collective-permute-start.11 = (f32[512,512]{1,0:T(8,128)S(1)}, f32[512,512]{1,0:T(8,128)S(1)}, u32[]{:S(2)}, u32[]{:S(2)}) collective-permute-start(f32[512,512]{1,0:T(8,128)S(1)} %get-tuple-element.34), channel_id=1, source_target_pairs={{0,1},{1,0},{2,3},{3,2},{4,5},{5,4},{6,7},{7,6},{8,9},{9,8},{10,11... | collective-permute-start | bytes 3145736 | tf_op jit(solution)/shard_map/ppermute | solution.py:81
  39.0 20.6 %collective-permute-start.4 = (f32[1,4,192,256]{3,2,1,0:T(8,128)S(1)}, f32[1,4,192,256]{3,2,1,0:T(8,128)S(1)}, u32[]{:S(2)}, u32[]{:S(2)}) collective-permute-start(f32[1,4,192,256]{3,2,1,0:T(8,128)S(1)} %get-tuple-element.30), channel_id=1, source_target_pairs={{0,16},{8,24},{16,0},{24,8},{1,17},{9,25},{17,1},{25,9},{2,18},{10... | collective-permute-start | bytes 2359304 | tf_op jit(solution)/shard_map/ppermute | solution.py:81
  52.0 2.8 %copy-start.8 = (f32[256,1024]{1,0:T(8,128)}, f32[256,1024]{1,0:T(8,128)S(1)}, u32[]{:S(2)}) copy-start(f32[256,1024]{1,0:T(8,128)S(1)} %collective-permute-done.6.refs_12_) | copy-start | bytes 3145732
  52.0 2.7 %collective-permute-start.7 = (f32[96,1024]{1,0:T(8,128)S(1)}, f32[96,1024]{1,0:T(8,128)S(1)}, u32[]{:S(2)}, u32[]{:S(2)}) collective-permute-start(f32[96,1024]{1,0:T(8,128)S(1)} %slice.29), channel_id=1, source_target_pairs={{0,8},{8,0},{16,24},{24,16},{1,9},{9,1},{17,25},{25,17},{2,10},{10... | collective-permute-start | bytes 1179656 | tf_op jit(solution)/shard_map/ppermute | solution.py:81
  52.2 2.1 %collective-permute-start.9 = (f32[80,1024]{1,0:T(8,128)S(1)}, f32[80,1024]{1,0:T(8,128)S(1)}, u32[]{:S(2)}, u32[]{:S(2)}) collective-permute-start(f32[80,1024]{1,0:T(8,128)S(1)} %get-tuple-element.47), channel_id=1, source_target_pairs={{0,8},{8,0},{16,24},{24,16},{1,9},{9,1},{17,25},{25,17},{2,10},{10... | collective-permute-start | bytes 983048 | tf_op jit(solution)/shard_map/ppermute | solution.py:81
  52.7 2.0 %collective-permute-start.8 = (f32[80,1024]{1,0:T(8,128)S(1)}, f32[80,1024]{1,0:T(8,128)S(1)}, u32[]{:S(2)}, u32[]{:S(2)}) collective-permute-start(f32[80,1024]{1,0:T(8,128)S(1)} %get-tuple-element.48), channel_id=1, source_target_pairs={{0,8},{8,0},{16,24},{24,16},{1,9},{9,1},{17,25},{25,17},{2,10},{10... | collective-permute-start | bytes 983048 | tf_op jit(solution)/shard_map/ppermute | solution.py:81
  59.5 16.5 %collective-permute-start.14 = (f32[1,2,256,256]{3,2,1,0:T(8,128)S(1)}, f32[1,2,256,256]{3,2,1,0:T(8,128)S(1)}, u32[]{:S(2)}, u32[]{:S(2)}) collective-permute-start(f32[1,2,256,256]{3,2,1,0:T(8,128)S(1)} %get-tuple-element.37), channel_id=1, source_target_pairs={{0,16},{8,24},{16,0},{24,8},{1,17},{9,25},{17,1},{25,9},{2,18},{10... | collective-permute-start | bytes 1572872 | tf_op jit(solution)/shard_map/ppermute | solution.py:81
  73.4 2.7 %collective-permute-start.13 = (f32[128,512]{1,0:T(8,128)S(1)}, f32[128,512]{1,0:T(8,128)S(1)}, u32[]{:S(2)}, u32[]{:S(2)}) collective-permute-start(f32[128,512]{1,0:T(8,128)S(1)} %get-tuple-element.45), channel_id=1, source_target_pairs={{0,8},{8,0},{16,24},{24,16},{1,9},{9,1},{17,25},{25,17},{2,10},{10... | collective-permute-start | bytes 786440 | tf_op jit(solution)/shard_map/ppermute | solution.py:81
  73.4 2.6 %collective-permute-start.12 = (f32[128,512]{1,0:T(8,128)S(1)}, f32[128,512]{1,0:T(8,128)S(1)}, u32[]{:S(2)}, u32[]{:S(2)}) collective-permute-start(f32[128,512]{1,0:T(8,128)S(1)} %get-tuple-element.46), channel_id=1, source_target_pairs={{0,8},{8,0},{16,24},{24,16},{1,9},{9,1},{17,25},{25,17},{2,10},{10... | collective-permute-start | bytes 786440 | tf_op jit(solution)/shard_map/ppermute | solution.py:81
  73.9 11.1 %collective-permute-start.10 = (f32[1,2,192,256]{3,2,1,0:T(8,128)S(1)}, f32[1,2,192,256]{3,2,1,0:T(8,128)S(1)}, u32[]{:S(2)}, u32[]{:S(2)}) collective-permute-start(f32[1,2,192,256]{3,2,1,0:T(8,128)S(1)} %halve.10.refs_16_), channel_id=1, source_target_pairs={{0,2},{1,3},{2,0},{3,1},{4,6},{5,7},{6,4},{7,5},{8,10},{9,11},{10,... | collective-permute-start | bytes 1179656 | tf_op jit(solution)/shard_map/ppermute | solution.py:81
  75.5 14.8 %collective-permute-start.16 = (f32[1,2,256,256]{3,2,1,0:T(8,128)S(1)}, f32[1,2,256,256]{3,2,1,0:T(8,128)S(1)}, u32[]{:S(2)}, u32[]{:S(2)}) collective-permute-start(f32[1,2,256,256]{3,2,1,0:T(8,128)S(1)} %get-tuple-element.39), channel_id=1, source_target_pairs={{0,16},{8,24},{16,0},{24,8},{1,17},{9,25},{17,1},{25,9},{2,18},{10... | collective-permute-start | bytes 1572872 | tf_op jit(solution)/shard_map/ppermute | solution.py:81
  83.1 18.5 %collective-permute-start.18 = (f32[1,4,128,256]{3,2,1,0:T(8,128)S(1)}, f32[1,4,128,256]{3,2,1,0:T(8,128)S(1)}, u32[]{:S(2)}, u32[]{:S(2)}) collective-permute-start(f32[1,4,128,256]{3,2,1,0:T(8,128)S(1)} %get-tuple-element.41), channel_id=1, source_target_pairs={{0,16},{8,24},{16,0},{24,8},{1,17},{9,25},{17,1},{25,9},{2,18},{10... | collective-permute-start | bytes 1572872 | tf_op jit(solution)/shard_map/ppermute | solution.py:81
  86.4 11.3 %collective-permute-start.15 = (f32[1,1,192,256]{3,2,1,0:T(8,128)S(1)}, f32[1,1,192,256]{3,2,1,0:T(8,128)S(1)}, u32[]{:S(2)}, u32[]{:S(2)}) collective-permute-start(f32[1,1,192,256]{3,2,1,0:T(8,128)S(1)} %halve.11.refs_4_), channel_id=1, source_target_pairs={{0,4},{1,5},{2,6},{3,7},{4,0},{5,1},{6,2},{7,3},{8,12},{9,13},{10,... | collective-permute-start | bytes 589832 | tf_op jit(solution)/shard_map/ppermute | solution.py:81
  91.3 29.3 %collective-permute-start.20 = (f32[1,2,256,256]{3,2,1,0:T(8,128)S(1)}, f32[1,2,256,256]{3,2,1,0:T(8,128)S(1)}, u32[]{:S(2)}, u32[]{:S(2)}) collective-permute-start(f32[1,2,256,256]{3,2,1,0:T(8,128)S(1)} %halve.12.refs_16_), channel_id=1, source_target_pairs={{0,2},{1,3},{2,0},{3,1},{4,6},{5,7},{6,4},{7,5},{8,10},{9,11},{10,... | collective-permute-start | bytes 1572872 | tf_op jit(solution)/shard_map/ppermute | solution.py:81
  97.2 25.3 %collective-permute-start.22 = (f32[1,4,128,256]{3,2,1,0:T(8,128)S(1)}, f32[1,4,128,256]{3,2,1,0:T(8,128)S(1)}, u32[]{:S(2)}, u32[]{:S(2)}) collective-permute-start(f32[1,4,128,256]{3,2,1,0:T(8,128)S(1)} %get-tuple-element.43), channel_id=1, source_target_pairs={{0,16},{8,24},{16,0},{24,8},{1,17},{9,25},{17,1},{25,9},{2,18},{10... | collective-permute-start | bytes 1572872 | tf_op jit(solution)/shard_map/ppermute | solution.py:81
  97.8 5.1 %copy-start.4 = (f32[256,1024]{1,0:T(8,128)S(1)}, f32[256,1024]{1,0:T(8,128)}, u32[]{:S(2)}) copy-start(f32[256,1024]{1,0:T(8,128)} %copy-done.3) | copy-start | bytes 3145732
  108.1 17.5 %collective-permute-start.24 = (f32[1,4,128,256]{3,2,1,0:T(8,128)S(1)}, f32[1,4,128,256]{3,2,1,0:T(8,128)S(1)}, u32[]{:S(2)}, u32[]{:S(2)}) collective-permute-start(f32[1,4,128,256]{3,2,1,0:T(8,128)S(1)} %get-tuple-element.44), channel_id=1, source_target_pairs={{0,16},{8,24},{16,0},{24,8},{1,17},{9,25},{17,1},{25,9},{2,18},{10... | collective-permute-start | bytes 1572872 | tf_op jit(solution)/shard_map/ppermute | solution.py:81
  108.7 12.6 %collective-permute-start.19 = (f32[1,2,128,256]{3,2,1,0:T(8,128)S(1)}, f32[1,2,128,256]{3,2,1,0:T(8,128)S(1)}, u32[]{:S(2)}, u32[]{:S(2)}) collective-permute-start(f32[1,2,128,256]{3,2,1,0:T(8,128)S(1)} %halve.13.refs_16_), channel_id=1, source_target_pairs={{0,2},{1,3},{2,0},{3,1},{4,6},{5,7},{6,4},{7,5},{8,10},{9,11},{10,... | collective-permute-start | bytes 786440 | tf_op jit(solution)/shard_map/ppermute | solution.py:81
  109.2 11.4 %collective-permute-start.17 = (f32[128,256]{1,0:T(8,128)S(1)}, f32[128,256]{1,0:T(8,128)S(1)}, u32[]{:S(2)}, u32[]{:S(2)}) collective-permute-start(f32[128,256]{1,0:T(8,128)S(1)} %slice.35), channel_id=1, source_target_pairs={{2,8},{3,9},{4,16},{5,17},{6,24},{7,25},{8,2},{9,3},{12,18},{13,19... | collective-permute-start | bytes 393224 | tf_op jit(solution)/shard_map/ppermute | solution.py:512
  121.3 12.9 %collective-permute-start.25 = (f32[1,1,256,256]{3,2,1,0:T(8,128)S(1)}, f32[1,1,256,256]{3,2,1,0:T(8,128)S(1)}, u32[]{:S(2)}, u32[]{:S(2)}) collective-permute-start(f32[1,1,256,256]{3,2,1,0:T(8,128)S(1)} %halve.14.refs_3_), channel_id=1, source_target_pairs={{0,4},{1,5},{2,6},{3,7},{4,0},{5,1},{6,2},{7,3},{8,12},{9,13},{10,... | collective-permute-start | bytes 786440 | tf_op jit(solution)/shard_map/ppermute | solution.py:81
  123.8 16.5 %collective-permute-start.23 = (f32[1,2,128,256]{3,2,1,0:T(8,128)S(1)}, f32[1,2,128,256]{3,2,1,0:T(8,128)S(1)}, u32[]{:S(2)}, u32[]{:S(2)}) collective-permute-start(f32[1,2,128,256]{3,2,1,0:T(8,128)S(1)} %halve.16.refs_2_), channel_id=1, source_target_pairs={{0,2},{1,3},{2,0},{3,1},{4,6},{5,7},{6,4},{7,5},{8,10},{9,11},{10,... | collective-permute-start | bytes 786440 | tf_op jit(solution)/shard_map/ppermute | solution.py:81
  127.0 20.0 %collective-permute-start.27 = (f32[1,2,128,256]{3,2,1,0:T(8,128)S(1)}, f32[1,2,128,256]{3,2,1,0:T(8,128)S(1)}, u32[]{:S(2)}, u32[]{:S(2)}) collective-permute-start(f32[1,2,128,256]{3,2,1,0:T(8,128)S(1)} %halve.17.refs_3_), channel_id=1, source_target_pairs={{0,2},{1,3},{2,0},{3,1},{4,6},{5,7},{6,4},{7,5},{8,10},{9,11},{10,... | collective-permute-start | bytes 786440 | tf_op jit(solution)/shard_map/ppermute | solution.py:81
  127.5 14.7 %collective-permute-start.21 = (f32[1,1,128,256]{3,2,1,0:T(8,128)S(1)}, f32[1,1,128,256]{3,2,1,0:T(8,128)S(1)}, u32[]{:S(2)}, u32[]{:S(2)}) collective-permute-start(f32[1,1,128,256]{3,2,1,0:T(8,128)S(1)} %halve.15.refs_2_), channel_id=1, source_target_pairs={{0,4},{1,5},{2,6},{3,7},{4,0},{5,1},{6,2},{7,3},{8,12},{9,13},{10,... | collective-permute-start | bytes 393224 | tf_op jit(solution)/shard_map/ppermute | solution.py:81
  141.4 18.2 %collective-permute-start.28 = (f32[1,1,128,256]{3,2,1,0:T(8,128)S(1)}, f32[1,1,128,256]{3,2,1,0:T(8,128)S(1)}, u32[]{:S(2)}, u32[]{:S(2)}) collective-permute-start(f32[1,1,128,256]{3,2,1,0:T(8,128)S(1)} %halve.18.refs_4_), channel_id=1, source_target_pairs={{0,4},{1,5},{2,6},{3,7},{4,0},{5,1},{6,2},{7,3},{8,12},{9,13},{10,... | collective-permute-start | bytes 393224 | tf_op jit(solution)/shard_map/ppermute | solution.py:81
  143.5 14.6 %collective-permute-start.26 = (f32[128,256]{1,0:T(8,128)S(1)}, f32[128,256]{1,0:T(8,128)S(1)}, u32[]{:S(2)}, u32[]{:S(2)}) collective-permute-start(f32[128,256]{1,0:T(8,128)S(1)} %finish.3.refs_3_.refs_2_), channel_id=1, source_target_pairs={{0,1},{1,0},{2,9},{3,8},{4,17},{5,16},{6,25},{7,24},{8,3},{9,2},{1... | collective-permute-start | bytes 393224 | tf_op jit(solution)/shard_map/ppermute | solution.py:532
  148.1 11.6 %collective-permute-start.29 = (f32[1,1,128,256]{3,2,1,0:T(8,128)S(1)}, f32[1,1,128,256]{3,2,1,0:T(8,128)S(1)}, u32[]{:S(2)}, u32[]{:S(2)}) collective-permute-start(f32[1,1,128,256]{3,2,1,0:T(8,128)S(1)} %halve.19.refs_4_), channel_id=1, source_target_pairs={{0,4},{1,5},{2,6},{3,7},{4,0},{5,1},{6,2},{7,3},{8,12},{9,13},{10,... | collective-permute-start | bytes 393224 | tf_op jit(solution)/shard_map/ppermute | solution.py:81

commit v4 on v3

--- a/solution.py
+++ b/solution.py
@@ -510,15 +510,15 @@
         for i in range(R) for j in range(Z) for p in range(2) if i != j
     ]
     same_half = lax.ppermute(same[:half], ("row", "col"), same_pairs)
-    halve(dev, [mixed], "z", dev.z_bits[0])
     for n in range(1, cuts):
         proj_other.append(reduced_x(w, *project(dev, far_rows, n, w, images)))
-    dev.waits.append(same_half)
+    halve(dev, [mixed], "z", dev.z_bits[0])
     for bit in dev.z_bits[1:]:
         halve(dev, [proj_own], "z", bit)
     for bit in dev.z_bits[1:]:
         halve(dev, [mixed], "z", bit)
     halve(dev, [proj_other[0]], "z", dev.z_bits[0])
+    dev.waits.append(same_half)
     for total in proj_other[1:]:
         halve(dev, [total], "z", dev.z_bits[0])
     dev.wait(proj_own)

time: 164 us -> 160 us (0.976)
  waiting for transfers between devices: 60.7 us -> 52.5 us
  starting transfers between devices: 29.1 us -> 33.5 us
    ppermute x28, waiting for transfers between devices: 45.9 us -> 35.1 us  [flip(): return lax.ppermute(value, axis, [(i, i ^ mask) for i in range(count)])]
    ppermute x28, starting transfers between devices: 20.2 us -> 28.9 us  [flip(): return lax.ppermute(value, axis, [(i, i ^ mask) for i in range(count)])]
    ppermute x1, starting transfers between devices: 3.46 us -> 0.08 us  [local(): mixed_half = lax.ppermute(mixed, ('row', 'col'), mixed_pairs)]
    ppermute x1, waiting for transfers between devices: 5.92 us -> 7.59 us  [local(): same_half = lax.ppermute(same[:half], ('row', 'col'), same_pairs)]
  transfers between devices with their start and end apart: 30 -> 30, of which waited for: 16 -> 13; matrix products, arithmetic and copies ran while one was open for 0% -> 0% of each run, Pallas kernels for 40% -> 41%
where the time goes in v4:
time: 160 us; the launch traced here: 159 us
  Pallas kernels  69.7 us (44%)
  waiting for transfers between devices  52.5 us (33%)
  starting transfers between devices  33.5 us (21%)
  local copies, waits for them, and re-layouts  2.11 us (1%)
    pallas_call x24, Pallas kernels, call(): pl.pallas_call(ordered, name=name, out_shape=[jax.ShapeDtypeStruct(s, jnp...  69.7 us
    ppermute x28, waiting for transfers between devices, flip(): return lax.ppermute(value, axis, [(i, i ^ mask) for i in range(count)])  35.1 us
    ppermute x28, starting transfers between devices, flip(): return lax.ppermute(value, axis, [(i, i ^ mask) for i in range(count)])  28.9 us
    ppermute x1, waiting for transfers between devices, local(): mixed_half = lax.ppermute(mixed, ('row', 'col'), mixed_pairs)  9.77 us
    ppermute x1, waiting for transfers between devices, local(): same_half = lax.ppermute(same[:half], ('row', 'col'), same_pairs)  7.59 us
    ppermute x1, starting transfers between devices, local(): same_half = lax.ppermute(same[:half], ('row', 'col'), same_pairs)  4.47 us
  transfers between devices with their start and end apart: 30, of which 13 were waited for; matrix products, arithmetic and copies ran while one was open for 0% of the time, Pallas kernels for 41%

profile of v4, /device:TPU:2, one launch (start us, length us, event | category | flops | bytes accessed | tf_op | source)
XLA Modules:
  0.0 158.9 jit_solution(3069695832159082478)
XLA Ops:
  0.7 1.6 %copy-done.5 = f32[256,2048]{1,0:T(8,128)S(1)} copy-done((f32[256,2048]{1,0:T(8,128)S(1)}, f32[256,2048]{1,0:T(8,128)}, u32[]{:S(2)}) %copy-start.5) | copy-done | bytes 2097176
  2.3 1.1 part_orbitals.1
  3.4 1.6 collective-permute-start.1
  5.0 1.1 part_images.1
  6.1 0.8 part_cores.1
  8.1 13.7 %rotate.1.refs_15_ = f32[256,2048]{1,0:T(8,128)} custom-call(s32[7]{0:T(128)S(1)} %stack.31.at, f32[256,2048]{1,0:T(8,128)S(1)} %copy-done.6, f32[2048,2048]{1,0:T(8,128)} %refs_1_.1, f32[256,1536]{1,0:T(8,128)S(1)} %get-tuple-element.27.refs_2_), custom_call_target="tpu_custom_call" | custom-call | tf_op jit(solution)/shard_map/rotate/pallas_call | solution.py:61
  21.8 7.8 %collective-permute-done.1.refs_4_.refs_5_.refs_12_ = f32[256,1024]{1,0:T(8,128)S(1)} collective-permute-done((f32[256,1024]{1,0:T(8,128)S(1)}, f32[256,1024]{1,0:T(8,128)S(1)}, u32[]{:S(2)}, u32[]{:S(2)}) %collective-permute-start.1) | collective-permute-done | bytes 1048608 | tf_op jit(solution)/shard_map/ppermute | solution.py:81
  30.2 1.5 collective-permute-start.11
  32.4 6.6 %overlap_same.1 = (f32[1,4,192,256]{3,2,1,0:T(8,128)S(1)}, f32[1,4,192,256]{3,2,1,0:T(8,128)S(1)}) custom-call(s32[7]{0:T(128)S(1)} %stack.31.at, f32[256,1024]{1,0:T(8,128)S(1)} %get-tuple-element.24.refs_1_.refs_2_.refs_0_.refs_10_, f32[256,1024]{1,0:T(8,128)S(1)} %get-tuple-element.24.refs_1_.refs_2_.refs_0_.refs_10_, ...), custom_call_target="tpu_custom_call" | custom-call | tf_op jit(solution)/shard_map/overlap_same/pallas_call | solution.py:61
  39.1 12.9 %collective-permute-done.6.refs_12_ = f32[256,1024]{1,0:T(8,128)S(1)} collective-permute-done((f32[256,1024]{1,0:T(8,128)S(1)}, f32[256,1024]{1,0:T(8,128)S(1)}, u32[]{:S(2)}, u32[]{:S(2)}) %collective-permute-start.6) | collective-permute-done | bytes 1048608 | tf_op jit(solution)/shard_map/ppermute | solution.py:81
  52.8 1.5 collective-permute-done.9.refs_15_
  54.8 4.8 %project.4 = (f32[1,2,256,256]{3,2,1,0:T(8,128)S(1)}, f32[1,2,256,256]{3,2,1,0:T(8,128)S(1)}) custom-call(s32[7]{0:T(128)S(1)} %stack.31.at, f32[256,1024]{1,0:T(8,128)S(1)} %get-tuple-element.24.refs_1_.refs_2_.refs_0_.refs_10_, f32[256,1024]{1,0:T(8,128)S(1)} %get-tuple-element.24.refs_1_.refs_2_.refs_0_.refs_10_, ...), custom_call_target="tpu_custom_call" | custom-call | tf_op jit(solution)/shard_map/project/pallas_call | solution.py:61
  59.7 1.6 %halve.10.refs_16_ = f32[1,2,192,256]{3,2,1,0:T(8,128)S(1)} custom-call(s32[7]{0:T(128)S(1)} %stack.31.at, f32[1,4,192,256]{3,2,1,0:T(8,128)S(1)} %get-tuple-element.29.refs_16_.refs_0_, f32[1,4,192,256]{3,2,1,0:T(8,128)S(1)} %collective-permute-done.4.refs_1_, f32[1,2,256,256]{3,2,1,0:T(8,128)S(1)} %get-tuple-element.33.refs_2_.refs_0_), custom_call_target="tpu_custom_call" | custom-call | tf_op jit(solution)/shard_map/halve/pallas_call | solution.py:61
  61.3 2.1 %collective-permute-start.10 = (f32[1,2,192,256]{3,2,1,0:T(8,128)S(1)}, f32[1,2,192,256]{3,2,1,0:T(8,128)S(1)}, u32[]{:S(2)}, u32[]{:S(2)}) collective-permute-start(f32[1,2,192,256]{3,2,1,0:T(8,128)S(1)} %halve.10.refs_16_), channel_id=1, source_target_pairs={{0,2},{1,3},{2,0},{3,1},{4,6},{5,7},{6,4},{7,5},{8,10},{9,11},{10,... | collective-permute-start | bytes 1179656 | tf_op jit(solution)/shard_map/ppermute | solution.py:81
  63.4 4.8 %project.5 = (f32[1,2,256,256]{3,2,1,0:T(8,128)S(1)}, f32[1,2,256,256]{3,2,1,0:T(8,128)S(1)}) custom-call(s32[7]{0:T(128)S(1)} %stack.31.at, f32[256,1024]{1,0:T(8,128)S(1)} %get-tuple-element.24.refs_1_.refs_2_.refs_0_.refs_10_, f32[256,1024]{1,0:T(8,128)S(1)} %get-tuple-element.24.refs_1_.refs_2_.refs_0_.refs_10_, ...), custom_call_target="tpu_custom_call" | custom-call | tf_op jit(solution)/shard_map/project/pallas_call | solution.py:61
  68.2 5.1 %collective-permute-done.11.refs_4_.refs_5_ = f32[512,512]{1,0:T(8,128)S(1)} collective-permute-done((f32[512,512]{1,0:T(8,128)S(1)}, f32[512,512]{1,0:T(8,128)S(1)}, u32[]{:S(2)}, u32[]{:S(2)}) %collective-permute-start.11) | collective-permute-done | bytes 1048608 | tf_op jit(solution)/shard_map/ppermute | solution.py:81
  74.3 0.7 collective-permute-done.13.refs_8_.refs_9_
  75.3 7.0 %overlap_mixed.1 = (f32[1,4,128,256]{3,2,1,0:T(8,128)S(1)}, f32[1,4,128,256]{3,2,1,0:T(8,128)S(1)}) custom-call(s32[7]{0:T(128)S(1)} %stack.31.at, f32[256,1024]{1,0:T(8,128)S(1)} %get-tuple-element.25.refs_1_.refs_0_, f32[256,1024]{1,0:T(8,128)S(1)} %get-tuple-element.25.refs_1_.refs_0_, f32[256,1536]{1,0:T(8,128)} %copy-done.8, f32[256,1536]{1,0:T(8,128)} %copy-done.8, ...), custom_call_target="tpu_custom_call" | custom-call | tf_op jit(solution)/shard_map/overlap_mixed/pallas_call | solution.py:61
  82.3 0.7 collective-permute-start.18
  83.0 1.4 halve.11.refs_4_
  84.4 2.7 %collective-permute-start.15 = (f32[1,1,192,256]{3,2,1,0:T(8,128)S(1)}, f32[1,1,192,256]{3,2,1,0:T(8,128)S(1)}, u32[]{:S(2)}, u32[]{:S(2)}) collective-permute-start(f32[1,1,192,256]{3,2,1,0:T(8,128)S(1)} %halve.11.refs_4_), channel_id=1, source_target_pairs={{0,4},{1,5},{2,6},{3,7},{4,0},{5,1},{6,2},{7,3},{8,12},{9,13},{10,... | collective-permute-start | bytes 589832 | tf_op jit(solution)/shard_map/ppermute | solution.py:81
  87.1 1.7 %collective-permute-done.16.refs_3_ = f32[1,2,256,256]{3,2,1,0:T(8,128)S(1)} collective-permute-done((f32[1,2,256,256]{3,2,1,0:T(8,128)S(1)}, f32[1,2,256,256]{3,2,1,0:T(8,128)S(1)}, u32[]{:S(2)}, u32[]{:S(2)}) %collective-permute-start.16) | collective-permute-done | bytes 524320 | tf_op jit(solution)/shard_map/ppermute | solution.py:81
  88.7 1.0 halve.12.refs_16_
  89.7 1.6 %collective-permute-start.20 = (f32[1,2,256,256]{3,2,1,0:T(8,128)S(1)}, f32[1,2,256,256]{3,2,1,0:T(8,128)S(1)}, u32[]{:S(2)}, u32[]{:S(2)}) collective-permute-start(f32[1,2,256,256]{3,2,1,0:T(8,128)S(1)} %halve.12.refs_16_), channel_id=1, source_target_pairs={{0,2},{1,3},{2,0},{3,1},{4,6},{5,7},{6,4},{7,5},{8,10},{9,11},{10,... | collective-permute-start | bytes 1572872 | tf_op jit(solution)/shard_map/ppermute | solution.py:81
  91.3 5.4 %project.6 = (f32[1,4,128,256]{3,2,1,0:T(8,128)S(1)}, f32[1,4,128,256]{3,2,1,0:T(8,128)S(1)}) custom-call(s32[7]{0:T(128)S(1)} %stack.31.at, f32[256,1024]{1,0:T(8,128)S(1)} %get-tuple-element.25.refs_1_.refs_0_, f32[256,1024]{1,0:T(8,128)S(1)} %get-tuple-element.25.refs_1_.refs_0_, f32[256,1536]{1,0:T(8,128)} %copy-done.8, f32[256,1536]{1,0:T(8,128)} %copy-done.8, ...), custom_call_target="tpu_custom_call" | custom-call | tf_op jit(solution)/shard_map/project/pallas_call | solution.py:61
  97.3 1.6 %finish.2.refs_16_.refs_0_ = f32[192,256]{1,0:T(8,128)S(1)} custom-call(s32[7]{0:T(128)S(1)} %stack.31.at, f32[1,4,192,256]{3,2,1,0:T(8,128)S(1)} %get-tuple-element.29.refs_16_.refs_0_, f32[1,4,192,256]{3,2,1,0:T(8,128)S(1)} %collective-permute-done.4.refs_1_, f32[1,2,192,256]{3,2,1,0:T(8,128)S(1)} %collective-permute-done.10.refs_2_, ...), custom_call_target="tpu_custom_call" | custom-call | tf_op jit(solution)/shard_map/finish/pallas_call | solution.py:61
  99.0 5.2 %project.7 = (f32[1,4,128,256]{3,2,1,0:T(8,128)S(1)}, f32[1,4,128,256]{3,2,1,0:T(8,128)S(1)}) custom-call(s32[7]{0:T(128)S(1)} %stack.31.at, f32[256,1024]{1,0:T(8,128)S(1)} %get-tuple-element.25.refs_1_.refs_0_, f32[256,1024]{1,0:T(8,128)S(1)} %get-tuple-element.25.refs_1_.refs_0_, f32[256,1536]{1,0:T(8,128)} %copy-done.8, f32[256,1536]{1,0:T(8,128)} %copy-done.8, ...), custom_call_target="tpu_custom_call" | custom-call | tf_op jit(solution)/shard_map/project/pallas_call | solution.py:61
  104.2 1.6 collective-permute-start.24
  105.8 1.3 halve.13.refs_5_
  107.6 4.5 %collective-permute-start.17 = (f32[128,256]{1,0:T(8,128)S(1)}, f32[128,256]{1,0:T(8,128)S(1)}, u32[]{:S(2)}, u32[]{:S(2)}) collective-permute-start(f32[128,256]{1,0:T(8,128)S(1)} %slice.35), channel_id=1, source_target_pairs={{2,8},{3,9},{4,16},{5,17},{6,24},{7,25},{8,2},{9,3},{12,18},{13,19... | collective-permute-start | bytes 393224 | tf_op jit(solution)/shard_map/ppermute | solution.py:512
  112.1 0.7 halve.14.refs_3_
  112.9 0.6 collective-permute-done.19.refs_2_
  113.5 1.1 halve.15.refs_2_
  114.6 1.3 halve.16.refs_2_
  116.0 1.2 collective-permute-start.23
  117.1 7.6 %collective-permute-done.17.refs_3_.refs_1_ = f32[128,256]{1,0:T(8,128)S(1)} collective-permute-done((f32[128,256]{1,0:T(8,128)S(1)}, f32[128,256]{1,0:T(8,128)S(1)}, u32[]{:S(2)}, u32[]{:S(2)}) %collective-permute-start.17) | collective-permute-done | bytes 131104 | tf_op jit(solution)/shard_map/ppermute | solution.py:512
  124.7 1.3 halve.17.refs_3_
  126.0 1.3 collective-permute-start.27
  127.3 0.6 collective-permute-start.21
  128.0 3.3 %collective-permute-done.23.refs_2_.refs_8_ = f32[1,2,128,256]{3,2,1,0:T(8,128)S(1)} collective-permute-done((f32[1,2,128,256]{3,2,1,0:T(8,128)S(1)}, f32[1,2,128,256]{3,2,1,0:T(8,128)S(1)}, u32[]{:S(2)}, u32[]{:S(2)}) %collective-permute-start.23) | collective-permute-done | bytes 262176 | tf_op jit(solution)/shard_map/ppermute | solution.py:81
  131.3 1.1 halve.18.refs_4_
  132.4 8.1 %collective-permute-start.28 = (f32[1,1,128,256]{3,2,1,0:T(8,128)S(1)}, f32[1,1,128,256]{3,2,1,0:T(8,128)S(1)}, u32[]{:S(2)}, u32[]{:S(2)}) collective-permute-start(f32[1,1,128,256]{3,2,1,0:T(8,128)S(1)} %halve.18.refs_4_), channel_id=1, source_target_pairs={{0,4},{1,5},{2,6},{3,7},{4,0},{5,1},{6,2},{7,3},{8,12},{9,13},{10,... | collective-permute-start | bytes 393224 | tf_op jit(solution)/shard_map/ppermute | solution.py:81
  140.5 1.3 finish.3.refs_3_.refs_2_
  141.9 1.1 halve.19.refs_4_
  143.0 1.4 collective-permute-start.29
  144.4 9.8 %collective-permute-done.26.refs_3_ = f32[128,256]{1,0:T(8,128)S(1)} collective-permute-done((f32[128,256]{1,0:T(8,128)S(1)}, f32[128,256]{1,0:T(8,128)S(1)}, u32[]{:S(2)}, u32[]{:S(2)}) %collective-permute-start.26) | collective-permute-done | bytes 131104 | tf_op jit(solution)/shard_map/ppermute | solution.py:532
  154.2 1.5 assemble_overlap.1.refs_14_
  155.7 3.1 %assemble.1 = f32[512,256]{1,0:T(8,128)} custom-call(s32[7]{0:T(128)S(1)} %stack.31.at, f32[1,2,256,256]{3,2,1,0:T(8,128)S(1)} %get-tuple-element.33.refs_2_.refs_0_, f32[1,2,256,256]{3,2,1,0:T(8,128)S(1)} %get-tuple-element.35.refs_15_.refs_1_, f32[1,2,256,256]{3,2,1,0:T(8,128)S(1)} %collective-permute-done.14.refs_16_.refs_2_, ...), custom_call_target="tpu_custom_call" | custom-call | tf_op jit(solution)/shard_map/assemble/pallas_call | solution.py:61
  (62 shorter events, 6.6 us)
Async XLA Ops:
  0.7 1.6 %copy-start.5 = (f32[256,2048]{1,0:T(8,128)S(1)}, f32[256,2048]{1,0:T(8,128)}, u32[]{:S(2)}) copy-start(f32[256,2048]{1,0:T(8,128)} %refs_0_.5) | copy-start | bytes 6291460
  2.3 2.7 %copy-start.7 = (f32[256,2048]{1,0:T(8,128)S(1)}, f32[256,2048]{1,0:T(8,128)}, u32[]{:S(2)}) copy-start(f32[256,2048]{1,0:T(8,128)} %refs_0_.4) | copy-start | bytes 6291460
  3.4 60.0 %copy-start = (f32[256,1024]{1,0:T(8,128)}, f32[256,1024]{1,0:T(8,128)S(1)}, u32[]{:S(2)}) copy-start(f32[256,1024]{1,0:T(8,128)S(1)} %get-tuple-element.24.refs_1_.refs_2_.refs_0_.refs_10_) | copy-start | bytes 3145732
  3.4 26.1 %collective-permute-start.1 = (f32[256,1024]{1,0:T(8,128)S(1)}, f32[256,1024]{1,0:T(8,128)S(1)}, u32[]{:S(2)}, u32[]{:S(2)}) collective-permute-start(f32[256,1024]{1,0:T(8,128)S(1)} %get-tuple-element.25.refs_1_.refs_0_), channel_id=1, source_target_pairs={{0,1},{1,0},{2,3},{3,2},{4,5},{5,4},{6,7},{7,6},{8,9},{9,8},{10,11... | collective-permute-start | bytes 3145736 | tf_op jit(solution)/shard_map/ppermute | solution.py:81
  5.0 25.2 %collective-permute-start = (f32[256,1024]{1,0:T(8,128)S(1)}, f32[256,1024]{1,0:T(8,128)S(1)}, u32[]{:S(2)}, u32[]{:S(2)}) collective-permute-start(f32[256,1024]{1,0:T(8,128)S(1)} %get-tuple-element.24.refs_1_.refs_2_.refs_0_.refs_10_), channel_id=1, source_target_pairs={{0,8},{8,0},{16,24},{24,16},{1,9},{9,1},{17,25},{25,17},{2,10},{10... | collective-permute-start | bytes 3145736 | tf_op jit(solution)/shard_map/ppermute | solution.py:81
  6.1 1.0 copy-start.3
  6.1 2.0 %copy-start.6 = (f32[256,2048]{1,0:T(8,128)S(1)}, f32[256,2048]{1,0:T(8,128)}, u32[]{:S(2)}) copy-start(f32[256,2048]{1,0:T(8,128)} %refs_0_.5) | copy-start | bytes 6291460
  7.1 45.7 %collective-permute-start.5 = (f32[256,1536]{1,0:T(8,128)S(1)}, f32[256,1536]{1,0:T(8,128)S(1)}, u32[]{:S(2)}, u32[]{:S(2)}) collective-permute-start(f32[256,1536]{1,0:T(8,128)S(1)} %get-tuple-element.27.refs_2_), channel_id=1, source_target_pairs={{0,8},{8,0},{16,24},{24,16},{1,9},{9,1},{17,25},{25,17},{2,10},{10... | collective-permute-start | bytes 4718600 | tf_op jit(solution)/shard_map/ppermute | solution.py:81
  7.6 44.4 %collective-permute-start.6 = (f32[256,1024]{1,0:T(8,128)S(1)}, f32[256,1024]{1,0:T(8,128)S(1)}, u32[]{:S(2)}, u32[]{:S(2)}) collective-permute-start(f32[256,1024]{1,0:T(8,128)S(1)} %get-tuple-element.31), channel_id=1, source_target_pairs={{0,1},{1,0},{2,3},{3,2},{4,5},{5,4},{6,7},{7,6},{8,9},{9,8},{10,11... | collective-permute-start | bytes 3145736 | tf_op jit(solution)/shard_map/ppermute | solution.py:81
  29.5 9.5 %copy-start.1 = (f32[256,1024]{1,0:T(8,128)}, f32[256,1024]{1,0:T(8,128)S(1)}, u32[]{:S(2)}) copy-start(f32[256,1024]{1,0:T(8,128)S(1)} %collective-permute-done.1.refs_4_.refs_5_.refs_12_) | copy-start | bytes 3145732
  29.6 2.1 %collective-permute-start.3 = (f32[128,1024]{1,0:T(8,128)S(1)}, f32[128,1024]{1,0:T(8,128)S(1)}, u32[]{:S(2)}, u32[]{:S(2)}) collective-permute-start(f32[128,1024]{1,0:T(8,128)S(1)} %get-tuple-element.49), channel_id=1, source_target_pairs={{0,8},{8,0},{16,24},{24,16},{1,9},{9,1},{17,25},{25,17},{2,10},{10... | collective-permute-start | bytes 1572872 | tf_op jit(solution)/shard_map/ppermute | solution.py:81
  29.7 2.6 %collective-permute-start.2 = (f32[128,1024]{1,0:T(8,128)S(1)}, f32[128,1024]{1,0:T(8,128)S(1)}, u32[]{:S(2)}, u32[]{:S(2)}) collective-permute-start(f32[128,1024]{1,0:T(8,128)S(1)} %get-tuple-element.50), channel_id=1, source_target_pairs={{0,8},{8,0},{16,24},{24,16},{1,9},{9,1},{17,25},{25,17},{2,10},{10... | collective-permute-start | bytes 1572872 | tf_op jit(solution)/shard_map/ppermute | solution.py:81
  30.2 33.2 %copy-start.2 = (f32[256,1024]{1,0:T(8,128)}, f32[256,1024]{1,0:T(8,128)S(1)}, u32[]{:S(2)}) copy-start(f32[256,1024]{1,0:T(8,128)S(1)} %collective-permute-done.refs_2_.refs_3_.refs_11_) | copy-start | bytes 3145732
  30.2 43.1 %collective-permute-start.11 = (f32[512,512]{1,0:T(8,128)S(1)}, f32[512,512]{1,0:T(8,128)S(1)}, u32[]{:S(2)}, u32[]{:S(2)}) collective-permute-start(f32[512,512]{1,0:T(8,128)S(1)} %get-tuple-element.34), channel_id=1, source_target_pairs={{0,1},{1,0},{2,3},{3,2},{4,5},{5,4},{6,7},{7,6},{8,9},{9,8},{10,11... | collective-permute-start | bytes 3145736 | tf_op jit(solution)/shard_map/ppermute | solution.py:81
  39.0 20.6 %collective-permute-start.4 = (f32[1,4,192,256]{3,2,1,0:T(8,128)S(1)}, f32[1,4,192,256]{3,2,1,0:T(8,128)S(1)}, u32[]{:S(2)}, u32[]{:S(2)}) collective-permute-start(f32[1,4,192,256]{3,2,1,0:T(8,128)S(1)} %get-tuple-element.30), channel_id=1, source_target_pairs={{0,16},{8,24},{16,0},{24,8},{1,17},{9,25},{17,1},{25,9},{2,18},{10... | collective-permute-start | bytes 2359304 | tf_op jit(solution)/shard_map/ppermute | solution.py:81
  52.0 2.8 %copy-start.9 = (f32[256,1024]{1,0:T(8,128)}, f32[256,1024]{1,0:T(8,128)S(1)}, u32[]{:S(2)}) copy-start(f32[256,1024]{1,0:T(8,128)S(1)} %collective-permute-done.6.refs_12_) | copy-start | bytes 3145732
  52.0 2.7 %collective-permute-start.7 = (f32[96,1024]{1,0:T(8,128)S(1)}, f32[96,1024]{1,0:T(8,128)S(1)}, u32[]{:S(2)}, u32[]{:S(2)}) collective-permute-start(f32[96,1024]{1,0:T(8,128)S(1)} %slice.29), channel_id=1, source_target_pairs={{0,8},{8,0},{16,24},{24,16},{1,9},{9,1},{17,25},{25,17},{2,10},{10... | collective-permute-start | bytes 1179656 | tf_op jit(solution)/shard_map/ppermute | solution.py:81
  52.2 2.1 %collective-permute-start.9 = (f32[80,1024]{1,0:T(8,128)S(1)}, f32[80,1024]{1,0:T(8,128)S(1)}, u32[]{:S(2)}, u32[]{:S(2)}) collective-permute-start(f32[80,1024]{1,0:T(8,128)S(1)} %get-tuple-element.47), channel_id=1, source_target_pairs={{0,8},{8,0},{16,24},{24,16},{1,9},{9,1},{17,25},{25,17},{2,10},{10... | collective-permute-start | bytes 983048 | tf_op jit(solution)/shard_map/ppermute | solution.py:81
  52.7 2.0 %copy-start.8 = (f32[256,1536]{1,0:T(8,128)}, f32[256,1536]{1,0:T(8,128)S(1)}, u32[]{:S(2)}) copy-start(f32[256,1536]{1,0:T(8,128)S(1)} %collective-permute-done.5.refs_11_.refs_2_.refs_3_) | copy-start | bytes 4718596
  52.7 2.0 %collective-permute-start.8 = (f32[80,1024]{1,0:T(8,128)S(1)}, f32[80,1024]{1,0:T(8,128)S(1)}, u32[]{:S(2)}, u32[]{:S(2)}) collective-permute-start(f32[80,1024]{1,0:T(8,128)S(1)} %get-tuple-element.48), channel_id=1, source_target_pairs={{0,8},{8,0},{16,24},{24,16},{1,9},{9,1},{17,25},{25,17},{2,10},{10... | collective-permute-start | bytes 983048 | tf_op jit(solution)/shard_map/ppermute | solution.py:81
  59.6 14.7 %collective-permute-start.14 = (f32[1,2,256,256]{3,2,1,0:T(8,128)S(1)}, f32[1,2,256,256]{3,2,1,0:T(8,128)S(1)}, u32[]{:S(2)}, u32[]{:S(2)}) collective-permute-start(f32[1,2,256,256]{3,2,1,0:T(8,128)S(1)} %get-tuple-element.37), channel_id=1, source_target_pairs={{0,16},{8,24},{16,0},{24,8},{1,17},{9,25},{17,1},{25,9},{2,18},{10... | collective-permute-start | bytes 1572872 | tf_op jit(solution)/shard_map/ppermute | solution.py:81
  61.3 21.7 %collective-permute-start.10 = (f32[1,2,192,256]{3,2,1,0:T(8,128)S(1)}, f32[1,2,192,256]{3,2,1,0:T(8,128)S(1)}, u32[]{:S(2)}, u32[]{:S(2)}) collective-permute-start(f32[1,2,192,256]{3,2,1,0:T(8,128)S(1)} %halve.10.refs_16_), channel_id=1, source_target_pairs={{0,2},{1,3},{2,0},{3,1},{4,6},{5,7},{6,4},{7,5},{8,10},{9,11},{10,... | collective-permute-start | bytes 1179656 | tf_op jit(solution)/shard_map/ppermute | solution.py:81
  73.4 1.6 %collective-permute-start.13 = (f32[128,512]{1,0:T(8,128)S(1)}, f32[128,512]{1,0:T(8,128)S(1)}, u32[]{:S(2)}, u32[]{:S(2)}) collective-permute-start(f32[128,512]{1,0:T(8,128)S(1)} %get-tuple-element.45), channel_id=1, source_target_pairs={{0,8},{8,0},{16,24},{24,16},{1,9},{9,1},{17,25},{25,17},{2,10},{10... | collective-permute-start | bytes 786440 | tf_op jit(solution)/shard_map/ppermute | solution.py:81
  73.4 1.9 %collective-permute-start.12 = (f32[128,512]{1,0:T(8,128)S(1)}, f32[128,512]{1,0:T(8,128)S(1)}, u32[]{:S(2)}, u32[]{:S(2)}) collective-permute-start(f32[128,512]{1,0:T(8,128)S(1)} %get-tuple-element.46), channel_id=1, source_target_pairs={{0,8},{8,0},{16,24},{24,16},{1,9},{9,1},{17,25},{25,17},{2,10},{10... | collective-permute-start | bytes 786440 | tf_op jit(solution)/shard_map/ppermute | solution.py:81
  73.9 14.8 %collective-permute-start.16 = (f32[1,2,256,256]{3,2,1,0:T(8,128)S(1)}, f32[1,2,256,256]{3,2,1,0:T(8,128)S(1)}, u32[]{:S(2)}, u32[]{:S(2)}) collective-permute-start(f32[1,2,256,256]{3,2,1,0:T(8,128)S(1)} %get-tuple-element.39), channel_id=1, source_target_pairs={{0,16},{8,24},{16,0},{24,8},{1,17},{9,25},{17,1},{25,9},{2,18},{10... | collective-permute-start | bytes 1572872 | tf_op jit(solution)/shard_map/ppermute | solution.py:81
  82.3 23.5 %collective-permute-start.18 = (f32[1,4,128,256]{3,2,1,0:T(8,128)S(1)}, f32[1,4,128,256]{3,2,1,0:T(8,128)S(1)}, u32[]{:S(2)}, u32[]{:S(2)}) collective-permute-start(f32[1,4,128,256]{3,2,1,0:T(8,128)S(1)} %get-tuple-element.41), channel_id=1, source_target_pairs={{0,16},{8,24},{16,0},{24,8},{1,17},{9,25},{17,1},{25,9},{2,18},{10... | collective-permute-start | bytes 1572872 | tf_op jit(solution)/shard_map/ppermute | solution.py:81
  84.4 12.9 %collective-permute-start.15 = (f32[1,1,192,256]{3,2,1,0:T(8,128)S(1)}, f32[1,1,192,256]{3,2,1,0:T(8,128)S(1)}, u32[]{:S(2)}, u32[]{:S(2)}) collective-permute-start(f32[1,1,192,256]{3,2,1,0:T(8,128)S(1)} %halve.11.refs_4_), channel_id=1, source_target_pairs={{0,4},{1,5},{2,6},{3,7},{4,0},{5,1},{6,2},{7,3},{8,12},{9,13},{10,... | collective-permute-start | bytes 589832 | tf_op jit(solution)/shard_map/ppermute | solution.py:81
  89.7 22.4 %collective-permute-start.20 = (f32[1,2,256,256]{3,2,1,0:T(8,128)S(1)}, f32[1,2,256,256]{3,2,1,0:T(8,128)S(1)}, u32[]{:S(2)}, u32[]{:S(2)}) collective-permute-start(f32[1,2,256,256]{3,2,1,0:T(8,128)S(1)} %halve.12.refs_16_), channel_id=1, source_target_pairs={{0,2},{1,3},{2,0},{3,1},{4,6},{5,7},{6,4},{7,5},{8,10},{9,11},{10,... | collective-permute-start | bytes 1572872 | tf_op jit(solution)/shard_map/ppermute | solution.py:81
  96.7 2.3 %copy-start.4 = (f32[256,1024]{1,0:T(8,128)S(1)}, f32[256,1024]{1,0:T(8,128)}, u32[]{:S(2)}) copy-start(f32[256,1024]{1,0:T(8,128)} %copy-done.3) | copy-start | bytes 3145732
  96.7 17.9 %collective-permute-start.22 = (f32[1,4,128,256]{3,2,1,0:T(8,128)S(1)}, f32[1,4,128,256]{3,2,1,0:T(8,128)S(1)}, u32[]{:S(2)}, u32[]{:S(2)}) collective-permute-start(f32[1,4,128,256]{3,2,1,0:T(8,128)S(1)} %get-tuple-element.43), channel_id=1, source_target_pairs={{0,16},{8,24},{16,0},{24,8},{1,17},{9,25},{17,1},{25,9},{2,18},{10... | collective-permute-start | bytes 1572872 | tf_op jit(solution)/shard_map/ppermute | solution.py:81
  104.2 20.5 %collective-permute-start.24 = (f32[1,4,128,256]{3,2,1,0:T(8,128)S(1)}, f32[1,4,128,256]{3,2,1,0:T(8,128)S(1)}, u32[]{:S(2)}, u32[]{:S(2)}) collective-permute-start(f32[1,4,128,256]{3,2,1,0:T(8,128)S(1)} %get-tuple-element.44), channel_id=1, source_target_pairs={{0,16},{8,24},{16,0},{24,8},{1,17},{9,25},{17,1},{25,9},{2,18},{10... | collective-permute-start | bytes 1572872 | tf_op jit(solution)/shard_map/ppermute | solution.py:81
  107.1 6.4 %collective-permute-start.19 = (f32[1,2,128,256]{3,2,1,0:T(8,128)S(1)}, f32[1,2,128,256]{3,2,1,0:T(8,128)S(1)}, u32[]{:S(2)}, u32[]{:S(2)}) collective-permute-start(f32[1,2,128,256]{3,2,1,0:T(8,128)S(1)} %halve.13.refs_5_), channel_id=1, source_target_pairs={{0,2},{1,3},{2,0},{3,1},{4,6},{5,7},{6,4},{7,5},{8,10},{9,11},{10,... | collective-permute-start | bytes 786440 | tf_op jit(solution)/shard_map/ppermute | solution.py:81
  107.6 17.1 %collective-permute-start.17 = (f32[128,256]{1,0:T(8,128)S(1)}, f32[128,256]{1,0:T(8,128)S(1)}, u32[]{:S(2)}, u32[]{:S(2)}) collective-permute-start(f32[128,256]{1,0:T(8,128)S(1)} %slice.35), channel_id=1, source_target_pairs={{2,8},{3,9},{4,16},{5,17},{6,24},{7,25},{8,2},{9,3},{12,18},{13,19... | collective-permute-start | bytes 393224 | tf_op jit(solution)/shard_map/ppermute | solution.py:512
  112.8 15.1 %collective-permute-start.25 = (f32[1,1,256,256]{3,2,1,0:T(8,128)S(1)}, f32[1,1,256,256]{3,2,1,0:T(8,128)S(1)}, u32[]{:S(2)}, u32[]{:S(2)}) collective-permute-start(f32[1,1,256,256]{3,2,1,0:T(8,128)S(1)} %halve.14.refs_3_), channel_id=1, source_target_pairs={{0,4},{1,5},{2,6},{3,7},{4,0},{5,1},{6,2},{7,3},{8,12},{9,13},{10,... | collective-permute-start | bytes 786440 | tf_op jit(solution)/shard_map/ppermute | solution.py:81
  116.0 15.3 %collective-permute-start.23 = (f32[1,2,128,256]{3,2,1,0:T(8,128)S(1)}, f32[1,2,128,256]{3,2,1,0:T(8,128)S(1)}, u32[]{:S(2)}, u32[]{:S(2)}) collective-permute-start(f32[1,2,128,256]{3,2,1,0:T(8,128)S(1)} %halve.16.refs_2_), channel_id=1, source_target_pairs={{0,2},{1,3},{2,0},{3,1},{4,6},{5,7},{6,4},{7,5},{8,10},{9,11},{10,... | collective-permute-start | bytes 786440 | tf_op jit(solution)/shard_map/ppermute | solution.py:81
  126.0 15.8 %collective-permute-start.27 = (f32[1,2,128,256]{3,2,1,0:T(8,128)S(1)}, f32[1,2,128,256]{3,2,1,0:T(8,128)S(1)}, u32[]{:S(2)}, u32[]{:S(2)}) collective-permute-start(f32[1,2,128,256]{3,2,1,0:T(8,128)S(1)} %halve.17.refs_3_), channel_id=1, source_target_pairs={{0,2},{1,3},{2,0},{3,1},{4,6},{5,7},{6,4},{7,5},{8,10},{9,11},{10,... | collective-permute-start | bytes 786440 | tf_op jit(solution)/shard_map/ppermute | solution.py:81
  127.3 13.2 %collective-permute-start.21 = (f32[1,1,128,256]{3,2,1,0:T(8,128)S(1)}, f32[1,1,128,256]{3,2,1,0:T(8,128)S(1)}, u32[]{:S(2)}, u32[]{:S(2)}) collective-permute-start(f32[1,1,128,256]{3,2,1,0:T(8,128)S(1)} %halve.15.refs_2_), channel_id=1, source_target_pairs={{0,4},{1,5},{2,6},{3,7},{4,0},{5,1},{6,2},{7,3},{8,12},{9,13},{10,... | collective-permute-start | bytes 393224 | tf_op jit(solution)/shard_map/ppermute | solution.py:81
  132.4 23.3 %collective-permute-start.28 = (f32[1,1,128,256]{3,2,1,0:T(8,128)S(1)}, f32[1,1,128,256]{3,2,1,0:T(8,128)S(1)}, u32[]{:S(2)}, u32[]{:S(2)}) collective-permute-start(f32[1,1,128,256]{3,2,1,0:T(8,128)S(1)} %halve.18.refs_4_), channel_id=1, source_target_pairs={{0,4},{1,5},{2,6},{3,7},{4,0},{5,1},{6,2},{7,3},{8,12},{9,13},{10,... | collective-permute-start | bytes 393224 | tf_op jit(solution)/shard_map/ppermute | solution.py:81
  141.8 12.4 %collective-permute-start.26 = (f32[128,256]{1,0:T(8,128)S(1)}, f32[128,256]{1,0:T(8,128)S(1)}, u32[]{:S(2)}, u32[]{:S(2)}) collective-permute-start(f32[128,256]{1,0:T(8,128)S(1)} %finish.3.refs_3_.refs_2_), channel_id=1, source_target_pairs={{0,1},{1,0},{2,9},{3,8},{4,17},{5,16},{6,25},{7,24},{8,3},{9,2},{1... | collective-permute-start | bytes 393224 | tf_op jit(solution)/shard_map/ppermute | solution.py:532
  143.0 12.7 %collective-permute-start.29 = (f32[1,1,128,256]{3,2,1,0:T(8,128)S(1)}, f32[1,1,128,256]{3,2,1,0:T(8,128)S(1)}, u32[]{:S(2)}, u32[]{:S(2)}) collective-permute-start(f32[1,1,128,256]{3,2,1,0:T(8,128)S(1)} %halve.19.refs_4_), channel_id=1, source_target_pairs={{0,4},{1,5},{2,6},{3,7},{4,0},{5,1},{6,2},{7,3},{8,12},{9,13},{10,... | collective-permute-start | bytes 393224 | tf_op jit(solution)/shard_map/ppermute | solution.py:81

commit v5 on v4

--- a/solution.py
+++ b/solution.py
@@ -18,6 +18,13 @@
     dot = lambda a, b: jnp.dot(a, b, preferred_element_type=jnp.float32)
     (lh, ll), (rh, rl) = left, right
     return dot(lh, rh) + (dot(ll, rh) + dot(lh, rl))
+
+
+def multiply_stacked(left, right):
+    rows = left.shape[0] // 2
+    both = jnp.dot(left[...], right[0], preferred_element_type=jnp.float32)
+    rest = jnp.dot(left[:rows], right[1], preferred_element_type=jnp.float32)
+    return both[:rows] + (both[rows:] + rest)
 
 
 class Device:
@@ -163,20 +170,22 @@
 
     def body(at, *refs):
         lefts, rights = refs[:nr], refs[nr : nr + nc]
-        keep, send, high, low = refs[nr + nc :]
+        keep, send, left = refs[nr + nc :]
 
         @pl.when(pl.program_id(0) == 0)
         def _():
             start = 0
             for cells, blocks in zip(rows.cells, rows.blocks(lefts)):
                 for xi, block in enumerate(blocks):
-                    index = (slice(xi * width, (xi + 1) * width), slice(start, start + cells))
+                    at_cells = slice(start, start + cells)
+                    first = slice(xi * width, (xi + 1) * width)
+                    second = slice((X + xi) * width, (X + xi + 1) * width)
                     turned = block.T[cut * width : (cut + 1) * width]
-                    high[index], low[index] = split(turned)
+                    left[first, at_cells], left[second, at_cells] = split(turned)
                 start += cells
 
         right = split(jnp.concatenate([ref[...] for ref in rights], 0))
-        value = multiply((high[...], low[...]), right)
+        value = multiply_stacked(left, right)
         zz = stride * pl.program_id(0) + first
         for xi in range(X):
             part = value[xi * width : (xi + 1) * width]
@@ -199,7 +208,7 @@
             for array in columns
         ],
         [(top, steps, out_rows, b)] * 2, [out] * 2, grid=(steps,),
-        scratch=[pltpu.VMEM((X * width, total), jnp.bfloat16)] * 2,
+        scratch=[pltpu.VMEM((2 * X * width, total), jnp.bfloat16)],
     )
 
 

time: 160 us -> 160 us (level)
  no operation moved by 1% of the time
where the time goes in v5:
time: 160 us; the launch traced here: 159 us
  Pallas kernels  69.6 us (43%)
  waiting for transfers between devices  51.1 us (32%)
  starting transfers between devices  34.9 us (22%)
  local copies, waits for them, and re-layouts  2.11 us (1%)
    pallas_call x24, Pallas kernels, call(): pl.pallas_call(ordered, name=name, out_shape=[jax.ShapeDtypeStruct(s, jnp...  69.6 us
    ppermute x28, waiting for transfers between devices, flip(): return lax.ppermute(value, axis, [(i, i ^ mask) for i in range(count)])  33.8 us
    ppermute x28, starting transfers between devices, flip(): return lax.ppermute(value, axis, [(i, i ^ mask) for i in range(count)])  30.4 us
    ppermute x1, waiting for transfers between devices, local(): mixed_half = lax.ppermute(mixed, ('row', 'col'), mixed_pairs)  9.7 us
    ppermute x1, waiting for transfers between devices, local(): same_half = lax.ppermute(same[:half], ('row', 'col'), same_pairs)  7.6 us
    ppermute x1, starting transfers between devices, local(): same_half = lax.ppermute(same[:half], ('row', 'col'), same_pairs)  4.45 us
  transfers between devices with their start and end apart: 30, of which 13 were waited for; matrix products, arithmetic and copies ran while one was open for 0% of the time, Pallas kernels for 41%

profile of v5, /device:TPU:2, one launch (start us, length us, event | category | flops | bytes accessed | tf_op | source)
XLA Modules:
  0.0 158.9 jit_solution(1324535994605382423)
XLA Ops:
  0.7 1.6 %copy-done.5 = f32[256,2048]{1,0:T(8,128)S(1)} copy-done((f32[256,2048]{1,0:T(8,128)S(1)}, f32[256,2048]{1,0:T(8,128)}, u32[]{:S(2)}) %copy-start.5) | copy-done | bytes 2097176
  2.3 1.1 part_orbitals.1
  3.4 1.6 collective-permute-start.1
  5.0 1.1 part_images.1
  6.1 0.8 part_cores.1
  8.1 13.7 %rotate.1.refs_15_ = f32[256,2048]{1,0:T(8,128)} custom-call(s32[7]{0:T(128)S(1)} %stack.31.at, f32[256,2048]{1,0:T(8,128)S(1)} %copy-done.6, f32[2048,2048]{1,0:T(8,128)} %refs_1_.1, f32[256,1536]{1,0:T(8,128)S(1)} %get-tuple-element.27.refs_2_), custom_call_target="tpu_custom_call" | custom-call | tf_op jit(solution)/shard_map/rotate/pallas_call | solution.py:68
  21.8 7.8 %collective-permute-done.1.refs_4_.refs_5_.refs_12_ = f32[256,1024]{1,0:T(8,128)S(1)} collective-permute-done((f32[256,1024]{1,0:T(8,128)S(1)}, f32[256,1024]{1,0:T(8,128)S(1)}, u32[]{:S(2)}, u32[]{:S(2)}) %collective-permute-start.1) | collective-permute-done | bytes 1048608 | tf_op jit(solution)/shard_map/ppermute | solution.py:88
  30.2 1.5 collective-permute-start.11
  32.4 6.6 %overlap_same.1 = (f32[1,4,192,256]{3,2,1,0:T(8,128)S(1)}, f32[1,4,192,256]{3,2,1,0:T(8,128)S(1)}) custom-call(s32[7]{0:T(128)S(1)} %stack.31.at, f32[256,1024]{1,0:T(8,128)S(1)} %get-tuple-element.24.refs_1_.refs_2_.refs_0_.refs_10_, f32[256,1024]{1,0:T(8,128)S(1)} %get-tuple-element.24.refs_1_.refs_2_.refs_0_.refs_10_, ...), custom_call_target="tpu_custom_call" | custom-call | tf_op jit(solution)/shard_map/overlap_same/pallas_call | solution.py:68
  39.0 13.0 %collective-permute-done.6.refs_12_ = f32[256,1024]{1,0:T(8,128)S(1)} collective-permute-done((f32[256,1024]{1,0:T(8,128)S(1)}, f32[256,1024]{1,0:T(8,128)S(1)}, u32[]{:S(2)}, u32[]{:S(2)}) %collective-permute-start.6) | collective-permute-done | bytes 1048608 | tf_op jit(solution)/shard_map/ppermute | solution.py:88
  52.8 1.5 collective-permute-done.9.refs_15_
  54.8 4.8 %project.4 = (f32[1,2,256,256]{3,2,1,0:T(8,128)S(1)}, f32[1,2,256,256]{3,2,1,0:T(8,128)S(1)}) custom-call(s32[7]{0:T(128)S(1)} %stack.31.at, f32[256,1024]{1,0:T(8,128)S(1)} %get-tuple-element.24.refs_1_.refs_2_.refs_0_.refs_10_, f32[256,1024]{1,0:T(8,128)S(1)} %get-tuple-element.24.refs_1_.refs_2_.refs_0_.refs_10_, ...), custom_call_target="tpu_custom_call" | custom-call | tf_op jit(solution)/shard_map/project/pallas_call | solution.py:68
  59.6 1.6 %halve.10.refs_16_ = f32[1,2,192,256]{3,2,1,0:T(8,128)S(1)} custom-call(s32[7]{0:T(128)S(1)} %stack.31.at, f32[1,4,192,256]{3,2,1,0:T(8,128)S(1)} %get-tuple-element.29.refs_16_.refs_0_, f32[1,4,192,256]{3,2,1,0:T(8,128)S(1)} %collective-permute-done.4.refs_1_, f32[1,2,256,256]{3,2,1,0:T(8,128)S(1)} %get-tuple-element.33.refs_2_.refs_0_), custom_call_target="tpu_custom_call" | custom-call | tf_op jit(solution)/shard_map/halve/pallas_call | solution.py:68
  61.3 2.1 %collective-permute-start.10 = (f32[1,2,192,256]{3,2,1,0:T(8,128)S(1)}, f32[1,2,192,256]{3,2,1,0:T(8,128)S(1)}, u32[]{:S(2)}, u32[]{:S(2)}) collective-permute-start(f32[1,2,192,256]{3,2,1,0:T(8,128)S(1)} %halve.10.refs_16_), channel_id=1, source_target_pairs={{0,2},{1,3},{2,0},{3,1},{4,6},{5,7},{6,4},{7,5},{8,10},{9,11},{10,... | collective-permute-start | bytes 1179656 | tf_op jit(solution)/shard_map/ppermute | solution.py:88
  63.4 4.8 %project.5 = (f32[1,2,256,256]{3,2,1,0:T(8,128)S(1)}, f32[1,2,256,256]{3,2,1,0:T(8,128)S(1)}) custom-call(s32[7]{0:T(128)S(1)} %stack.31.at, f32[256,1024]{1,0:T(8,128)S(1)} %get-tuple-element.24.refs_1_.refs_2_.refs_0_.refs_10_, f32[256,1024]{1,0:T(8,128)S(1)} %get-tuple-element.24.refs_1_.refs_2_.refs_0_.refs_10_, ...), custom_call_target="tpu_custom_call" | custom-call | tf_op jit(solution)/shard_map/project/pallas_call | solution.py:68
  68.2 5.1 %collective-permute-done.11.refs_4_.refs_5_ = f32[512,512]{1,0:T(8,128)S(1)} collective-permute-done((f32[512,512]{1,0:T(8,128)S(1)}, f32[512,512]{1,0:T(8,128)S(1)}, u32[]{:S(2)}, u32[]{:S(2)}) %collective-permute-start.11) | collective-permute-done | bytes 1048608 | tf_op jit(solution)/shard_map/ppermute | solution.py:88
  74.3 0.7 collective-permute-done.13.refs_8_.refs_9_
  75.3 6.9 %overlap_mixed.1 = (f32[1,4,128,256]{3,2,1,0:T(8,128)S(1)}, f32[1,4,128,256]{3,2,1,0:T(8,128)S(1)}) custom-call(s32[7]{0:T(128)S(1)} %stack.31.at, f32[256,1024]{1,0:T(8,128)S(1)} %get-tuple-element.25.refs_1_.refs_0_, f32[256,1024]{1,0:T(8,128)S(1)} %get-tuple-element.25.refs_1_.refs_0_, f32[256,1536]{1,0:T(8,128)} %copy-done.8, f32[256,1536]{1,0:T(8,128)} %copy-done.8, ...), custom_call_target="tpu_custom_call" | custom-call | tf_op jit(solution)/shard_map/overlap_mixed/pallas_call | solution.py:68
  82.3 0.7 collective-permute-start.18
  83.0 1.4 halve.11.refs_4_
  84.4 2.7 %collective-permute-start.15 = (f32[1,1,192,256]{3,2,1,0:T(8,128)S(1)}, f32[1,1,192,256]{3,2,1,0:T(8,128)S(1)}, u32[]{:S(2)}, u32[]{:S(2)}) collective-permute-start(f32[1,1,192,256]{3,2,1,0:T(8,128)S(1)} %halve.11.refs_4_), channel_id=1, source_target_pairs={{0,4},{1,5},{2,6},{3,7},{4,0},{5,1},{6,2},{7,3},{8,12},{9,13},{10,... | collective-permute-start | bytes 589832 | tf_op jit(solution)/shard_map/ppermute | solution.py:88
  87.0 1.7 %collective-permute-done.16.refs_3_ = f32[1,2,256,256]{3,2,1,0:T(8,128)S(1)} collective-permute-done((f32[1,2,256,256]{3,2,1,0:T(8,128)S(1)}, f32[1,2,256,256]{3,2,1,0:T(8,128)S(1)}, u32[]{:S(2)}, u32[]{:S(2)}) %collective-permute-start.16) | collective-permute-done | bytes 524320 | tf_op jit(solution)/shard_map/ppermute | solution.py:88
  88.7 1.0 halve.12.refs_16_
  89.7 1.6 %collective-permute-start.20 = (f32[1,2,256,256]{3,2,1,0:T(8,128)S(1)}, f32[1,2,256,256]{3,2,1,0:T(8,128)S(1)}, u32[]{:S(2)}, u32[]{:S(2)}) collective-permute-start(f32[1,2,256,256]{3,2,1,0:T(8,128)S(1)} %halve.12.refs_16_), channel_id=1, source_target_pairs={{0,2},{1,3},{2,0},{3,1},{4,6},{5,7},{6,4},{7,5},{8,10},{9,11},{10,... | collective-permute-start | bytes 1572872 | tf_op jit(solution)/shard_map/ppermute | solution.py:88
  91.3 5.3 %project.6 = (f32[1,4,128,256]{3,2,1,0:T(8,128)S(1)}, f32[1,4,128,256]{3,2,1,0:T(8,128)S(1)}) custom-call(s32[7]{0:T(128)S(1)} %stack.31.at, f32[256,1024]{1,0:T(8,128)S(1)} %get-tuple-element.25.refs_1_.refs_0_, f32[256,1024]{1,0:T(8,128)S(1)} %get-tuple-element.25.refs_1_.refs_0_, f32[256,1536]{1,0:T(8,128)} %copy-done.8, f32[256,1536]{1,0:T(8,128)} %copy-done.8, ...), custom_call_target="tpu_custom_call" | custom-call | tf_op jit(solution)/shard_map/project/pallas_call | solution.py:68
  97.3 1.6 %finish.2.refs_16_.refs_0_ = f32[192,256]{1,0:T(8,128)S(1)} custom-call(s32[7]{0:T(128)S(1)} %stack.31.at, f32[1,4,192,256]{3,2,1,0:T(8,128)S(1)} %get-tuple-element.29.refs_16_.refs_0_, f32[1,4,192,256]{3,2,1,0:T(8,128)S(1)} %collective-permute-done.4.refs_1_, f32[1,2,192,256]{3,2,1,0:T(8,128)S(1)} %collective-permute-done.10.refs_2_, ...), custom_call_target="tpu_custom_call" | custom-call | tf_op jit(solution)/shard_map/finish/pallas_call | solution.py:68
  98.9 5.2 %project.7 = (f32[1,4,128,256]{3,2,1,0:T(8,128)S(1)}, f32[1,4,128,256]{3,2,1,0:T(8,128)S(1)}) custom-call(s32[7]{0:T(128)S(1)} %stack.31.at, f32[256,1024]{1,0:T(8,128)S(1)} %get-tuple-element.25.refs_1_.refs_0_, f32[256,1024]{1,0:T(8,128)S(1)} %get-tuple-element.25.refs_1_.refs_0_, f32[256,1536]{1,0:T(8,128)} %copy-done.8, f32[256,1536]{1,0:T(8,128)} %copy-done.8, ...), custom_call_target="tpu_custom_call" | custom-call | tf_op jit(solution)/shard_map/project/pallas_call | solution.py:68
  104.2 1.6 collective-permute-start.24
  105.8 1.3 halve.13.refs_5_
  107.6 4.5 %collective-permute-start.17 = (f32[128,256]{1,0:T(8,128)S(1)}, f32[128,256]{1,0:T(8,128)S(1)}, u32[]{:S(2)}, u32[]{:S(2)}) collective-permute-start(f32[128,256]{1,0:T(8,128)S(1)} %slice.35), channel_id=1, source_target_pairs={{2,8},{3,9},{4,16},{5,17},{6,24},{7,25},{8,2},{9,3},{12,18},{13,19... | collective-permute-start | bytes 393224 | tf_op jit(solution)/shard_map/ppermute | solution.py:521
  112.0 0.7 halve.14.refs_3_
  112.8 0.6 collective-permute-done.19.refs_2_
  113.5 1.1 halve.15.refs_2_
  114.6 1.3 halve.16.refs_2_
  115.9 1.2 collective-permute-start.23
  117.1 7.6 %collective-permute-done.17.refs_3_.refs_1_ = f32[128,256]{1,0:T(8,128)S(1)} collective-permute-done((f32[128,256]{1,0:T(8,128)S(1)}, f32[128,256]{1,0:T(8,128)S(1)}, u32[]{:S(2)}, u32[]{:S(2)}) %collective-permute-start.17) | collective-permute-done | bytes 131104 | tf_op jit(solution)/shard_map/ppermute | solution.py:521
  124.7 1.3 halve.17.refs_3_
  126.0 1.3 collective-permute-start.27
  127.3 0.6 collective-permute-start.21
  128.0 1.9 %collective-permute-done.23.refs_2_.refs_8_ = f32[1,2,128,256]{3,2,1,0:T(8,128)S(1)} collective-permute-done((f32[1,2,128,256]{3,2,1,0:T(8,128)S(1)}, f32[1,2,128,256]{3,2,1,0:T(8,128)S(1)}, u32[]{:S(2)}, u32[]{:S(2)}) %collective-permute-start.23) | collective-permute-done | bytes 262176 | tf_op jit(solution)/shard_map/ppermute | solution.py:88
  129.9 1.1 halve.18.refs_4_
  131.0 9.5 %collective-permute-start.28 = (f32[1,1,128,256]{3,2,1,0:T(8,128)S(1)}, f32[1,1,128,256]{3,2,1,0:T(8,128)S(1)}, u32[]{:S(2)}, u32[]{:S(2)}) collective-permute-start(f32[1,1,128,256]{3,2,1,0:T(8,128)S(1)} %halve.18.refs_4_), channel_id=1, source_target_pairs={{0,4},{1,5},{2,6},{3,7},{4,0},{5,1},{6,2},{7,3},{8,12},{9,13},{10,... | collective-permute-start | bytes 393224 | tf_op jit(solution)/shard_map/ppermute | solution.py:88
  140.4 1.3 finish.3.refs_3_.refs_2_
  141.8 1.1 halve.19.refs_4_
  142.9 1.5 collective-permute-start.29
  144.4 9.7 %collective-permute-done.26.refs_3_ = f32[128,256]{1,0:T(8,128)S(1)} collective-permute-done((f32[128,256]{1,0:T(8,128)S(1)}, f32[128,256]{1,0:T(8,128)S(1)}, u32[]{:S(2)}, u32[]{:S(2)}) %collective-permute-start.26) | collective-permute-done | bytes 131104 | tf_op jit(solution)/shard_map/ppermute | solution.py:541
  154.1 1.5 assemble_overlap.1.refs_14_
  155.6 3.1 %assemble.1 = f32[512,256]{1,0:T(8,128)} custom-call(s32[7]{0:T(128)S(1)} %stack.31.at, f32[1,2,256,256]{3,2,1,0:T(8,128)S(1)} %get-tuple-element.33.refs_2_.refs_0_, f32[1,2,256,256]{3,2,1,0:T(8,128)S(1)} %get-tuple-element.35.refs_15_.refs_1_, f32[1,2,256,256]{3,2,1,0:T(8,128)S(1)} %collective-permute-done.14.refs_16_.refs_2_, ...), custom_call_target="tpu_custom_call" | custom-call | tf_op jit(solution)/shard_map/assemble/pallas_call | solution.py:68
  (62 shorter events, 6.6 us)
Async XLA Ops:
  0.7 1.6 %copy-start.5 = (f32[256,2048]{1,0:T(8,128)S(1)}, f32[256,2048]{1,0:T(8,128)}, u32[]{:S(2)}) copy-start(f32[256,2048]{1,0:T(8,128)} %refs_0_.5) | copy-start | bytes 6291460
  2.3 2.7 %copy-start.7 = (f32[256,2048]{1,0:T(8,128)S(1)}, f32[256,2048]{1,0:T(8,128)}, u32[]{:S(2)}) copy-start(f32[256,2048]{1,0:T(8,128)} %refs_0_.4) | copy-start | bytes 6291460
  3.4 60.0 %copy-start = (f32[256,1024]{1,0:T(8,128)}, f32[256,1024]{1,0:T(8,128)S(1)}, u32[]{:S(2)}) copy-start(f32[256,1024]{1,0:T(8,128)S(1)} %get-tuple-element.24.refs_1_.refs_2_.refs_0_.refs_10_) | copy-start | bytes 3145732
  3.4 26.1 %collective-permute-start.1 = (f32[256,1024]{1,0:T(8,128)S(1)}, f32[256,1024]{1,0:T(8,128)S(1)}, u32[]{:S(2)}, u32[]{:S(2)}) collective-permute-start(f32[256,1024]{1,0:T(8,128)S(1)} %get-tuple-element.25.refs_1_.refs_0_), channel_id=1, source_target_pairs={{0,1},{1,0},{2,3},{3,2},{4,5},{5,4},{6,7},{7,6},{8,9},{9,8},{10,11... | collective-permute-start | bytes 3145736 | tf_op jit(solution)/shard_map/ppermute | solution.py:88
  5.0 25.2 %collective-permute-start = (f32[256,1024]{1,0:T(8,128)S(1)}, f32[256,1024]{1,0:T(8,128)S(1)}, u32[]{:S(2)}, u32[]{:S(2)}) collective-permute-start(f32[256,1024]{1,0:T(8,128)S(1)} %get-tuple-element.24.refs_1_.refs_2_.refs_0_.refs_10_), channel_id=1, source_target_pairs={{0,8},{8,0},{16,24},{24,16},{1,9},{9,1},{17,25},{25,17},{2,10},{10... | collective-permute-start | bytes 3145736 | tf_op jit(solution)/shard_map/ppermute | solution.py:88
  6.1 1.0 copy-start.3
  6.1 2.0 %copy-start.6 = (f32[256,2048]{1,0:T(8,128)S(1)}, f32[256,2048]{1,0:T(8,128)}, u32[]{:S(2)}) copy-start(f32[256,2048]{1,0:T(8,128)} %refs_0_.5) | copy-start | bytes 6291460
  7.1 45.7 %collective-permute-start.5 = (f32[256,1536]{1,0:T(8,128)S(1)}, f32[256,1536]{1,0:T(8,128)S(1)}, u32[]{:S(2)}, u32[]{:S(2)}) collective-permute-start(f32[256,1536]{1,0:T(8,128)S(1)} %get-tuple-element.27.refs_2_), channel_id=1, source_target_pairs={{0,8},{8,0},{16,24},{24,16},{1,9},{9,1},{17,25},{25,17},{2,10},{10... | collective-permute-start | bytes 4718600 | tf_op jit(solution)/shard_map/ppermute | solution.py:88
  7.6 44.4 %collective-permute-start.6 = (f32[256,1024]{1,0:T(8,128)S(1)}, f32[256,1024]{1,0:T(8,128)S(1)}, u32[]{:S(2)}, u32[]{:S(2)}) collective-permute-start(f32[256,1024]{1,0:T(8,128)S(1)} %get-tuple-element.31), channel_id=1, source_target_pairs={{0,1},{1,0},{2,3},{3,2},{4,5},{5,4},{6,7},{7,6},{8,9},{9,8},{10,11... | collective-permute-start | bytes 3145736 | tf_op jit(solution)/shard_map/ppermute | solution.py:88
  29.5 9.4 %copy-start.1 = (f32[256,1024]{1,0:T(8,128)}, f32[256,1024]{1,0:T(8,128)S(1)}, u32[]{:S(2)}) copy-start(f32[256,1024]{1,0:T(8,128)S(1)} %collective-permute-done.1.refs_4_.refs_5_.refs_12_) | copy-start | bytes 3145732
  29.6 2.1 %collective-permute-start.3 = (f32[128,1024]{1,0:T(8,128)S(1)}, f32[128,1024]{1,0:T(8,128)S(1)}, u32[]{:S(2)}, u32[]{:S(2)}) collective-permute-start(f32[128,1024]{1,0:T(8,128)S(1)} %get-tuple-element.49), channel_id=1, source_target_pairs={{0,8},{8,0},{16,24},{24,16},{1,9},{9,1},{17,25},{25,17},{2,10},{10... | collective-permute-start | bytes 1572872 | tf_op jit(solution)/shard_map/ppermute | solution.py:88
  29.7 2.6 %collective-permute-start.2 = (f32[128,1024]{1,0:T(8,128)S(1)}, f32[128,1024]{1,0:T(8,128)S(1)}, u32[]{:S(2)}, u32[]{:S(2)}) collective-permute-start(f32[128,1024]{1,0:T(8,128)S(1)} %get-tuple-element.50), channel_id=1, source_target_pairs={{0,8},{8,0},{16,24},{24,16},{1,9},{9,1},{17,25},{25,17},{2,10},{10... | collective-permute-start | bytes 1572872 | tf_op jit(solution)/shard_map/ppermute | solution.py:88
  30.2 33.2 %copy-start.2 = (f32[256,1024]{1,0:T(8,128)}, f32[256,1024]{1,0:T(8,128)S(1)}, u32[]{:S(2)}) copy-start(f32[256,1024]{1,0:T(8,128)S(1)} %collective-permute-done.refs_2_.refs_3_.refs_11_) | copy-start | bytes 3145732
  30.2 43.1 %collective-permute-start.11 = (f32[512,512]{1,0:T(8,128)S(1)}, f32[512,512]{1,0:T(8,128)S(1)}, u32[]{:S(2)}, u32[]{:S(2)}) collective-permute-start(f32[512,512]{1,0:T(8,128)S(1)} %get-tuple-element.34), channel_id=1, source_target_pairs={{0,1},{1,0},{2,3},{3,2},{4,5},{5,4},{6,7},{7,6},{8,9},{9,8},{10,11... | collective-permute-start | bytes 3145736 | tf_op jit(solution)/shard_map/ppermute | solution.py:88
  39.0 20.7 %collective-permute-start.4 = (f32[1,4,192,256]{3,2,1,0:T(8,128)S(1)}, f32[1,4,192,256]{3,2,1,0:T(8,128)S(1)}, u32[]{:S(2)}, u32[]{:S(2)}) collective-permute-start(f32[1,4,192,256]{3,2,1,0:T(8,128)S(1)} %get-tuple-element.30), channel_id=1, source_target_pairs={{0,16},{8,24},{16,0},{24,8},{1,17},{9,25},{17,1},{25,9},{2,18},{10... | collective-permute-start | bytes 2359304 | tf_op jit(solution)/shard_map/ppermute | solution.py:88
  52.0 2.8 %copy-start.9 = (f32[256,1024]{1,0:T(8,128)}, f32[256,1024]{1,0:T(8,128)S(1)}, u32[]{:S(2)}) copy-start(f32[256,1024]{1,0:T(8,128)S(1)} %collective-permute-done.6.refs_12_) | copy-start | bytes 3145732
  52.0 2.7 %collective-permute-start.7 = (f32[96,1024]{1,0:T(8,128)S(1)}, f32[96,1024]{1,0:T(8,128)S(1)}, u32[]{:S(2)}, u32[]{:S(2)}) collective-permute-start(f32[96,1024]{1,0:T(8,128)S(1)} %slice.29), channel_id=1, source_target_pairs={{0,8},{8,0},{16,24},{24,16},{1,9},{9,1},{17,25},{25,17},{2,10},{10... | collective-permute-start | bytes 1179656 | tf_op jit(solution)/shard_map/ppermute | solution.py:88
  52.2 2.1 %collective-permute-start.9 = (f32[80,1024]{1,0:T(8,128)S(1)}, f32[80,1024]{1,0:T(8,128)S(1)}, u32[]{:S(2)}, u32[]{:S(2)}) collective-permute-start(f32[80,1024]{1,0:T(8,128)S(1)} %get-tuple-element.47), channel_id=1, source_target_pairs={{0,8},{8,0},{16,24},{24,16},{1,9},{9,1},{17,25},{25,17},{2,10},{10... | collective-permute-start | bytes 983048 | tf_op jit(solution)/shard_map/ppermute | solution.py:88
  52.7 2.0 %copy-start.8 = (f32[256,1536]{1,0:T(8,128)}, f32[256,1536]{1,0:T(8,128)S(1)}, u32[]{:S(2)}) copy-start(f32[256,1536]{1,0:T(8,128)S(1)} %collective-permute-done.5.refs_11_.refs_2_.refs_3_) | copy-start | bytes 4718596
  52.7 2.0 %collective-permute-start.8 = (f32[80,1024]{1,0:T(8,128)S(1)}, f32[80,1024]{1,0:T(8,128)S(1)}, u32[]{:S(2)}, u32[]{:S(2)}) collective-permute-start(f32[80,1024]{1,0:T(8,128)S(1)} %get-tuple-element.48), channel_id=1, source_target_pairs={{0,8},{8,0},{16,24},{24,16},{1,9},{9,1},{17,25},{25,17},{2,10},{10... | collective-permute-start | bytes 983048 | tf_op jit(solution)/shard_map/ppermute | solution.py:88
  59.5 14.7 %collective-permute-start.14 = (f32[1,2,256,256]{3,2,1,0:T(8,128)S(1)}, f32[1,2,256,256]{3,2,1,0:T(8,128)S(1)}, u32[]{:S(2)}, u32[]{:S(2)}) collective-permute-start(f32[1,2,256,256]{3,2,1,0:T(8,128)S(1)} %get-tuple-element.37), channel_id=1, source_target_pairs={{0,16},{8,24},{16,0},{24,8},{1,17},{9,25},{17,1},{25,9},{2,18},{10... | collective-permute-start | bytes 1572872 | tf_op jit(solution)/shard_map/ppermute | solution.py:88
  61.3 21.7 %collective-permute-start.10 = (f32[1,2,192,256]{3,2,1,0:T(8,128)S(1)}, f32[1,2,192,256]{3,2,1,0:T(8,128)S(1)}, u32[]{:S(2)}, u32[]{:S(2)}) collective-permute-start(f32[1,2,192,256]{3,2,1,0:T(8,128)S(1)} %halve.10.refs_16_), channel_id=1, source_target_pairs={{0,2},{1,3},{2,0},{3,1},{4,6},{5,7},{6,4},{7,5},{8,10},{9,11},{10,... | collective-permute-start | bytes 1179656 | tf_op jit(solution)/shard_map/ppermute | solution.py:88
  73.4 1.6 %collective-permute-start.13 = (f32[128,512]{1,0:T(8,128)S(1)}, f32[128,512]{1,0:T(8,128)S(1)}, u32[]{:S(2)}, u32[]{:S(2)}) collective-permute-start(f32[128,512]{1,0:T(8,128)S(1)} %get-tuple-element.45), channel_id=1, source_target_pairs={{0,8},{8,0},{16,24},{24,16},{1,9},{9,1},{17,25},{25,17},{2,10},{10... | collective-permute-start | bytes 786440 | tf_op jit(solution)/shard_map/ppermute | solution.py:88
  73.4 1.9 %collective-permute-start.12 = (f32[128,512]{1,0:T(8,128)S(1)}, f32[128,512]{1,0:T(8,128)S(1)}, u32[]{:S(2)}, u32[]{:S(2)}) collective-permute-start(f32[128,512]{1,0:T(8,128)S(1)} %get-tuple-element.46), channel_id=1, source_target_pairs={{0,8},{8,0},{16,24},{24,16},{1,9},{9,1},{17,25},{25,17},{2,10},{10... | collective-permute-start | bytes 786440 | tf_op jit(solution)/shard_map/ppermute | solution.py:88
  73.9 14.8 %collective-permute-start.16 = (f32[1,2,256,256]{3,2,1,0:T(8,128)S(1)}, f32[1,2,256,256]{3,2,1,0:T(8,128)S(1)}, u32[]{:S(2)}, u32[]{:S(2)}) collective-permute-start(f32[1,2,256,256]{3,2,1,0:T(8,128)S(1)} %get-tuple-element.39), channel_id=1, source_target_pairs={{0,16},{8,24},{16,0},{24,8},{1,17},{9,25},{17,1},{25,9},{2,18},{10... | collective-permute-start | bytes 1572872 | tf_op jit(solution)/shard_map/ppermute | solution.py:88
  82.3 23.5 %collective-permute-start.18 = (f32[1,4,128,256]{3,2,1,0:T(8,128)S(1)}, f32[1,4,128,256]{3,2,1,0:T(8,128)S(1)}, u32[]{:S(2)}, u32[]{:S(2)}) collective-permute-start(f32[1,4,128,256]{3,2,1,0:T(8,128)S(1)} %get-tuple-element.41), channel_id=1, source_target_pairs={{0,16},{8,24},{16,0},{24,8},{1,17},{9,25},{17,1},{25,9},{2,18},{10... | collective-permute-start | bytes 1572872 | tf_op jit(solution)/shard_map/ppermute | solution.py:88
  84.4 12.9 %collective-permute-start.15 = (f32[1,1,192,256]{3,2,1,0:T(8,128)S(1)}, f32[1,1,192,256]{3,2,1,0:T(8,128)S(1)}, u32[]{:S(2)}, u32[]{:S(2)}) collective-permute-start(f32[1,1,192,256]{3,2,1,0:T(8,128)S(1)} %halve.11.refs_4_), channel_id=1, source_target_pairs={{0,4},{1,5},{2,6},{3,7},{4,0},{5,1},{6,2},{7,3},{8,12},{9,13},{10,... | collective-permute-start | bytes 589832 | tf_op jit(solution)/shard_map/ppermute | solution.py:88
  89.7 22.4 %collective-permute-start.20 = (f32[1,2,256,256]{3,2,1,0:T(8,128)S(1)}, f32[1,2,256,256]{3,2,1,0:T(8,128)S(1)}, u32[]{:S(2)}, u32[]{:S(2)}) collective-permute-start(f32[1,2,256,256]{3,2,1,0:T(8,128)S(1)} %halve.12.refs_16_), channel_id=1, source_target_pairs={{0,2},{1,3},{2,0},{3,1},{4,6},{5,7},{6,4},{7,5},{8,10},{9,11},{10,... | collective-permute-start | bytes 1572872 | tf_op jit(solution)/shard_map/ppermute | solution.py:88
  96.7 2.3 %copy-start.4 = (f32[256,1024]{1,0:T(8,128)S(1)}, f32[256,1024]{1,0:T(8,128)}, u32[]{:S(2)}) copy-start(f32[256,1024]{1,0:T(8,128)} %copy-done.3) | copy-start | bytes 3145732
  96.7 17.9 %collective-permute-start.22 = (f32[1,4,128,256]{3,2,1,0:T(8,128)S(1)}, f32[1,4,128,256]{3,2,1,0:T(8,128)S(1)}, u32[]{:S(2)}, u32[]{:S(2)}) collective-permute-start(f32[1,4,128,256]{3,2,1,0:T(8,128)S(1)} %get-tuple-element.43), channel_id=1, source_target_pairs={{0,16},{8,24},{16,0},{24,8},{1,17},{9,25},{17,1},{25,9},{2,18},{10... | collective-permute-start | bytes 1572872 | tf_op jit(solution)/shard_map/ppermute | solution.py:88
  104.2 20.5 %collective-permute-start.24 = (f32[1,4,128,256]{3,2,1,0:T(8,128)S(1)}, f32[1,4,128,256]{3,2,1,0:T(8,128)S(1)}, u32[]{:S(2)}, u32[]{:S(2)}) collective-permute-start(f32[1,4,128,256]{3,2,1,0:T(8,128)S(1)} %get-tuple-element.44), channel_id=1, source_target_pairs={{0,16},{8,24},{16,0},{24,8},{1,17},{9,25},{17,1},{25,9},{2,18},{10... | collective-permute-start | bytes 1572872 | tf_op jit(solution)/shard_map/ppermute | solution.py:88
  107.1 6.4 %collective-permute-start.19 = (f32[1,2,128,256]{3,2,1,0:T(8,128)S(1)}, f32[1,2,128,256]{3,2,1,0:T(8,128)S(1)}, u32[]{:S(2)}, u32[]{:S(2)}) collective-permute-start(f32[1,2,128,256]{3,2,1,0:T(8,128)S(1)} %halve.13.refs_5_), channel_id=1, source_target_pairs={{0,2},{1,3},{2,0},{3,1},{4,6},{5,7},{6,4},{7,5},{8,10},{9,11},{10,... | collective-permute-start | bytes 786440 | tf_op jit(solution)/shard_map/ppermute | solution.py:88
  107.6 17.1 %collective-permute-start.17 = (f32[128,256]{1,0:T(8,128)S(1)}, f32[128,256]{1,0:T(8,128)S(1)}, u32[]{:S(2)}, u32[]{:S(2)}) collective-permute-start(f32[128,256]{1,0:T(8,128)S(1)} %slice.35), channel_id=1, source_target_pairs={{2,8},{3,9},{4,16},{5,17},{6,24},{7,25},{8,2},{9,3},{12,18},{13,19... | collective-permute-start | bytes 393224 | tf_op jit(solution)/shard_map/ppermute | solution.py:521
  112.8 15.2 %collective-permute-start.25 = (f32[1,1,256,256]{3,2,1,0:T(8,128)S(1)}, f32[1,1,256,256]{3,2,1,0:T(8,128)S(1)}, u32[]{:S(2)}, u32[]{:S(2)}) collective-permute-start(f32[1,1,256,256]{3,2,1,0:T(8,128)S(1)} %halve.14.refs_3_), channel_id=1, source_target_pairs={{0,4},{1,5},{2,6},{3,7},{4,0},{5,1},{6,2},{7,3},{8,12},{9,13},{10,... | collective-permute-start | bytes 786440 | tf_op jit(solution)/shard_map/ppermute | solution.py:88
  115.9 13.9 %collective-permute-start.23 = (f32[1,2,128,256]{3,2,1,0:T(8,128)S(1)}, f32[1,2,128,256]{3,2,1,0:T(8,128)S(1)}, u32[]{:S(2)}, u32[]{:S(2)}) collective-permute-start(f32[1,2,128,256]{3,2,1,0:T(8,128)S(1)} %halve.16.refs_2_), channel_id=1, source_target_pairs={{0,2},{1,3},{2,0},{3,1},{4,6},{5,7},{6,4},{7,5},{8,10},{9,11},{10,... | collective-permute-start | bytes 786440 | tf_op jit(solution)/shard_map/ppermute | solution.py:88
  126.0 15.8 %collective-permute-start.27 = (f32[1,2,128,256]{3,2,1,0:T(8,128)S(1)}, f32[1,2,128,256]{3,2,1,0:T(8,128)S(1)}, u32[]{:S(2)}, u32[]{:S(2)}) collective-permute-start(f32[1,2,128,256]{3,2,1,0:T(8,128)S(1)} %halve.17.refs_3_), channel_id=1, source_target_pairs={{0,2},{1,3},{2,0},{3,1},{4,6},{5,7},{6,4},{7,5},{8,10},{9,11},{10,... | collective-permute-start | bytes 786440 | tf_op jit(solution)/shard_map/ppermute | solution.py:88
  127.3 13.1 %collective-permute-start.21 = (f32[1,1,128,256]{3,2,1,0:T(8,128)S(1)}, f32[1,1,128,256]{3,2,1,0:T(8,128)S(1)}, u32[]{:S(2)}, u32[]{:S(2)}) collective-permute-start(f32[1,1,128,256]{3,2,1,0:T(8,128)S(1)} %halve.15.refs_2_), channel_id=1, source_target_pairs={{0,4},{1,5},{2,6},{3,7},{4,0},{5,1},{6,2},{7,3},{8,12},{9,13},{10,... | collective-permute-start | bytes 393224 | tf_op jit(solution)/shard_map/ppermute | solution.py:88
  131.0 24.7 %collective-permute-start.28 = (f32[1,1,128,256]{3,2,1,0:T(8,128)S(1)}, f32[1,1,128,256]{3,2,1,0:T(8,128)S(1)}, u32[]{:S(2)}, u32[]{:S(2)}) collective-permute-start(f32[1,1,128,256]{3,2,1,0:T(8,128)S(1)} %halve.18.refs_4_), channel_id=1, source_target_pairs={{0,4},{1,5},{2,6},{3,7},{4,0},{5,1},{6,2},{7,3},{8,12},{9,13},{10,... | collective-permute-start | bytes 393224 | tf_op jit(solution)/shard_map/ppermute | solution.py:88
  141.7 12.4 %collective-permute-start.26 = (f32[128,256]{1,0:T(8,128)S(1)}, f32[128,256]{1,0:T(8,128)S(1)}, u32[]{:S(2)}, u32[]{:S(2)}) collective-permute-start(f32[128,256]{1,0:T(8,128)S(1)} %finish.3.refs_3_.refs_2_), channel_id=1, source_target_pairs={{0,1},{1,0},{2,9},{3,8},{4,17},{5,16},{6,25},{7,24},{8,3},{9,2},{1... | collective-permute-start | bytes 393224 | tf_op jit(solution)/shard_map/ppermute | solution.py:541
  142.9 12.7 %collective-permute-start.29 = (f32[1,1,128,256]{3,2,1,0:T(8,128)S(1)}, f32[1,1,128,256]{3,2,1,0:T(8,128)S(1)}, u32[]{:S(2)}, u32[]{:S(2)}) collective-permute-start(f32[1,1,128,256]{3,2,1,0:T(8,128)S(1)} %halve.19.refs_4_), channel_id=1, source_target_pairs={{0,4},{1,5},{2,6},{3,7},{4,0},{5,1},{6,2},{7,3},{8,12},{9,13},{10,... | collective-permute-start | bytes 393224 | tf_op jit(solution)/shard_map/ppermute | solution.py:88

commit v6 on v4

--- a/solution.py
+++ b/solution.py
@@ -257,6 +257,17 @@
         return n0 >> len(xs), (n1 * len(arrays)) >> len(zs)
 
 
+class Arriving:
+    def __init__(self, values, waits):
+        self.values, self.waits = values, waits
+
+    def __getitem__(self, k):
+        for copy in self.waits[k]:
+            copy.wait()
+        self.waits[k] = []
+        return self.values[k]
+
+
 def gather(dev, body, name, sums, pick, arrays_in, out_shapes):
     arrays, slots, shapes = [], [], []
     for total in sums:
@@ -278,6 +289,7 @@
         buffers, sems = refs[:-1], refs[-1]
         waits, k = [], 0
         for total in sums:
+            waits.append([])
             for _, xs, zs, row in total.terms:
                 n0, n1, rows, _ = shapes[k]
                 xs = [at[bit] for bit in xs]
@@ -306,15 +318,13 @@
                         else:
                             for parity in range(2):
                                 pl.when(zi % 2 == parity)(copies[parity].start)
-                        waits.append(copies[0])
+                        waits[-1].append(copies[0])
                 k += 1
-        for copy in waits:
-            copy.wait()
         values, k = [], 0
         for total in sums:
             values.append(buffers[k : k + len(total.terms)])
             k += len(total.terms)
-        body(at, values, inputs, outs)
+        body(at, Arriving(values, waits), inputs, outs)
 
     most = max(shape[0] * shape[1] for shape in shapes)
     return dev.call(

time: 160 us -> 160 us (level)
  no operation moved by 1% of the time
where the time goes in v6:
time: 160 us; the launch traced here: 159 us
  Pallas kernels  69.7 us (44%)
  waiting for transfers between devices  52.5 us (33%)
  starting transfers between devices  33.5 us (21%)
  local copies, waits for them, and re-layouts  2.11 us (1%)
    pallas_call x24, Pallas kernels, call(): pl.pallas_call(ordered, name=name, out_shape=[jax.ShapeDtypeStruct(s, jnp...  69.7 us
    ppermute x28, waiting for transfers between devices, flip(): return lax.ppermute(value, axis, [(i, i ^ mask) for i in range(count)])  35.1 us
    ppermute x28, starting transfers between devices, flip(): return lax.ppermute(value, axis, [(i, i ^ mask) for i in range(count)])  28.9 us
    ppermute x1, waiting for transfers between devices, local(): mixed_half = lax.ppermute(mixed, ('row', 'col'), mixed_pairs)  9.77 us
    ppermute x1, waiting for transfers between devices, local(): same_half = lax.ppermute(same[:half], ('row', 'col'), same_pairs)  7.59 us
    ppermute x1, starting transfers between devices, local(): same_half = lax.ppermute(same[:half], ('row', 'col'), same_pairs)  4.47 us
  transfers between devices with their start and end apart: 30, of which 13 were waited for; matrix products, arithmetic and copies ran while one was open for 0% of the time, Pallas kernels for 41%

profile of v6, /device:TPU:2, one launch (start us, length us, event | category | flops | bytes accessed | tf_op | source)
XLA Modules:
  0.0 158.9 jit_solution(6664096694200260246)
XLA Ops:
  0.7 1.6 %copy-done.5 = f32[256,2048]{1,0:T(8,128)S(1)} copy-done((f32[256,2048]{1,0:T(8,128)S(1)}, f32[256,2048]{1,0:T(8,128)}, u32[]{:S(2)}) %copy-start.5) | copy-done | bytes 2097176
  2.3 1.1 part_orbitals.1
  3.4 1.6 collective-permute-start.1
  5.0 1.1 part_images.1
  6.1 0.8 part_cores.1
  8.1 13.7 %rotate.1.refs_15_ = f32[256,2048]{1,0:T(8,128)} custom-call(s32[7]{0:T(128)S(1)} %stack.31.at, f32[256,2048]{1,0:T(8,128)S(1)} %copy-done.6, f32[2048,2048]{1,0:T(8,128)} %refs_1_.1, f32[256,1536]{1,0:T(8,128)S(1)} %get-tuple-element.27.refs_2_), custom_call_target="tpu_custom_call" | custom-call | tf_op jit(solution)/shard_map/rotate/pallas_call | solution.py:61
  21.8 7.8 %collective-permute-done.1.refs_4_.refs_5_.refs_12_ = f32[256,1024]{1,0:T(8,128)S(1)} collective-permute-done((f32[256,1024]{1,0:T(8,128)S(1)}, f32[256,1024]{1,0:T(8,128)S(1)}, u32[]{:S(2)}, u32[]{:S(2)}) %collective-permute-start.1) | collective-permute-done | bytes 1048608 | tf_op jit(solution)/shard_map/ppermute | solution.py:81
  30.2 1.5 collective-permute-start.11
  32.4 6.6 %overlap_same.1 = (f32[1,4,192,256]{3,2,1,0:T(8,128)S(1)}, f32[1,4,192,256]{3,2,1,0:T(8,128)S(1)}) custom-call(s32[7]{0:T(128)S(1)} %stack.31.at, f32[256,1024]{1,0:T(8,128)S(1)} %get-tuple-element.24.refs_1_.refs_2_.refs_0_.refs_10_, f32[256,1024]{1,0:T(8,128)S(1)} %get-tuple-element.24.refs_1_.refs_2_.refs_0_.refs_10_, ...), custom_call_target="tpu_custom_call" | custom-call | tf_op jit(solution)/shard_map/overlap_same/pallas_call | solution.py:61
  39.1 12.9 %collective-permute-done.6.refs_12_ = f32[256,1024]{1,0:T(8,128)S(1)} collective-permute-done((f32[256,1024]{1,0:T(8,128)S(1)}, f32[256,1024]{1,0:T(8,128)S(1)}, u32[]{:S(2)}, u32[]{:S(2)}) %collective-permute-start.6) | collective-permute-done | bytes 1048608 | tf_op jit(solution)/shard_map/ppermute | solution.py:81
  52.8 1.5 collective-permute-done.9.refs_15_
  54.8 4.8 %project.4 = (f32[1,2,256,256]{3,2,1,0:T(8,128)S(1)}, f32[1,2,256,256]{3,2,1,0:T(8,128)S(1)}) custom-call(s32[7]{0:T(128)S(1)} %stack.31.at, f32[256,1024]{1,0:T(8,128)S(1)} %get-tuple-element.24.refs_1_.refs_2_.refs_0_.refs_10_, f32[256,1024]{1,0:T(8,128)S(1)} %get-tuple-element.24.refs_1_.refs_2_.refs_0_.refs_10_, ...), custom_call_target="tpu_custom_call" | custom-call | tf_op jit(solution)/shard_map/project/pallas_call | solution.py:61
  59.7 1.6 %halve.10.refs_16_ = f32[1,2,192,256]{3,2,1,0:T(8,128)S(1)} custom-call(s32[7]{0:T(128)S(1)} %stack.31.at, f32[1,4,192,256]{3,2,1,0:T(8,128)S(1)} %get-tuple-element.29.refs_16_.refs_0_, f32[1,4,192,256]{3,2,1,0:T(8,128)S(1)} %collective-permute-done.4.refs_1_, f32[1,2,256,256]{3,2,1,0:T(8,128)S(1)} %get-tuple-element.33.refs_2_.refs_0_), custom_call_target="tpu_custom_call" | custom-call | tf_op jit(solution)/shard_map/halve/pallas_call | solution.py:61
  61.3 2.1 %collective-permute-start.10 = (f32[1,2,192,256]{3,2,1,0:T(8,128)S(1)}, f32[1,2,192,256]{3,2,1,0:T(8,128)S(1)}, u32[]{:S(2)}, u32[]{:S(2)}) collective-permute-start(f32[1,2,192,256]{3,2,1,0:T(8,128)S(1)} %halve.10.refs_16_), channel_id=1, source_target_pairs={{0,2},{1,3},{2,0},{3,1},{4,6},{5,7},{6,4},{7,5},{8,10},{9,11},{10,... | collective-permute-start | bytes 1179656 | tf_op jit(solution)/shard_map/ppermute | solution.py:81
  63.4 4.8 %project.5 = (f32[1,2,256,256]{3,2,1,0:T(8,128)S(1)}, f32[1,2,256,256]{3,2,1,0:T(8,128)S(1)}) custom-call(s32[7]{0:T(128)S(1)} %stack.31.at, f32[256,1024]{1,0:T(8,128)S(1)} %get-tuple-element.24.refs_1_.refs_2_.refs_0_.refs_10_, f32[256,1024]{1,0:T(8,128)S(1)} %get-tuple-element.24.refs_1_.refs_2_.refs_0_.refs_10_, ...), custom_call_target="tpu_custom_call" | custom-call | tf_op jit(solution)/shard_map/project/pallas_call | solution.py:61
  68.2 5.1 %collective-permute-done.11.refs_4_.refs_5_ = f32[512,512]{1,0:T(8,128)S(1)} collective-permute-done((f32[512,512]{1,0:T(8,128)S(1)}, f32[512,512]{1,0:T(8,128)S(1)}, u32[]{:S(2)}, u32[]{:S(2)}) %collective-permute-start.11) | collective-permute-done | bytes 1048608 | tf_op jit(solution)/shard_map/ppermute | solution.py:81
  74.3 0.7 collective-permute-done.13.refs_8_.refs_9_
  75.3 7.0 %overlap_mixed.1 = (f32[1,4,128,256]{3,2,1,0:T(8,128)S(1)}, f32[1,4,128,256]{3,2,1,0:T(8,128)S(1)}) custom-call(s32[7]{0:T(128)S(1)} %stack.31.at, f32[256,1024]{1,0:T(8,128)S(1)} %get-tuple-element.25.refs_1_.refs_0_, f32[256,1024]{1,0:T(8,128)S(1)} %get-tuple-element.25.refs_1_.refs_0_, f32[256,1536]{1,0:T(8,128)} %copy-done.8, f32[256,1536]{1,0:T(8,128)} %copy-done.8, ...), custom_call_target="tpu_custom_call" | custom-call | tf_op jit(solution)/shard_map/overlap_mixed/pallas_call | solution.py:61
  82.3 0.7 collective-permute-start.18
  83.0 1.4 halve.11.refs_4_
  84.4 2.7 %collective-permute-start.15 = (f32[1,1,192,256]{3,2,1,0:T(8,128)S(1)}, f32[1,1,192,256]{3,2,1,0:T(8,128)S(1)}, u32[]{:S(2)}, u32[]{:S(2)}) collective-permute-start(f32[1,1,192,256]{3,2,1,0:T(8,128)S(1)} %halve.11.refs_4_), channel_id=1, source_target_pairs={{0,4},{1,5},{2,6},{3,7},{4,0},{5,1},{6,2},{7,3},{8,12},{9,13},{10,... | collective-permute-start | bytes 589832 | tf_op jit(solution)/shard_map/ppermute | solution.py:81
  87.1 1.7 %collective-permute-done.16.refs_3_ = f32[1,2,256,256]{3,2,1,0:T(8,128)S(1)} collective-permute-done((f32[1,2,256,256]{3,2,1,0:T(8,128)S(1)}, f32[1,2,256,256]{3,2,1,0:T(8,128)S(1)}, u32[]{:S(2)}, u32[]{:S(2)}) %collective-permute-start.16) | collective-permute-done | bytes 524320 | tf_op jit(solution)/shard_map/ppermute | solution.py:81
  88.7 1.0 halve.12.refs_16_
  89.7 1.6 %collective-permute-start.20 = (f32[1,2,256,256]{3,2,1,0:T(8,128)S(1)}, f32[1,2,256,256]{3,2,1,0:T(8,128)S(1)}, u32[]{:S(2)}, u32[]{:S(2)}) collective-permute-start(f32[1,2,256,256]{3,2,1,0:T(8,128)S(1)} %halve.12.refs_16_), channel_id=1, source_target_pairs={{0,2},{1,3},{2,0},{3,1},{4,6},{5,7},{6,4},{7,5},{8,10},{9,11},{10,... | collective-permute-start | bytes 1572872 | tf_op jit(solution)/shard_map/ppermute | solution.py:81
  91.3 5.4 %project.6 = (f32[1,4,128,256]{3,2,1,0:T(8,128)S(1)}, f32[1,4,128,256]{3,2,1,0:T(8,128)S(1)}) custom-call(s32[7]{0:T(128)S(1)} %stack.31.at, f32[256,1024]{1,0:T(8,128)S(1)} %get-tuple-element.25.refs_1_.refs_0_, f32[256,1024]{1,0:T(8,128)S(1)} %get-tuple-element.25.refs_1_.refs_0_, f32[256,1536]{1,0:T(8,128)} %copy-done.8, f32[256,1536]{1,0:T(8,128)} %copy-done.8, ...), custom_call_target="tpu_custom_call" | custom-call | tf_op jit(solution)/shard_map/project/pallas_call | solution.py:61
  97.3 1.6 %finish.2.refs_16_.refs_0_ = f32[192,256]{1,0:T(8,128)S(1)} custom-call(s32[7]{0:T(128)S(1)} %stack.31.at, f32[1,4,192,256]{3,2,1,0:T(8,128)S(1)} %get-tuple-element.29.refs_16_.refs_0_, f32[1,4,192,256]{3,2,1,0:T(8,128)S(1)} %collective-permute-done.4.refs_1_, f32[1,2,192,256]{3,2,1,0:T(8,128)S(1)} %collective-permute-done.10.refs_2_, ...), custom_call_target="tpu_custom_call" | custom-call | tf_op jit(solution)/shard_map/finish/pallas_call | solution.py:61
  99.0 5.2 %project.7 = (f32[1,4,128,256]{3,2,1,0:T(8,128)S(1)}, f32[1,4,128,256]{3,2,1,0:T(8,128)S(1)}) custom-call(s32[7]{0:T(128)S(1)} %stack.31.at, f32[256,1024]{1,0:T(8,128)S(1)} %get-tuple-element.25.refs_1_.refs_0_, f32[256,1024]{1,0:T(8,128)S(1)} %get-tuple-element.25.refs_1_.refs_0_, f32[256,1536]{1,0:T(8,128)} %copy-done.8, f32[256,1536]{1,0:T(8,128)} %copy-done.8, ...), custom_call_target="tpu_custom_call" | custom-call | tf_op jit(solution)/shard_map/project/pallas_call | solution.py:61
  104.2 1.6 collective-permute-start.24
  105.8 1.3 halve.13.refs_5_
  107.6 4.5 %collective-permute-start.17 = (f32[128,256]{1,0:T(8,128)S(1)}, f32[128,256]{1,0:T(8,128)S(1)}, u32[]{:S(2)}, u32[]{:S(2)}) collective-permute-start(f32[128,256]{1,0:T(8,128)S(1)} %slice.35), channel_id=1, source_target_pairs={{2,8},{3,9},{4,16},{5,17},{6,24},{7,25},{8,2},{9,3},{12,18},{13,19... | collective-permute-start | bytes 393224 | tf_op jit(solution)/shard_map/ppermute | solution.py:522
  112.1 0.7 halve.14.refs_3_
  112.9 0.6 collective-permute-done.19.refs_2_
  113.5 1.1 halve.15.refs_2_
  114.6 1.3 halve.16.refs_2_
  116.0 1.2 collective-permute-start.23
  117.1 7.6 %collective-permute-done.17.refs_3_.refs_1_ = f32[128,256]{1,0:T(8,128)S(1)} collective-permute-done((f32[128,256]{1,0:T(8,128)S(1)}, f32[128,256]{1,0:T(8,128)S(1)}, u32[]{:S(2)}, u32[]{:S(2)}) %collective-permute-start.17) | collective-permute-done | bytes 131104 | tf_op jit(solution)/shard_map/ppermute | solution.py:522
  124.7 1.3 halve.17.refs_3_
  126.0 1.3 collective-permute-start.27
  127.3 0.6 collective-permute-start.21
  128.0 3.3 %collective-permute-done.23.refs_2_.refs_8_ = f32[1,2,128,256]{3,2,1,0:T(8,128)S(1)} collective-permute-done((f32[1,2,128,256]{3,2,1,0:T(8,128)S(1)}, f32[1,2,128,256]{3,2,1,0:T(8,128)S(1)}, u32[]{:S(2)}, u32[]{:S(2)}) %collective-permute-start.23) | collective-permute-done | bytes 262176 | tf_op jit(solution)/shard_map/ppermute | solution.py:81
  131.3 1.1 halve.18.refs_4_
  132.4 8.1 %collective-permute-start.28 = (f32[1,1,128,256]{3,2,1,0:T(8,128)S(1)}, f32[1,1,128,256]{3,2,1,0:T(8,128)S(1)}, u32[]{:S(2)}, u32[]{:S(2)}) collective-permute-start(f32[1,1,128,256]{3,2,1,0:T(8,128)S(1)} %halve.18.refs_4_), channel_id=1, source_target_pairs={{0,4},{1,5},{2,6},{3,7},{4,0},{5,1},{6,2},{7,3},{8,12},{9,13},{10,... | collective-permute-start | bytes 393224 | tf_op jit(solution)/shard_map/ppermute | solution.py:81
  140.5 1.3 finish.3.refs_3_.refs_2_
  141.9 1.1 halve.19.refs_4_
  143.0 1.4 collective-permute-start.29
  144.4 9.8 %collective-permute-done.26.refs_3_ = f32[128,256]{1,0:T(8,128)S(1)} collective-permute-done((f32[128,256]{1,0:T(8,128)S(1)}, f32[128,256]{1,0:T(8,128)S(1)}, u32[]{:S(2)}, u32[]{:S(2)}) %collective-permute-start.26) | collective-permute-done | bytes 131104 | tf_op jit(solution)/shard_map/ppermute | solution.py:542
  154.2 1.5 assemble_overlap.1.refs_14_
  155.7 3.1 %assemble.1 = f32[512,256]{1,0:T(8,128)} custom-call(s32[7]{0:T(128)S(1)} %stack.31.at, f32[1,2,256,256]{3,2,1,0:T(8,128)S(1)} %get-tuple-element.33.refs_2_.refs_0_, f32[1,2,256,256]{3,2,1,0:T(8,128)S(1)} %get-tuple-element.35.refs_15_.refs_1_, f32[1,2,256,256]{3,2,1,0:T(8,128)S(1)} %collective-permute-done.14.refs_16_.refs_2_, ...), custom_call_target="tpu_custom_call" | custom-call | tf_op jit(solution)/shard_map/assemble/pallas_call | solution.py:61
  (62 shorter events, 6.6 us)
Async XLA Ops:
  0.7 1.6 %copy-start.5 = (f32[256,2048]{1,0:T(8,128)S(1)}, f32[256,2048]{1,0:T(8,128)}, u32[]{:S(2)}) copy-start(f32[256,2048]{1,0:T(8,128)} %refs_0_.5) | copy-start | bytes 6291460
  2.3 2.7 %copy-start.7 = (f32[256,2048]{1,0:T(8,128)S(1)}, f32[256,2048]{1,0:T(8,128)}, u32[]{:S(2)}) copy-start(f32[256,2048]{1,0:T(8,128)} %refs_0_.4) | copy-start | bytes 6291460
  3.4 60.0 %copy-start = (f32[256,1024]{1,0:T(8,128)}, f32[256,1024]{1,0:T(8,128)S(1)}, u32[]{:S(2)}) copy-start(f32[256,1024]{1,0:T(8,128)S(1)} %get-tuple-element.24.refs_1_.refs_2_.refs_0_.refs_10_) | copy-start | bytes 3145732
  3.4 26.1 %collective-permute-start.1 = (f32[256,1024]{1,0:T(8,128)S(1)}, f32[256,1024]{1,0:T(8,128)S(1)}, u32[]{:S(2)}, u32[]{:S(2)}) collective-permute-start(f32[256,1024]{1,0:T(8,128)S(1)} %get-tuple-element.25.refs_1_.refs_0_), channel_id=1, source_target_pairs={{0,1},{1,0},{2,3},{3,2},{4,5},{5,4},{6,7},{7,6},{8,9},{9,8},{10,11... | collective-permute-start | bytes 3145736 | tf_op jit(solution)/shard_map/ppermute | solution.py:81
  5.0 25.2 %collective-permute-start = (f32[256,1024]{1,0:T(8,128)S(1)}, f32[256,1024]{1,0:T(8,128)S(1)}, u32[]{:S(2)}, u32[]{:S(2)}) collective-permute-start(f32[256,1024]{1,0:T(8,128)S(1)} %get-tuple-element.24.refs_1_.refs_2_.refs_0_.refs_10_), channel_id=1, source_target_pairs={{0,8},{8,0},{16,24},{24,16},{1,9},{9,1},{17,25},{25,17},{2,10},{10... | collective-permute-start | bytes 3145736 | tf_op jit(solution)/shard_map/ppermute | solution.py:81
  6.1 1.0 copy-start.3
  6.1 2.0 %copy-start.6 = (f32[256,2048]{1,0:T(8,128)S(1)}, f32[256,2048]{1,0:T(8,128)}, u32[]{:S(2)}) copy-start(f32[256,2048]{1,0:T(8,128)} %refs_0_.5) | copy-start | bytes 6291460
  7.1 45.7 %collective-permute-start.5 = (f32[256,1536]{1,0:T(8,128)S(1)}, f32[256,1536]{1,0:T(8,128)S(1)}, u32[]{:S(2)}, u32[]{:S(2)}) collective-permute-start(f32[256,1536]{1,0:T(8,128)S(1)} %get-tuple-element.27.refs_2_), channel_id=1, source_target_pairs={{0,8},{8,0},{16,24},{24,16},{1,9},{9,1},{17,25},{25,17},{2,10},{10... | collective-permute-start | bytes 4718600 | tf_op jit(solution)/shard_map/ppermute | solution.py:81
  7.6 44.4 %collective-permute-start.6 = (f32[256,1024]{1,0:T(8,128)S(1)}, f32[256,1024]{1,0:T(8,128)S(1)}, u32[]{:S(2)}, u32[]{:S(2)}) collective-permute-start(f32[256,1024]{1,0:T(8,128)S(1)} %get-tuple-element.31), channel_id=1, source_target_pairs={{0,1},{1,0},{2,3},{3,2},{4,5},{5,4},{6,7},{7,6},{8,9},{9,8},{10,11... | collective-permute-start | bytes 3145736 | tf_op jit(solution)/shard_map/ppermute | solution.py:81
  29.5 9.5 %copy-start.1 = (f32[256,1024]{1,0:T(8,128)}, f32[256,1024]{1,0:T(8,128)S(1)}, u32[]{:S(2)}) copy-start(f32[256,1024]{1,0:T(8,128)S(1)} %collective-permute-done.1.refs_4_.refs_5_.refs_12_) | copy-start | bytes 3145732
  29.6 2.1 %collective-permute-start.3 = (f32[128,1024]{1,0:T(8,128)S(1)}, f32[128,1024]{1,0:T(8,128)S(1)}, u32[]{:S(2)}, u32[]{:S(2)}) collective-permute-start(f32[128,1024]{1,0:T(8,128)S(1)} %get-tuple-element.49), channel_id=1, source_target_pairs={{0,8},{8,0},{16,24},{24,16},{1,9},{9,1},{17,25},{25,17},{2,10},{10... | collective-permute-start | bytes 1572872 | tf_op jit(solution)/shard_map/ppermute | solution.py:81
  29.7 2.6 %collective-permute-start.2 = (f32[128,1024]{1,0:T(8,128)S(1)}, f32[128,1024]{1,0:T(8,128)S(1)}, u32[]{:S(2)}, u32[]{:S(2)}) collective-permute-start(f32[128,1024]{1,0:T(8,128)S(1)} %get-tuple-element.50), channel_id=1, source_target_pairs={{0,8},{8,0},{16,24},{24,16},{1,9},{9,1},{17,25},{25,17},{2,10},{10... | collective-permute-start | bytes 1572872 | tf_op jit(solution)/shard_map/ppermute | solution.py:81
  30.2 33.2 %copy-start.2 = (f32[256,1024]{1,0:T(8,128)}, f32[256,1024]{1,0:T(8,128)S(1)}, u32[]{:S(2)}) copy-start(f32[256,1024]{1,0:T(8,128)S(1)} %collective-permute-done.refs_2_.refs_3_.refs_11_) | copy-start | bytes 3145732
  30.2 43.1 %collective-permute-start.11 = (f32[512,512]{1,0:T(8,128)S(1)}, f32[512,512]{1,0:T(8,128)S(1)}, u32[]{:S(2)}, u32[]{:S(2)}) collective-permute-start(f32[512,512]{1,0:T(8,128)S(1)} %get-tuple-element.34), channel_id=1, source_target_pairs={{0,1},{1,0},{2,3},{3,2},{4,5},{5,4},{6,7},{7,6},{8,9},{9,8},{10,11... | collective-permute-start | bytes 3145736 | tf_op jit(solution)/shard_map/ppermute | solution.py:81
  39.0 20.6 %collective-permute-start.4 = (f32[1,4,192,256]{3,2,1,0:T(8,128)S(1)}, f32[1,4,192,256]{3,2,1,0:T(8,128)S(1)}, u32[]{:S(2)}, u32[]{:S(2)}) collective-permute-start(f32[1,4,192,256]{3,2,1,0:T(8,128)S(1)} %get-tuple-element.30), channel_id=1, source_target_pairs={{0,16},{8,24},{16,0},{24,8},{1,17},{9,25},{17,1},{25,9},{2,18},{10... | collective-permute-start | bytes 2359304 | tf_op jit(solution)/shard_map/ppermute | solution.py:81
  52.0 2.8 %copy-start.9 = (f32[256,1024]{1,0:T(8,128)}, f32[256,1024]{1,0:T(8,128)S(1)}, u32[]{:S(2)}) copy-start(f32[256,1024]{1,0:T(8,128)S(1)} %collective-permute-done.6.refs_12_) | copy-start | bytes 3145732
  52.0 2.7 %collective-permute-start.7 = (f32[96,1024]{1,0:T(8,128)S(1)}, f32[96,1024]{1,0:T(8,128)S(1)}, u32[]{:S(2)}, u32[]{:S(2)}) collective-permute-start(f32[96,1024]{1,0:T(8,128)S(1)} %slice.29), channel_id=1, source_target_pairs={{0,8},{8,0},{16,24},{24,16},{1,9},{9,1},{17,25},{25,17},{2,10},{10... | collective-permute-start | bytes 1179656 | tf_op jit(solution)/shard_map/ppermute | solution.py:81
  52.2 2.1 %collective-permute-start.9 = (f32[80,1024]{1,0:T(8,128)S(1)}, f32[80,1024]{1,0:T(8,128)S(1)}, u32[]{:S(2)}, u32[]{:S(2)}) collective-permute-start(f32[80,1024]{1,0:T(8,128)S(1)} %get-tuple-element.47), channel_id=1, source_target_pairs={{0,8},{8,0},{16,24},{24,16},{1,9},{9,1},{17,25},{25,17},{2,10},{10... | collective-permute-start | bytes 983048 | tf_op jit(solution)/shard_map/ppermute | solution.py:81
  52.7 2.0 %copy-start.8 = (f32[256,1536]{1,0:T(8,128)}, f32[256,1536]{1,0:T(8,128)S(1)}, u32[]{:S(2)}) copy-start(f32[256,1536]{1,0:T(8,128)S(1)} %collective-permute-done.5.refs_11_.refs_2_.refs_3_) | copy-start | bytes 4718596
  52.7 2.0 %collective-permute-start.8 = (f32[80,1024]{1,0:T(8,128)S(1)}, f32[80,1024]{1,0:T(8,128)S(1)}, u32[]{:S(2)}, u32[]{:S(2)}) collective-permute-start(f32[80,1024]{1,0:T(8,128)S(1)} %get-tuple-element.48), channel_id=1, source_target_pairs={{0,8},{8,0},{16,24},{24,16},{1,9},{9,1},{17,25},{25,17},{2,10},{10... | collective-permute-start | bytes 983048 | tf_op jit(solution)/shard_map/ppermute | solution.py:81
  59.6 14.7 %collective-permute-start.14 = (f32[1,2,256,256]{3,2,1,0:T(8,128)S(1)}, f32[1,2,256,256]{3,2,1,0:T(8,128)S(1)}, u32[]{:S(2)}, u32[]{:S(2)}) collective-permute-start(f32[1,2,256,256]{3,2,1,0:T(8,128)S(1)} %get-tuple-element.37), channel_id=1, source_target_pairs={{0,16},{8,24},{16,0},{24,8},{1,17},{9,25},{17,1},{25,9},{2,18},{10... | collective-permute-start | bytes 1572872 | tf_op jit(solution)/shard_map/ppermute | solution.py:81
  61.3 21.7 %collective-permute-start.10 = (f32[1,2,192,256]{3,2,1,0:T(8,128)S(1)}, f32[1,2,192,256]{3,2,1,0:T(8,128)S(1)}, u32[]{:S(2)}, u32[]{:S(2)}) collective-permute-start(f32[1,2,192,256]{3,2,1,0:T(8,128)S(1)} %halve.10.refs_16_), channel_id=1, source_target_pairs={{0,2},{1,3},{2,0},{3,1},{4,6},{5,7},{6,4},{7,5},{8,10},{9,11},{10,... | collective-permute-start | bytes 1179656 | tf_op jit(solution)/shard_map/ppermute | solution.py:81
  73.4 1.6 %collective-permute-start.13 = (f32[128,512]{1,0:T(8,128)S(1)}, f32[128,512]{1,0:T(8,128)S(1)}, u32[]{:S(2)}, u32[]{:S(2)}) collective-permute-start(f32[128,512]{1,0:T(8,128)S(1)} %get-tuple-element.45), channel_id=1, source_target_pairs={{0,8},{8,0},{16,24},{24,16},{1,9},{9,1},{17,25},{25,17},{2,10},{10... | collective-permute-start | bytes 786440 | tf_op jit(solution)/shard_map/ppermute | solution.py:81
  73.4 1.9 %collective-permute-start.12 = (f32[128,512]{1,0:T(8,128)S(1)}, f32[128,512]{1,0:T(8,128)S(1)}, u32[]{:S(2)}, u32[]{:S(2)}) collective-permute-start(f32[128,512]{1,0:T(8,128)S(1)} %get-tuple-element.46), channel_id=1, source_target_pairs={{0,8},{8,0},{16,24},{24,16},{1,9},{9,1},{17,25},{25,17},{2,10},{10... | collective-permute-start | bytes 786440 | tf_op jit(solution)/shard_map/ppermute | solution.py:81
  73.9 14.8 %collective-permute-start.16 = (f32[1,2,256,256]{3,2,1,0:T(8,128)S(1)}, f32[1,2,256,256]{3,2,1,0:T(8,128)S(1)}, u32[]{:S(2)}, u32[]{:S(2)}) collective-permute-start(f32[1,2,256,256]{3,2,1,0:T(8,128)S(1)} %get-tuple-element.39), channel_id=1, source_target_pairs={{0,16},{8,24},{16,0},{24,8},{1,17},{9,25},{17,1},{25,9},{2,18},{10... | collective-permute-start | bytes 1572872 | tf_op jit(solution)/shard_map/ppermute | solution.py:81
  82.3 23.5 %collective-permute-start.18 = (f32[1,4,128,256]{3,2,1,0:T(8,128)S(1)}, f32[1,4,128,256]{3,2,1,0:T(8,128)S(1)}, u32[]{:S(2)}, u32[]{:S(2)}) collective-permute-start(f32[1,4,128,256]{3,2,1,0:T(8,128)S(1)} %get-tuple-element.41), channel_id=1, source_target_pairs={{0,16},{8,24},{16,0},{24,8},{1,17},{9,25},{17,1},{25,9},{2,18},{10... | collective-permute-start | bytes 1572872 | tf_op jit(solution)/shard_map/ppermute | solution.py:81
  84.4 12.9 %collective-permute-start.15 = (f32[1,1,192,256]{3,2,1,0:T(8,128)S(1)}, f32[1,1,192,256]{3,2,1,0:T(8,128)S(1)}, u32[]{:S(2)}, u32[]{:S(2)}) collective-permute-start(f32[1,1,192,256]{3,2,1,0:T(8,128)S(1)} %halve.11.refs_4_), channel_id=1, source_target_pairs={{0,4},{1,5},{2,6},{3,7},{4,0},{5,1},{6,2},{7,3},{8,12},{9,13},{10,... | collective-permute-start | bytes 589832 | tf_op jit(solution)/shard_map/ppermute | solution.py:81
  89.7 22.4 %collective-permute-start.20 = (f32[1,2,256,256]{3,2,1,0:T(8,128)S(1)}, f32[1,2,256,256]{3,2,1,0:T(8,128)S(1)}, u32[]{:S(2)}, u32[]{:S(2)}) collective-permute-start(f32[1,2,256,256]{3,2,1,0:T(8,128)S(1)} %halve.12.refs_16_), channel_id=1, source_target_pairs={{0,2},{1,3},{2,0},{3,1},{4,6},{5,7},{6,4},{7,5},{8,10},{9,11},{10,... | collective-permute-start | bytes 1572872 | tf_op jit(solution)/shard_map/ppermute | solution.py:81
  96.7 2.3 %copy-start.4 = (f32[256,1024]{1,0:T(8,128)S(1)}, f32[256,1024]{1,0:T(8,128)}, u32[]{:S(2)}) copy-start(f32[256,1024]{1,0:T(8,128)} %copy-done.3) | copy-start | bytes 3145732
  96.7 17.9 %collective-permute-start.22 = (f32[1,4,128,256]{3,2,1,0:T(8,128)S(1)}, f32[1,4,128,256]{3,2,1,0:T(8,128)S(1)}, u32[]{:S(2)}, u32[]{:S(2)}) collective-permute-start(f32[1,4,128,256]{3,2,1,0:T(8,128)S(1)} %get-tuple-element.43), channel_id=1, source_target_pairs={{0,16},{8,24},{16,0},{24,8},{1,17},{9,25},{17,1},{25,9},{2,18},{10... | collective-permute-start | bytes 1572872 | tf_op jit(solution)/shard_map/ppermute | solution.py:81
  104.2 20.5 %collective-permute-start.24 = (f32[1,4,128,256]{3,2,1,0:T(8,128)S(1)}, f32[1,4,128,256]{3,2,1,0:T(8,128)S(1)}, u32[]{:S(2)}, u32[]{:S(2)}) collective-permute-start(f32[1,4,128,256]{3,2,1,0:T(8,128)S(1)} %get-tuple-element.44), channel_id=1, source_target_pairs={{0,16},{8,24},{16,0},{24,8},{1,17},{9,25},{17,1},{25,9},{2,18},{10... | collective-permute-start | bytes 1572872 | tf_op jit(solution)/shard_map/ppermute | solution.py:81
  107.1 6.4 %collective-permute-start.19 = (f32[1,2,128,256]{3,2,1,0:T(8,128)S(1)}, f32[1,2,128,256]{3,2,1,0:T(8,128)S(1)}, u32[]{:S(2)}, u32[]{:S(2)}) collective-permute-start(f32[1,2,128,256]{3,2,1,0:T(8,128)S(1)} %halve.13.refs_5_), channel_id=1, source_target_pairs={{0,2},{1,3},{2,0},{3,1},{4,6},{5,7},{6,4},{7,5},{8,10},{9,11},{10,... | collective-permute-start | bytes 786440 | tf_op jit(solution)/shard_map/ppermute | solution.py:81
  107.6 17.1 %collective-permute-start.17 = (f32[128,256]{1,0:T(8,128)S(1)}, f32[128,256]{1,0:T(8,128)S(1)}, u32[]{:S(2)}, u32[]{:S(2)}) collective-permute-start(f32[128,256]{1,0:T(8,128)S(1)} %slice.35), channel_id=1, source_target_pairs={{2,8},{3,9},{4,16},{5,17},{6,24},{7,25},{8,2},{9,3},{12,18},{13,19... | collective-permute-start | bytes 393224 | tf_op jit(solution)/shard_map/ppermute | solution.py:522
  112.8 15.1 %collective-permute-start.25 = (f32[1,1,256,256]{3,2,1,0:T(8,128)S(1)}, f32[1,1,256,256]{3,2,1,0:T(8,128)S(1)}, u32[]{:S(2)}, u32[]{:S(2)}) collective-permute-start(f32[1,1,256,256]{3,2,1,0:T(8,128)S(1)} %halve.14.refs_3_), channel_id=1, source_target_pairs={{0,4},{1,5},{2,6},{3,7},{4,0},{5,1},{6,2},{7,3},{8,12},{9,13},{10,... | collective-permute-start | bytes 786440 | tf_op jit(solution)/shard_map/ppermute | solution.py:81
  116.0 15.3 %collective-permute-start.23 = (f32[1,2,128,256]{3,2,1,0:T(8,128)S(1)}, f32[1,2,128,256]{3,2,1,0:T(8,128)S(1)}, u32[]{:S(2)}, u32[]{:S(2)}) collective-permute-start(f32[1,2,128,256]{3,2,1,0:T(8,128)S(1)} %halve.16.refs_2_), channel_id=1, source_target_pairs={{0,2},{1,3},{2,0},{3,1},{4,6},{5,7},{6,4},{7,5},{8,10},{9,11},{10,... | collective-permute-start | bytes 786440 | tf_op jit(solution)/shard_map/ppermute | solution.py:81
  126.0 15.8 %collective-permute-start.27 = (f32[1,2,128,256]{3,2,1,0:T(8,128)S(1)}, f32[1,2,128,256]{3,2,1,0:T(8,128)S(1)}, u32[]{:S(2)}, u32[]{:S(2)}) collective-permute-start(f32[1,2,128,256]{3,2,1,0:T(8,128)S(1)} %halve.17.refs_3_), channel_id=1, source_target_pairs={{0,2},{1,3},{2,0},{3,1},{4,6},{5,7},{6,4},{7,5},{8,10},{9,11},{10,... | collective-permute-start | bytes 786440 | tf_op jit(solution)/shard_map/ppermute | solution.py:81
  127.3 13.2 %collective-permute-start.21 = (f32[1,1,128,256]{3,2,1,0:T(8,128)S(1)}, f32[1,1,128,256]{3,2,1,0:T(8,128)S(1)}, u32[]{:S(2)}, u32[]{:S(2)}) collective-permute-start(f32[1,1,128,256]{3,2,1,0:T(8,128)S(1)} %halve.15.refs_2_), channel_id=1, source_target_pairs={{0,4},{1,5},{2,6},{3,7},{4,0},{5,1},{6,2},{7,3},{8,12},{9,13},{10,... | collective-permute-start | bytes 393224 | tf_op jit(solution)/shard_map/ppermute | solution.py:81
  132.4 23.3 %collective-permute-start.28 = (f32[1,1,128,256]{3,2,1,0:T(8,128)S(1)}, f32[1,1,128,256]{3,2,1,0:T(8,128)S(1)}, u32[]{:S(2)}, u32[]{:S(2)}) collective-permute-start(f32[1,1,128,256]{3,2,1,0:T(8,128)S(1)} %halve.18.refs_4_), channel_id=1, source_target_pairs={{0,4},{1,5},{2,6},{3,7},{4,0},{5,1},{6,2},{7,3},{8,12},{9,13},{10,... | collective-permute-start | bytes 393224 | tf_op jit(solution)/shard_map/ppermute | solution.py:81
  141.8 12.4 %collective-permute-start.26 = (f32[128,256]{1,0:T(8,128)S(1)}, f32[128,256]{1,0:T(8,128)S(1)}, u32[]{:S(2)}, u32[]{:S(2)}) collective-permute-start(f32[128,256]{1,0:T(8,128)S(1)} %finish.3.refs_3_.refs_2_), channel_id=1, source_target_pairs={{0,1},{1,0},{2,9},{3,8},{4,17},{5,16},{6,25},{7,24},{8,3},{9,2},{1... | collective-permute-start | bytes 393224 | tf_op jit(solution)/shard_map/ppermute | solution.py:542
  143.0 12.7 %collective-permute-start.29 = (f32[1,1,128,256]{3,2,1,0:T(8,128)S(1)}, f32[1,1,128,256]{3,2,1,0:T(8,128)S(1)}, u32[]{:S(2)}, u32[]{:S(2)}) collective-permute-start(f32[1,1,128,256]{3,2,1,0:T(8,128)S(1)} %halve.19.refs_4_), channel_id=1, source_target_pairs={{0,4},{1,5},{2,6},{3,7},{4,0},{5,1},{6,2},{7,3},{8,12},{9,13},{10,... | collective-permute-start | bytes 393224 | tf_op jit(solution)/shard_map/ppermute | solution.py:81
